TPU v7x, 32 devices: a whole 2x2x4 slice. The times are simulated.
32 devices in a mesh: dp: 8 (over y, x, core), mp: 4 (over z).
Axes of the slice: x: 2, y: 2, z: 4, core: 2. Of those that a mesh axis runs over, the one named last changes fastest.
Arguments:
- item_ids: int32 [4, 3072], P(None, 'dp'), may hold values from 0 to 36863
- session_ends: int32 [3, 3072], P(None, 'dp'), may hold values 0 or 1
- negatives: int32 [2048], replicated, may hold values from 0 to 36863
- embedding: bfloat16 [1000, 36864], P('mp'), may hold values from -6 to 6
- in_weight: bfloat16 [3, 1000, 1000], P(None, None, 'mp'), may hold values from -0.1875 to 0.1875
- hid_weight: bfloat16 [3, 1000, 1000], P(None, None, 'mp'), may hold values from -0.1875 to 0.1875
- gate_bias: float32 [3, 1000], P(None, 'mp'), may hold values from -3 to 3
- cand_bias: float32 [1000], P('mp'), may hold values from -3 to 3
- out_table: bfloat16 [1000, 36864], P('mp'), may hold values from -0.75 to 0.75
- out_bias: float32 [36864], replicated, may hold values from -6 to 6
Outputs:
- loss: float32 [], replicated
- in_weight_grad: float32 [3, 1000, 1000], P(None, None, 'mp')
- hid_weight_grad: float32 [3, 1000, 1000], P(None, None, 'mp')
- gate_bias_grad: float32 [3, 1000], P(None, 'mp')
- cand_bias_grad: float32 [1000], P('mp')
- embedding_grad: float32 [1000, 36864], P('mp', 'dp')
- out_table_grad: float32 [1000, 36864], P('mp', 'dp')
- out_bias_grad: float32 [36864], P('dp')
All inputs are finite; a program needn't handle non-finite values. No bound on the sum of `session_ends` on one device may be relied on, other than what follows from the above.
Results may differ from a plain program's by a relative error of at most 0.0017.
Values may be sent and summed in bfloat16 or wider, within the bound.
No kernel may reach another device: no remote copies, remote signals or barrier semaphores. Data moves between devices by JAX's collectives and lax.ppermute only.
A program may use at most 384 MiB of HBM per device.

v0:
```python
import jax
import jax.numpy as jnp
from jax import lax
from jax.sharding import PartitionSpec as P

bpr_weight = 1.0


def gate_parts(gate_in, from_state, gate_bias, cand_bias):
    update = jax.nn.sigmoid(gate_in[:, 0] + from_state[:, 0] + gate_bias[0])
    reset_gate = jax.nn.sigmoid(gate_in[:, 1] + from_state[:, 1] + gate_bias[1])
    inner_sum = from_state[:, 2] + cand_bias
    candidate = jnp.tanh(gate_in[:, 2] + gate_bias[2] + reset_gate * inner_sum)
    return (update, reset_gate, inner_sum, candidate)


def on_device(
    item_ids,
    session_ends,
    negatives,
    embedding,
    in_weight,
    hid_weight,
    gate_bias,
    cand_bias,
    out_table,
    out_bias,
):
    step_count = session_ends.shape[0]
    slot_count = session_ends.shape[1]
    event_count = step_count * slot_count
    share_rows = event_count // lax.axis_size("mp")
    all_slots = slot_count * lax.axis_size("dp")
    unit_count = hid_weight.shape[2]
    end_float = session_ends.astype(jnp.float32)
    starts = jnp.concatenate([jnp.ones((1, slot_count), jnp.float32), end_float[:-1]], axis=0)
    keep_mask = 1.0 - starts
    valid_weight = ((1.0 - end_float) / (step_count * all_slots)).reshape(event_count)
    sources = item_ids[:-1].reshape(event_count)
    targets = item_ids[1:].reshape(event_count)
    local_feats = jnp.take(embedding, sources, axis=1).T
    embedded = lax.all_gather(local_feats, "mp", axis=1, tiled=True)
    from_input = jnp.einsum("ne,geh->ngh", embedded, in_weight, preferred_element_type=jnp.float32)
    from_input = from_input.reshape(step_count, slot_count, 3, unit_count)

    def forward_step(hidden, pieces):
        gate_in, keep_now = pieces
        previous = hidden * keep_now[:, None]
        gathered = lax.all_gather(previous.astype(jnp.bfloat16), "mp", axis=1, tiled=True)
        from_state = jnp.einsum(
            "bk,gkh->bgh", gathered, hid_weight, preferred_element_type=jnp.float32
        )
        update, reset_gate, inner_sum, candidate = gate_parts(
            gate_in, from_state, gate_bias, cand_bias
        )
        fresh_state = (1.0 - update) * previous + update * candidate
        return (fresh_state, (fresh_state, previous, gathered, from_state))

    start_state = jnp.zeros((slot_count, unit_count), jnp.float32)
    _, (fresh_all, prev_all, gathered_all, state_all) = lax.scan(
        forward_step, start_state, (from_input, keep_mask)
    )
    shown_state = fresh_all.reshape(event_count, unit_count).astype(jnp.bfloat16)
    neg_cols = jnp.take(out_table, negatives, axis=1)
    tgt_rows = jnp.take(out_table, targets, axis=1).T
    first_row = lax.axis_index("mp") * share_rows
    own_targets = lax.dynamic_slice_in_dim(targets, first_row, share_rows)
    own_weight = lax.dynamic_slice_in_dim(valid_weight, first_row, share_rows)
    neg_part = jnp.dot(shown_state, neg_cols, preferred_element_type=jnp.float32)
    tgt_part = jnp.einsum("nh,nh->n", shown_state, tgt_rows, preferred_element_type=jnp.float32)
    neg_sum, tgt_sum = (
        lax.psum_scatter(neg_part, "mp", scatter_dimension=0, tiled=True),
        lax.psum_scatter(tgt_part, "mp", scatter_dimension=0, tiled=True),
    )
    neg_scores = neg_sum + out_bias[negatives][None, :]
    tgt_scores = tgt_sum + out_bias[own_targets]
    weights = jax.nn.softmax(neg_scores, axis=1)
    above_prob = jax.nn.sigmoid(tgt_scores[:, None] - neg_scores)
    mixture = jnp.sum(weights * above_prob, axis=1)
    spread = jnp.sum(weights * neg_scores * neg_scores, axis=1)
    per_event = -jnp.log(mixture) + bpr_weight * spread
    loss_part = jnp.sum(own_weight * per_event)
    neg_grad = (
        own_weight[:, None]
        * weights
        * (
            1.0
            - above_prob * above_prob / mixture[:, None]
            + bpr_weight * (neg_scores * neg_scores + 2.0 * neg_scores - spread[:, None])
        )
    )
    tgt_grad = -own_weight * jnp.sum(weights * above_prob * (1.0 - above_prob), axis=1) / mixture
    neg_low, tgt_low = (
        lax.all_gather(neg_grad.astype(jnp.bfloat16), "mp", axis=0, tiled=True),
        lax.all_gather(tgt_grad.astype(jnp.bfloat16), "mp", axis=0, tiled=True),
    )
    tgt_float = tgt_low.astype(jnp.float32)
    grad_shown = jnp.einsum(
        "nj,hj->nh", neg_low, neg_cols, preferred_element_type=jnp.float32
    ) + tgt_float[:, None] * tgt_rows.astype(jnp.float32)
    neg_table = jnp.einsum("nh,nj->hj", shown_state, neg_low, preferred_element_type=jnp.float32)
    neg_bias_part = jnp.sum(neg_low, axis=0, dtype=jnp.float32)
    tgt_table_rows = tgt_float[:, None] * shown_state.astype(jnp.float32)
    grad_shown = grad_shown.reshape(step_count, slot_count, unit_count)

    def backward_step(carry, pieces):
        later_grad, bias_acc, cand_acc = carry
        gate_in, state_now, prev_now, keep_now, extra_now = pieces
        update, reset_gate, inner_sum, candidate = gate_parts(
            gate_in, state_now, gate_bias, cand_bias
        )
        grad_fresh = later_grad + extra_now
        grad_update = grad_fresh * (candidate - prev_now) * update * (1.0 - update)
        grad_pre = grad_fresh * update * (1.0 - candidate * candidate)
        grad_reset = grad_pre * inner_sum * reset_gate * (1.0 - reset_gate)
        grad_inner = grad_pre * reset_gate
        input_grad = jnp.stack([grad_update, grad_reset, grad_pre], axis=1)
        state_grad = jnp.stack([grad_update, grad_reset, grad_inner], axis=1)
        input_low = input_grad.astype(jnp.bfloat16)
        state_low = state_grad.astype(jnp.bfloat16)
        spread_back = jnp.einsum(
            "bgh,gkh->bk", state_low, hid_weight, preferred_element_type=jnp.float32
        )
        owned = lax.psum_scatter(spread_back, "mp", scatter_dimension=1, tiled=True)
        grad_prev = grad_fresh * (1.0 - update) + owned
        new_carry = (
            grad_prev * keep_now[:, None],
            bias_acc + jnp.sum(input_grad, axis=0),
            cand_acc + jnp.sum(grad_inner, axis=0),
        )
        return (new_carry, (input_low, state_low))

    zero_carry = (
        jnp.zeros((slot_count, unit_count), jnp.float32),
        jnp.zeros((3, unit_count), jnp.float32),
        jnp.zeros((unit_count,), jnp.float32),
    )
    (_, bias_grad, cand_grad), (input_lows, state_lows) = lax.scan(
        backward_step,
        zero_carry,
        (from_input, state_all, prev_all, keep_mask, grad_shown),
        reverse=True,
    )
    input_lows = input_lows.reshape(event_count, 3, unit_count)
    state_lows = state_lows.reshape(event_count, 3, unit_count)
    in_grad = jnp.einsum("ne,ngh->geh", embedded, input_lows, preferred_element_type=jnp.float32)
    hid_grad = jnp.einsum(
        "nk,ngh->gkh",
        gathered_all.reshape(event_count, -1),
        state_lows,
        preferred_element_type=jnp.float32,
    )
    feat_cols = lax.psum_scatter(
        jnp.einsum("geh,ngh->en", in_weight, input_lows, preferred_element_type=jnp.float32),
        "mp",
        scatter_dimension=0,
        tiled=True,
    )
    in_sum, hid_sum, gate_sum, cand_sum = lax.psum((in_grad, hid_grad, bias_grad, cand_grad), "dp")
    loss_value = lax.psum(loss_part, ("dp", "mp"))
    table_local = (
        jnp.zeros(out_table.shape, jnp.float32)
        .at[:, negatives]
        .add(neg_table)
        .at[:, targets]
        .add(tgt_table_rows.T)
    )
    bias_local = (
        jnp.zeros(out_bias.shape, jnp.float32)
        .at[negatives]
        .add(neg_bias_part)
        .at[targets]
        .add(tgt_float)
    )
    embed_local = jnp.zeros(embedding.shape, jnp.float32).at[:, sources].add(feat_cols)
    embed_sum, table_sum, bias_rows = (
        lax.psum_scatter(embed_local, "dp", scatter_dimension=1, tiled=True),
        lax.psum_scatter(table_local, "dp", scatter_dimension=1, tiled=True),
        lax.psum_scatter(bias_local.reshape(1, -1), "dp", scatter_dimension=1, tiled=True),
    )
    bias_sum = bias_rows.reshape(-1)
    return (loss_value, in_sum, hid_sum, gate_sum, cand_sum, embed_sum, table_sum, bias_sum)


def solution(mesh):
    return jax.shard_map(
        on_device,
        mesh=mesh,
        in_specs=(
            P(None, "dp"),
            P(None, "dp"),
            P(),
            P("mp", None),
            P(None, None, "mp"),
            P(None, None, "mp"),
            P(None, "mp"),
            P("mp"),
            P("mp", None),
            P(),
        ),
        out_specs=(
            P(),
            P(None, None, "mp"),
            P(None, None, "mp"),
            P(None, "mp"),
            P("mp"),
            P("mp", "dp"),
            P("mp", "dp"),
            P("dp"),
        ),
        check_vma=False,
    )
```

profile of v0, /device:TPU:27, one launch (start us, length us, event | category | flops | bytes accessed | tf_op | source)
XLA Modules:
  0.0 1433.9 jit_solution(204653213820521559)
XLA Ops:
  8.7 24.7 %copy.42 = bf16[250,36864]{0,1:T(8,128)(2,1)} copy(bf16[250,36864]{1,0:T(8,128)(2,1)} %param.19) | data formatting | bytes 36864000 | tf_op args[3]
  33.4 12.1 gather_fusion.3
  47.1 24.7 %copy.45 = bf16[250,36864]{0,1:T(8,128)(2,1)} copy(bf16[250,36864]{1,0:T(8,128)(2,1)} %param.24) | data formatting | bytes 36864000 | tf_op args[8]
  72.4 17.3 %gather_fusion = bf16[2048,250]{1,0:T(8,128)(2,1)} fusion(bf16[250,36864]{0,1:T(8,128)(2,1)} %copy.45, s32[2048]{0:T(1024)S(1)} %get-tuple-element.619), kind=kCustom, calls=%fused_computation.2 | custom fusion | bytes 2056192 | tf_op jit(solution)/shard_map/jit(_take)/gather | solution.py:64
  105.8 70.6 %while.42 = (s32[]{:T(128)}, f32[384,250]{1,0:T(8,128)S(1)}, bf16[3,384,250]{2,1,0:T(8,128)(2,1)}, f32[3,384,250]{2,1,0:T(8,128)}, bf16[3,384,1000]{1,2,0:T(8,12...) while((s32[]{:T(128)}, f32[384,250]{1,0:T(8,128)S(1)}, ...), condition=%wide.region_1.3_spmd.clone, body=%wide.region_0.0_spmd.clone.sunk | while | flops 578208000 | bytes 31060836 | solution.py:60
  106.1 16.1 %all-gather.4 = bf16[4,250,384]{2,1,0:T(8,128)(2,1)S(1)} all-gather(bf16[1,250,384]{2,1,0:T(8,128)(2,1)S(1)} %copy.67), channel_id=1, replica_groups=mesh['dp'=8,'mp'=4] {'mp'}, dimensions={0}, use_global_device_ids=true | all-gather | bytes 960000 | tf_op jit(solution)/shard_map/while/body/eval_jaxpr/all_gather | solution.py:49
  130.1 16.3 %all-gather.4 = bf16[4,250,384]{2,1,0:T(8,128)(2,1)S(1)} all-gather(bf16[1,250,384]{2,1,0:T(8,128)(2,1)S(1)} %copy.67), channel_id=1, replica_groups=mesh['dp'=8,'mp'=4] {'mp'}, dimensions={0}, use_global_device_ids=true | all-gather | bytes 960000 | tf_op jit(solution)/shard_map/while/body/eval_jaxpr/all_gather | solution.py:49
  154.2 14.5 %all-gather.4 = bf16[4,250,384]{2,1,0:T(8,128)(2,1)S(1)} all-gather(bf16[1,250,384]{2,1,0:T(8,128)(2,1)S(1)} %copy.67), channel_id=1, replica_groups=mesh['dp'=8,'mp'=4] {'mp'}, dimensions={0}, use_global_device_ids=true | all-gather | bytes 960000 | tf_op jit(solution)/shard_map/while/body/eval_jaxpr/all_gather | solution.py:49
  198.1 12.3 gather_fusion.4
  219.8 133.0 %reduce-scatter.10.cloned.1.call-done = f32[288,2048]{1,0:T(8,128)} async-done(((f32[1152,2048]{1,0:T(8,128)}), f32[288,2048]{1,0:T(8,128)}) %reduce-scatter.10.cloned.1.call-update) | async-done | bytes 2359312 | tf_op jit(solution)/shard_map/reduce_scatter | solution.py:72
  367.9 80.7 %all-gather.8.cloned.1.call-done = bf16[1152,2048]{1,0:T(8,128)(2,1)} async-done(((bf16[288,2048]{1,0:T(8,128)(2,1)}), bf16[1152,2048]{1,0:T(8,128)(2,1)}) %all-gather.8.cloned.1.call-update) | async-done | bytes 4718608 | tf_op jit(solution)/shard_map/all_gather | solution.py:94
  488.1 234.5 %while.43 = (s32[]{:T(128)}, f32[384,250]{1,0:T(8,128)S(1)}, f32[3,250]{1,0:T(4,128)S(1)}, f32[250]{0:T(256)S(1)}, bf16[3,384,3,250]{3,1,0,2:T(8,128)(2,1)}, /*i...) while((s32[]{:T(128)}, f32[384,250]{1,0:T(8,128)S(1)}, ...), condition=%wide.region_15.17_spmd.clone, body=%wide.region_11.16_spmd.clone.sunk | while | flops 585312960 | bytes 42399804 | solution.py:138
  500.9 64.0 %all-reduce.15.cloned.1.call-done = f32[384,1000]{1,0:T(8,128)} async-done(((f32[384,1000]{1,0:T(8,128)}), f32[384,1000]{1,0:T(8,128)}) %all-reduce.15.cloned.1.call-update) | async-done | bytes 1536016 | tf_op jit(solution)/shard_map/while
  579.2 63.9 %all-reduce.15.cloned.1.call-done = f32[384,1000]{1,0:T(8,128)} async-done(((f32[384,1000]{1,0:T(8,128)}), f32[384,1000]{1,0:T(8,128)}) %all-reduce.15.cloned.1.call-update) | async-done | bytes 1536016 | tf_op jit(solution)/shard_map/while
  657.3 64.0 %all-reduce.15.cloned.1.call-done = f32[384,1000]{1,0:T(8,128)} async-done(((f32[384,1000]{1,0:T(8,128)}), f32[384,1000]{1,0:T(8,128)}) %all-reduce.15.cloned.1.call-update) | async-done | bytes 1536016 | tf_op jit(solution)/shard_map/while
  728.9 32.5 %scatter_custom_fusion.1 = f32[250,36864]{0,1:T(8,128)} fusion(s32[2048]{0:T(1024)} %get-tuple-element.618, f32[2048,250]{1,0:T(8,128)} %fusion.86, f32[]{:T(128)} %constant.134.clone.1), kind=kCustom, calls=%fused_computation.96 | custom fusion | flops 512000 | bytes 36864512 | tf_op jit(solution)/shard_map/scatter-add | solution.py:164
  761.4 37.3 %scatter_custom_fusion.2 = f32[250,36864]{0,1:T(8,128)} fusion(f32[250,36864]{0,1:T(8,128)} %scatter_custom_fusion.1, s32[1152]{0:T(1024)S(1)} %fusion.73, bf16[1152,250]{1,0:T(8,128)(2,1)S(1)} %bitcast.283, f32[1152]{0:T(1024)S(1)} %convert_element_type.69), kind=kCustom, calls=%fused_computation.125 | custom fusion | flops 864000 | bytes 37462016 | tf_op jit(solution)/shard_map/scatter-add | solution.py:166
  804.6 82.0 %fusion = f32[256,1152]{1,0:T(8,128)S(1)} fusion(f32[1000,1152]{1,0:T(8,128)} %convolution_bitcast_fusion.1), kind=kCustom, calls=%all-reduce-scatter | all-reduce-scatter fusion | flops 1179649 | bytes 5788160
  899.5 24.4 %scatter_custom_fusion = f32[250,36864]{0,1:T(8,128)} fusion(s32[1152]{0:T(1024)S(1)} %fusion.72, f32[1152,250]{1,0:T(8,128)} %copy.49, f32[]{:T(128)} %constant.134.clone.1), kind=kCustom, calls=%fused_computation.98 | custom fusion | flops 288000 | bytes 36864512 | tf_op jit(solution)/shard_map/scatter-add | solution.py:175
  935.9 42.4 %psum.35 = f32[]{:T(128)} all-reduce(f32[]{:T(128)} %multiply_reduce_fusion.3), channel_id=1, replica_groups=mesh['dp'=8,'mp'=4] {'dp','mp'}, use_global_device_ids=true, to_apply=%region_9.11 | all-reduce | flops 1 | bytes 8 | tf_op jit(solution)/shard_map/psum | solution.py:160
  978.3 13.1 all-reduce.6
  994.3 90.4 %reduce-scatter.14.cloned.1.call-done = f32[250,4608]{0,1:T(8,128)} async-done(((f32[250,36864]{0,1:T(8,128)}), f32[250,4608]{0,1:T(8,128)}) %reduce-scatter.14.cloned.1.call-update) | async-done | bytes 4608016 | tf_op jit(solution)/shard_map/reduce_scatter | solution.py:178
  1090.8 223.4 %reduce-scatter.12.cloned.1.call-done = f32[250,4608]{0,1:T(8,128)} async-done(((f32[250,36864]{0,1:T(8,128)}), f32[250,4608]{0,1:T(8,128)}) %reduce-scatter.12.cloned.1.call-update) | async-done | bytes 4608016 | tf_op jit(solution)/shard_map/reduce_scatter | solution.py:177
  1320.2 100.8 %all-reduce.13.cloned.1.call-done = (f32[3,1000,250]{2,1,0:T(8,128)}, f32[3,1000,250]{2,1,0:T(8,128)}) async-done(((f32[3,1000,250]{2,1,0:T(8,128)}, f32[3,1000,250]{2,1,0:T(8,128)}), (f32[3,1000,250]{2,1,0:T(8,128)}, f32[3,1000,250]{2,1,0:T(8,128)})) %all-reduce.13.cloned.1.call-update) | async-done | bytes 6000016 | tf_op jit(solution)/shard_map/psum | solution.py:159
  (281 shorter events, 225.1 us)
Async XLA Ops:
  7.2 92.9 %copy-start = (bf16[3,1000,250]{2,1,0:T(8,128)(2,1)S(1)}, bf16[3,1000,250]{2,1,0:T(8,128)(2,1)}, u32[]{:S(2)}) copy-start(bf16[3,1000,250]{2,1,0:T(8,128)(2,1)} %param.20) | copy-start | bytes 4500004
  7.2 89.2 %all-gather.10.cloned.1.call-start = ((), (), s32[]{:S(2)}) async-start(), calls=%async_computation.8 | async-start | bytes 2949120 | tf_op jit(solution)/shard_map/all_gather | solution.py:42
  46.7 306.0 %reduce-scatter.10.cloned.1.call-start = ((), (), s32[]{:S(2)}) async-start(), calls=%async_computation.4 | async-start | bytes 11796480 | tf_op jit(solution)/shard_map/reduce_scatter | solution.py:72
  47.1 24.7 %copy-start.27 = (f32[3,384]{1,0:T(4,128)}, f32[3,384]{1,0:T(4,128)S(1)}, u32[]{:S(2)}) copy-start(f32[3,384]{1,0:T(4,128)S(1)} %convert_element_type.64) | copy-start | bytes 13828
  47.1 24.7 %copy-start.19 = (s32[2048]{0:T(1024)S(1)}, s32[2048]{0:T(1024)}, u32[]{:S(2)}) copy-start(s32[2048]{0:T(1024)} %param.18) | copy-start | bytes 24580
  72.4 17.3 %slice-start = ((f32[3,384]{1,0:T(4,128)}), f32[2,384]{1,0:T(2,128)S(1)}, s32[]{:S(2)}) async-start(f32[3,384]{1,0:T(4,128)} %copy-done.27), calls=%async_computation.12 | async-start | bytes 6144 | tf_op jit(solution)/shard_map/slice | solution.py:36
  89.7 86.6 %copy-start.28 = (pred[2048]{0:T(1024)(128)(4,1)}, pred[2048]{0:T(1024)(128)(4,1)S(1)}, u32[]{:S(2)}) copy-start(pred[2048]{0:T(1024)(128)(4,1)S(1)} %compare_and_fusion.2) | copy-start | bytes 6148
  183.0 265.6 %all-gather.8.cloned.1.call-start = ((), (), s32[]{:S(2)}) async-start(), calls=%async_computation.5 | async-start | bytes 5898240 | tf_op jit(solution)/shard_map/all_gather | solution.py:94
  198.0 12.3 copy-start.30
  198.0 13.7 copy-start.12
  357.3 3.2 copy-start.23
  357.4 3.2 copy-start.22
  470.6 9.5 copy-start.29
  488.1 76.8 %all-reduce.15.cloned.1.call-start = ((), (), s32[]{:S(2)}) async-start(), calls=%async_computation.11 | async-start | bytes 3145728 | tf_op jit(solution)/shard_map/while
  566.2 76.9 %all-reduce.15.cloned.1.call-start = ((), (), s32[]{:S(2)}) async-start(), calls=%async_computation.11 | async-start | bytes 3145728 | tf_op jit(solution)/shard_map/while
  644.4 76.9 %all-reduce.15.cloned.1.call-start = ((), (), s32[]{:S(2)}) async-start(), calls=%async_computation.11 | async-start | bytes 3145728 | tf_op jit(solution)/shard_map/while
  722.6 268.8 %reduce-scatter.16.cloned.1.call-start = ((), (), s32[]{:S(2)}) async-start(), calls=%async_computation.9 | async-start | bytes 21233664
  723.3 361.4 %reduce-scatter.14.cloned.1.call-start = ((), (), s32[]{:S(2)}) async-start(), calls=%async_computation.7 | async-start | bytes 42467328 | tf_op jit(solution)/shard_map/reduce_scatter | solution.py:178
  798.7 515.4 %reduce-scatter.12.cloned.1.call-start = ((), (), s32[]{:S(2)}) async-start(), calls=%async_computation.6 | async-start | bytes 42467328 | tf_op jit(solution)/shard_map/reduce_scatter | solution.py:177
  886.6 5.5 collective-permute-start
  923.9 6.8 copy-start.15
  923.9 497.1 %all-reduce.13.cloned.1.call-start = ((), (), s32[]{:S(2)}) async-start(), calls=%async_computation.10 | async-start | bytes 12288000 | tf_op jit(solution)/shard_map/psum | solution.py:159
  924.3 6.5 copy-start.32
  1421.0 3.9 copy-start.14
  (41 other events, 72.8 us)
Sparse Core Ops, SparseCore 0:
  46.9 49.4 all-gather.9
  183.1 169.6 reduce-scatter.9
  360.7 87.9 all-gather.7
  496.6 68.2 all-reduce.14
  574.9 68.1 all-reduce.14
  653.0 68.1 all-reduce.14
  727.0 126.7 reduce-scatter.15
  857.4 227.2 reduce-scatter.13
  1088.8 225.3 reduce-scatter.11
  1318.1 102.9 all-reduce.12
where the time goes:
time: 1440 us; the launch traced here: 1430 us
  waiting for transfers between devices  831 us (58%)
  blocking collectives  198 us (14%)
  local copies, waits for them, and re-layouts  181 us (13%)
  other arithmetic  155 us (11%)
  matrix products  47 us (3%)
  between operations  17 us (1%)
    reduce_scatter x1, waiting for transfers between devices, on_device(): lax.psum_scatter(embed_local, 'dp', scatter_dimension=1, tiled=True)  223 us
    while x6, waiting for transfers between devices  192 us
    reduce_scatter x1, waiting for transfers between devices, on_device(): lax.psum_scatter(neg_part, 'mp', scatter_dimension=0, tiled=True)  133 us
    psum x1, waiting for transfers between devices, on_device(): lax.psum((in_grad, hid_grad, bias_grad, cand_grad), 'dp')  101 us
    unnamed x3, blocking collectives  95.9 us
    unnamed x64, local copies, waits for them, and re-layouts  92.4 us
    reduce_scatter x1, waiting for transfers between devices, on_device(): lax.psum_scatter(table_local, 'dp', scatter_dimension=1, tiled=True)  90.4 us
    all_gather x1, waiting for transfers between devices, on_device(): lax.all_gather(neg_grad.astype(jnp.bfloat16), 'mp', axis=0, tiled=True)  80.7 us
  transfers between devices with their start and end apart: 11, of which 10 were waited for; matrix products, arithmetic and copies ran while one was open for 21% of the time, Pallas kernels for 0%

commit v1 on v0

v1 whole, which is shorter than its diff:
```python
import functools

import jax
import jax.numpy as jnp
from jax import lax
from jax.experimental import pallas as pl
from jax.experimental.pallas import tpu as pltpu
from jax.sharding import PartitionSpec as P

bpr_weight = 1.0
BF = jnp.bfloat16
F32 = jnp.float32
ITEM_BLOCK = 4096
CHUNK = 256
MIB = 1024 * 1024


def up(count, unit):
    return -(-count // unit) * unit


def lookup_kernel(has_bias, feats, cnt_ref, idr_ref, idc_ref, tab_ref, *rest):
    if has_bias:
        bias_ref, out_ref, perm, sid, xs, held, sems = rest
    else:
        out_ref, perm, sid, xs, held, sems = rest
    count = idr_ref.shape[1]
    blocks, _, width = held.shape

    def fetch(b):
        return pltpu.make_async_copy(
            tab_ref.at[:, pl.ds(b * width, width)], held.at[b], sems.at[b]
        )

    for b in range(blocks):
        fetch(b).start()
    lane = lax.broadcasted_iota(jnp.int32, (CHUNK, count), 1)
    keyr = idr_ref[...] * 4096 + lax.broadcasted_iota(jnp.int32, (1, count), 1)
    sid[...] = jnp.zeros_like(sid)

    def sort_rows(i, _):
        rows = pl.ds(pl.multiple_of(i * CHUNK, CHUNK), CHUNK)
        idc = idc_ref[rows, :]
        keyc = idc * 4096 + i * CHUNK + lax.broadcasted_iota(jnp.int32, (CHUNK, 1), 0)
        rank = jnp.sum((keyr < keyc).astype(F32), axis=1, keepdims=True).astype(jnp.int32)
        hit = rank == lane
        perm[rows, :] = hit.astype(F32).astype(BF)
        sid[...] += jnp.sum(jnp.where(hit, idc, 0).astype(F32), axis=0, keepdims=True)
        return 0

    lax.fori_loop(0, count // CHUNK, sort_rows, 0)
    xs[...] = jnp.zeros_like(xs)
    for b in range(blocks):
        fetch(b).wait()
        base = b * width

        def pick_chunk(c, _, b=b, base=base):
            cols = pl.ds(pl.multiple_of(c * CHUNK, CHUNK), CHUNK)
            ids = sid[:, cols].astype(jnp.int32) - base
            pick = (lax.broadcasted_iota(jnp.int32, (width, CHUNK), 0) == ids).astype(F32).astype(BF)
            xs[0:feats, cols] += jnp.dot(held[b], pick, preferred_element_type=F32)
            if has_bias:
                low = feats // 8 * 8
                value = bias_ref[:, base : base + width]
                first = value.astype(BF).astype(F32)
                second = (value - first).astype(BF).astype(F32)
                third = value - first - second
                row = lax.broadcasted_iota(jnp.int32, (8, width), 0) - (feats - low)
                parts = jnp.where(
                    row == 0, first, jnp.where(row == 1, second, jnp.where(row == 2, third, 0.0))
                ).astype(BF)
                xs[low : low + 8, cols] += jnp.dot(parts, pick, preferred_element_type=F32)
            return 0

        lax.fori_loop(
            cnt_ref[b] // CHUNK, (cnt_ref[b + 1] + CHUNK - 1) // CHUNK, pick_chunk, 0
        )
    out_ref[...] = lax.dot_general(
        perm[...], xs[...].astype(BF), (((1,), (1,)), ((), ())), preferred_element_type=F32
    ).astype(BF)


def lookup(ids, table, bias=None):
    feats, vocab = table.shape
    width = up(feats, 128)
    count = ids.shape[0]
    padded = up(count, CHUNK)
    ids = jnp.concatenate([ids, jnp.full((padded - count,), vocab, jnp.int32)])
    blocks = vocab // ITEM_BLOCK
    edges = jnp.arange(blocks + 1, dtype=jnp.int32) * ITEM_BLOCK
    cnt = jnp.sum((ids[None, :] < edges[:, None]).astype(jnp.int32), axis=1)
    vmem = pl.BlockSpec(memory_space=pltpu.VMEM)
    in_specs = [pl.BlockSpec(memory_space=pltpu.SMEM), vmem, vmem, pl.BlockSpec(memory_space=pl.ANY)]
    args = [cnt, ids.reshape(1, padded), ids.reshape(padded, 1), table]
    if bias is not None:
        in_specs.append(vmem)
        args.append(bias.reshape(1, vocab))
    return pl.pallas_call(
        functools.partial(lookup_kernel, bias is not None, feats),
        in_specs=in_specs,
        out_specs=vmem,
        scratch_shapes=[
            pltpu.VMEM((padded, padded), BF),
            pltpu.VMEM((1, padded), F32),
            pltpu.VMEM((width, padded), F32),
            pltpu.VMEM((blocks, feats, ITEM_BLOCK), BF),
            pltpu.SemaphoreType.DMA((blocks,)),
        ],
        out_shape=jax.ShapeDtypeStruct((padded, width), BF),
        compiler_params=pltpu.CompilerParams(vmem_limit_bytes=56 * MIB),
        cost_estimate=pl.CostEstimate(
            flops=2 * vocab * feats * 512, bytes_accessed=vocab * feats * 2, transcendentals=0
        ),
    )(*args)


def scatter_kernel(feats, tile, plan, base_ref, *refs):
    out_ref = refs[-1]
    first = base_ref[0] + pl.program_id(0) * tile
    out_ref[...] = jnp.zeros_like(out_ref)

    def add(piece, spot):
        out_ref[...] += lax.dot_general(
            piece, spot, (((0,), (0,)), ((), ())), preferred_element_type=F32
        )

    for ref, kind in zip(refs, plan):
        count, depth, _ = ref.shape

        def coded(part, _, ref=ref, depth=depth):
            wide = ref[part].astype(F32)
            ids = wide[:, feats + 1 : feats + 2] * 256.0 + wide[:, feats + 2 : feats + 3]
            lanes = lax.broadcasted_iota(jnp.int32, (depth, tile), 1)
            spot = jnp.where(lanes == ids.astype(jnp.int32) - first, wide[:, feats : feats + 1], 0.0)
            col = lax.broadcasted_iota(jnp.int32, wide.shape, 1)
            add(jnp.where(col == feats, 1.0, wide).astype(BF), spot.astype(BF))
            return 0

        def plain(part, _, ref=ref, depth=depth):
            rows = ref[part]
            ids = rows[:, feats + 1 : feats + 2].astype(jnp.int32) - first
            lanes = lax.broadcasted_iota(jnp.int32, (depth, tile), 1)
            spot = (lanes == ids).astype(F32).astype(BF)
            high = rows.astype(BF)
            add(high, spot)
            add((rows - high.astype(F32)).astype(BF), spot)
            return 0

        lax.fori_loop(0, count, coded if kind == "coded" else plain, 0)


def scatter(base, feats, items, arrays, plan):
    width = arrays[0].shape[-1]
    rows = sum(a.shape[0] * a.shape[1] * (1 if k == "coded" else 2) for a, k in zip(arrays, plan))
    tile = 512 if items % 512 == 0 else 128
    return pl.pallas_call(
        functools.partial(scatter_kernel, feats, tile, plan),
        grid=(items // tile,),
        in_specs=[pl.BlockSpec(memory_space=pltpu.SMEM)]
        + [pl.BlockSpec(memory_space=pltpu.VMEM)] * len(arrays),
        out_specs=pl.BlockSpec((width, tile), lambda i: (0, i)),
        out_shape=jax.ShapeDtypeStruct((width, items), F32),
        compiler_params=pltpu.CompilerParams(vmem_limit_bytes=56 * MIB),
        cost_estimate=pl.CostEstimate(
            flops=2 * rows * width * items, bytes_accessed=rows * width * 2, transcendentals=0
        ),
    )(base, *arrays)


def place_kernel(axis, where_ref, *refs):
    *pieces, out_ref, sems = refs
    copies = []
    for k, piece in enumerate(pieces):
        size = piece.shape[axis]
        spot = pl.ds(pl.multiple_of(where_ref[k] * size, size), size)
        target = out_ref.at[spot, :] if axis == 0 else out_ref.at[:, spot]
        copies.append(pltpu.make_async_copy(piece, target, sems.at[k]))
    for copy in copies:
        copy.start()
    for copy in copies:
        copy.wait()


def place(pieces, where, axis):
    shape = list(pieces[0].shape)
    shape[axis] *= len(pieces)
    anywhere = pl.BlockSpec(memory_space=pl.ANY)
    return pl.pallas_call(
        functools.partial(place_kernel, axis),
        in_specs=[pl.BlockSpec(memory_space=pltpu.SMEM)] + [anywhere] * len(pieces),
        out_specs=anywhere,
        scratch_shapes=[pltpu.SemaphoreType.DMA((len(pieces),))],
        out_shape=jax.ShapeDtypeStruct(tuple(shape), pieces[0].dtype),
        cost_estimate=pl.CostEstimate(
            flops=0, bytes_accessed=2 * sum(p.size * p.dtype.itemsize for p in pieces), transcendentals=0
        ),
    )(where, *pieces)


def swap(value, k, axis):
    count = lax.axis_size(axis)
    return lax.ppermute(value, axis, [(i, i ^ k) for i in range(count)])


def gather_mp(value):
    count = lax.axis_size("mp")
    pieces = [value] + [swap(value, k, "mp") for k in range(1, count)]
    where = lax.axis_index("mp") ^ jnp.arange(count, dtype=jnp.int32)
    return place(pieces, where, 1)


def gather_dp(value):
    count = lax.axis_size("dp")
    chips = [value] + [swap(value, k, "dp") for k in range(2, count, 2)]
    other = [swap(piece, 1, "dp") for piece in chips]
    return [piece for pair in zip(chips, other) for piece in pair]


def reduce_dp(blocks):
    kept, sent = blocks[0::2], blocks[1::2]
    got = swap(jnp.concatenate(sent), 1, "dp").reshape((len(kept),) + kept[0].shape)
    mine = [block + got[i] for i, block in enumerate(kept)]
    total = mine[0]
    for i in range(1, len(mine)):
        total = total + swap(mine[i], 2 * i, "dp")
    return total


def low(value):
    return lax.reduce_precision(value, 8, 7).astype(BF)


def on_device(
    item_ids,
    session_ends,
    negatives,
    embedding,
    in_weight,
    hid_weight,
    gate_bias,
    cand_bias,
    out_table,
    out_bias,
):
    dp, mp = lax.axis_size("dp"), lax.axis_size("mp")
    me_dp, me_mp = lax.axis_index("dp"), lax.axis_index("mp")
    order_dp = me_dp ^ jnp.arange(dp, dtype=jnp.int32)
    steps, slots = session_ends.shape
    events = steps * slots
    feats, vocab = embedding.shape
    units = hid_weight.shape[2]
    width = up(units, 128)
    full = mp * width
    neg_count = negatives.shape[0]
    neg_share = neg_count // dp

    end_float = session_ends.astype(F32)
    keep = jnp.concatenate([jnp.zeros((1, slots), F32), 1.0 - end_float[:-1]], axis=0)
    weight = ((1.0 - end_float) / (steps * slots * dp)).reshape(events, 1)
    sources = item_ids[:-1].reshape(events)
    targets = item_ids[1:].reshape(events)
    own_negs = lax.dynamic_slice_in_dim(negatives, me_dp * neg_share, neg_share)

    def padded_rows(value):
        value = value.reshape(3, mp, units, units)
        value = jnp.pad(value, ((0, 0), (0, 0), (0, width - units), (0, width - units)))
        return value.reshape(3 * full, width)

    share = 3 * full // dp
    in_share = lax.dynamic_slice_in_dim(padded_rows(in_weight), me_dp * share, share)
    hid_share = lax.dynamic_slice_in_dim(padded_rows(hid_weight), me_dp * share, share)
    biases = jnp.pad(
        jnp.concatenate([gate_bias, cand_bias[None]]), ((0, 0), (0, width - units))
    )
    first = low(biases)
    second = low(biases - first.astype(F32))
    third = low(biases - first.astype(F32) - second.astype(F32))
    bias_rows = jnp.concatenate([first, second, third, jnp.zeros((4, width), BF)])
    in_cols = gather_mp(jnp.concatenate([in_share, bias_rows]))
    bias_all = in_cols[share : share + 12].astype(F32)
    bias_all = bias_all[0:4] + bias_all[4:8] + bias_all[8:12]
    in_full = place(gather_dp(in_cols[:share]), order_dp, 0).reshape(3, full, full)
    hid_cols = gather_mp(hid_share)
    hid_full = place(gather_dp(hid_cols), order_dp, 0).reshape(3, full, full)

    x_rows = lookup(sources, embedding)[:events]
    x_all = gather_mp(x_rows)
    t_rows = lookup(jnp.concatenate([targets, own_negs]), out_table, out_bias)
    t_all = gather_mp(t_rows[: events + neg_share])
    tgt = t_all[:events]
    neg = jnp.concatenate(gather_dp(t_all[events:]))

    gi = jnp.einsum("ne,geh->gnh", x_all, in_full, preferred_element_type=F32)
    gi = gi.reshape(3, steps, slots, full)
    saved = []
    hidden = None
    for t in range(steps):
        if t == 0:
            prev = jnp.zeros((slots, full), F32)
            low_prev = low(prev)
            update = jax.nn.sigmoid(gi[0, t] + bias_all[0])
            reset = jax.nn.sigmoid(gi[1, t] + bias_all[1])
            inner = jnp.broadcast_to(bias_all[3], (slots, full))
        else:
            prev = hidden * keep[t][:, None]
            low_prev = low(prev)
            gh = jnp.einsum("bk,gkh->gbh", low_prev, hid_full, preferred_element_type=F32)
            update = jax.nn.sigmoid(gi[0, t] + gh[0] + bias_all[0])
            reset = jax.nn.sigmoid(gi[1, t] + gh[1] + bias_all[1])
            inner = gh[2] + bias_all[3]
        cand = jnp.tanh(gi[2, t] + bias_all[2] + reset * inner)
        hidden = (1.0 - update) * prev + update * cand
        saved.append((prev, low_prev, update, reset, inner, cand, hidden))
    shown = low(jnp.concatenate([s[6] for s in saved]))

    col = jnp.arange(full)
    is_bias = (col >= units) & (col < units + 3)
    shown_one = jnp.where(is_bias[None, :], BF(1.0), shown)
    s = jnp.einsum("nh,jh->nj", shown_one, neg, preferred_element_type=F32)
    u = jnp.sum(shown_one.astype(F32) * tgt.astype(F32), axis=1, keepdims=True)
    prob = jax.nn.softmax(s, axis=1)
    above = jax.nn.sigmoid(u - s)
    mixture = jnp.sum(prob * above, axis=1, keepdims=True)
    spread = jnp.sum(prob * s * s, axis=1, keepdims=True)
    loss_part = jnp.sum(weight * (-jnp.log(mixture) + bpr_weight * spread))
    neg_grad = weight * prob * (
        1.0 - above * above / mixture + bpr_weight * (s * s + 2.0 * s - spread)
    )
    tgt_grad = -weight * jnp.sum(prob * above * (1.0 - above), axis=1, keepdims=True) / mixture
    neg_low = low(neg_grad)
    tgt_low = low(tgt_grad)
    dhs = jnp.dot(neg_low, neg, preferred_element_type=F32) + tgt_low.astype(F32) * tgt.astype(F32)
    dhs = dhs.reshape(steps, slots, full)

    own_cols = lambda v: lax.dynamic_slice_in_dim(v, me_mp * width, width, axis=v.ndim - 1)
    own_shown = own_cols(shown)
    spare = jnp.arange(width)[None, :]
    tgt_hi = (targets // 256).astype(BF)[:, None]
    tgt_lo = (targets % 256).astype(BF)[:, None]
    rows = jnp.where(
        spare == units,
        tgt_low,
        jnp.where(spare == units + 1, tgt_hi, jnp.where(spare == units + 2, tgt_lo, own_shown)),
    )
    rows_all = gather_dp(rows)
    counted = jnp.where(spare == units, BF(1.0), own_shown)
    neg_table = jnp.einsum("nj,nh->jh", neg_low, counted, preferred_element_type=F32)
    neg_sum = reduce_dp([neg_table[k * neg_share : (k + 1) * neg_share] for k in range(dp)])
    neg_sum = jnp.where(spare == units + 1, own_negs.astype(F32)[:, None], neg_sum)
    neg_all = gather_dp(neg_sum)

    in_own = lax.dynamic_slice_in_dim(in_full, me_mp * width, width, axis=1)
    later = jnp.zeros((slots, full), F32)
    bias_sums = 0.0
    gi_low, gh_low, dx_all = [None] * steps, [None] * steps, []
    for t in reversed(range(steps)):
        prev, low_prev, update, reset, inner, cand, _ = saved[t]
        dh = later + dhs[t]
        dz = dh * (cand - prev) * update * (1.0 - update)
        da = dh * update * (1.0 - cand * cand)
        dr = da * inner * reset * (1.0 - reset)
        dq = da * reset
        zl, rl, al, ql = low(dz), low(dr), low(da), low(dq)
        bias_sums = bias_sums + jnp.stack([jnp.sum(own_cols(v), axis=0) for v in (dz, dr, da, dq)])
        if t > 0:
            back = jnp.einsum(
                "gbh,gkh->bk", jnp.stack([zl, rl, ql]), hid_full, preferred_element_type=F32
            )
            later = (dh * (1.0 - update) + back) * keep[t][:, None]
        dx = jnp.einsum("gbh,gkh->bk", jnp.stack([zl, rl, al]), in_own, preferred_element_type=F32)
        dx = jnp.where(
            spare == units + 1, sources[t * slots : (t + 1) * slots].astype(F32)[:, None], dx
        )
        dx_all += gather_dp(dx)
        gi_low[t] = jnp.stack([own_cols(v) for v in (zl, rl, al)])
        gh_low[t] = jnp.stack([own_cols(v) for v in (zl, rl, ql)])

    def summed(parts):
        flat = parts.reshape(dp, share, width)
        blocks = [lax.dynamic_index_in_dim(flat, order_dp[k], 0, keepdims=False) for k in range(dp)]
        return place(gather_dp(reduce_dp(blocks)), order_dp, 0).reshape(3, mp, width, width)

    low_prevs = jnp.concatenate([saved[t][1] for t in range(1, steps)])
    hid_parts = jnp.einsum(
        "nk,gnh->gkh", low_prevs, jnp.concatenate(gh_low[1:], axis=1), preferred_element_type=F32
    )
    hid_sum = summed(hid_parts)
    in_parts = jnp.einsum(
        "ne,gnh->geh", x_all, jnp.concatenate(gi_low, axis=1), preferred_element_type=F32
    )
    in_parts = in_parts.at[0, units : units + 2].set(bias_sums[0:2])
    in_parts = in_parts.at[1, units : units + 2].set(bias_sums[2:4])
    in_parts = in_parts.at[2, units].set(jnp.full((width,), loss_part))
    in_sum = summed(in_parts)

    gate_sum = jnp.stack([in_sum[0, 0, units], in_sum[0, 0, units + 1], in_sum[1, 0, units]])
    gate_sum, cand_sum = gate_sum[:, :units], in_sum[1, 0, units + 1, :units]
    loss_value = in_sum[2, 0, units, 0]
    unpad = lambda v: v[:, :, :units, :units].reshape(3, mp * units, units)

    items = vocab // dp
    base = (me_dp * items).astype(jnp.int32).reshape(1)
    table_sum = scatter(
        base,
        units,
        items,
        [jnp.stack(rows_all).reshape(-1, slots, width), jnp.stack(neg_all)],
        ("coded", "plain"),
    )
    embed_sum = scatter(base, units, items, [jnp.stack(dx_all)], ("plain",))
    return (
        loss_value,
        unpad(in_sum),
        unpad(hid_sum),
        gate_sum,
        cand_sum,
        embed_sum[:feats],
        table_sum[:units],
        table_sum[units],
    )


def solution(mesh):
    return jax.shard_map(
        on_device,
        mesh=mesh,
        in_specs=(
            P(None, "dp"),
            P(None, "dp"),
            P(),
            P("mp", None),
            P(None, None, "mp"),
            P(None, None, "mp"),
            P(None, "mp"),
            P("mp"),
            P("mp", None),
            P(),
        ),
        out_specs=(
            P(),
            P(None, None, "mp"),
            P(None, None, "mp"),
            P(None, "mp"),
            P("mp"),
            P("mp", "dp"),
            P("mp", "dp"),
            P("dp"),
        ),
        check_vma=False,
    )
```

time: 1440 us -> 1660 us (1.15)
  Pallas kernels: 0 us -> 1110 us
  waiting for transfers between devices: 831 us -> 130 us
  blocking collectives: 198 us -> 0 us
  starting transfers between devices: 2.83 us -> 110 us
  other arithmetic: 155 us -> 73.4 us
  local copies, waits for them, and re-layouts: 181 us -> 118 us
  matrix products: 47 us -> 87.5 us
    pallas_call x0 -> x12, Pallas kernels: none -> 1110 us  [the longest x8 794 us: place(): pl.pallas_call(functools.partial(place_kernel, axis), in_specs=[pl.BlockS...]
    reduce_scatter x3 -> x0, waiting for transfers between devices: 447 us -> none  [the longest x1 223 us: on_device(): lax.psum_scatter(embed_local, 'dp', scatter_dimension=1, tiled=True)]
    while x6 -> x0, waiting for transfers between devices: 192 us -> none
    ppermute x0 -> x94, waiting for transfers between devices: none -> 130 us  [swap(): return lax.ppermute(value, axis, [(i, i ^ k) for i in range(count)])]
    scatter-add x5 -> x0, other arithmetic: 113 us -> none  [the longest x2 69.8 us: on_device(): table_local = jnp.zeros(out_table.shape, jnp.float32).at[:, negatives].ad...]
    ppermute x0 -> x94, starting transfers between devices: none -> 110 us  [swap(): return lax.ppermute(value, axis, [(i, i ^ k) for i in range(count)])]
    psum x1 -> x0, waiting for transfers between devices: 101 us -> none  [on_device(): lax.psum((in_grad, hid_grad, bias_grad, cand_grad), 'dp')]
    unnamed x3 -> x0, blocking collectives: 95.9 us -> none
  transfers between devices with their start and end apart: 11 -> 94, of which waited for: 10 -> 21; matrix products, arithmetic and copies ran while one was open for 21% -> 8% of each run, Pallas kernels for 0% -> 50%
where the time goes in v1:
time: 1660 us; the launch traced here: 1650 us
  Pallas kernels  1110 us (67%)
  waiting for transfers between devices  130 us (8%)
  local copies, waits for them, and re-layouts  118 us (7%)
  starting transfers between devices  110 us (7%)
  matrix products  87.5 us (5%)
  other arithmetic  73.4 us (4%)
  between operations  17.6 us (1%)
    pallas_call x8, Pallas kernels, place(): pl.pallas_call(functools.partial(place_kernel, axis), in_specs=[pl.BlockS...  794 us
    pallas_call x2, Pallas kernels, scatter(): pl.pallas_call(functools.partial(scatter_kernel, feats, tile, plan), grid...  279 us
    ppermute x94, waiting for transfers between devices, swap(): return lax.ppermute(value, axis, [(i, i ^ k) for i in range(count)])  130 us
    ppermute x94, starting transfers between devices, swap(): return lax.ppermute(value, axis, [(i, i ^ k) for i in range(count)])  110 us
    pallas_call x2, Pallas kernels, lookup(): pl.pallas_call(functools.partial(lookup_kernel, bias is not None, feats),...  38.7 us
    unnamed x233, local copies, waits for them, and re-layouts  38 us
    convert_element_type x9, other arithmetic, low(): return lax.reduce_precision(value, 8, 7).astype(BF)  34.6 us
  transfers between devices with their start and end apart: 94, of which 21 were waited for; matrix products, arithmetic and copies ran while one was open for 8% of the time, Pallas kernels for 50%

profile of v1, /device:TPU:27, one launch (start us, length us, event | category | flops | bytes accessed | tf_op | source)
XLA Modules:
  0.0 1647.2 jit_solution(8403160135833212205)
XLA Ops:
  9.0 15.5 shard_map.163
  36.3 14.0 collective-permute-done.refs_1_
  53.3 23.2 %shard_map.167 = bf16[1536,256]{1,0:T(8,128)(2,1)} custom-call(s32[10]{0:T(128)} %convert_reduce_fusion.cnt_ref, s32[1,1536]{1,0:T(1,128)} %broadcast_in_dim.160.idr_ref, s32[1536,1]{1,0:T(8,128)} %reshape.525.idc_ref, bf16[250,36864]{1,0:T(8,128)(2,1)} %tab_ref.3, f32[1,36864]{1,0:T(1,128)} %bitcast.549), custom_call_target="tpu_custom_call" | custom-call | flops 9437184000 | bytes 18432000 | tf_op jit(solution)/shard_map/pallas_call | solution.py:98
  77.7 20.7 %collective-permute-done.1.refs_2_ = bf16[400,256]{1,0:T(8,128)(2,1)S(1)} collective-permute-done((bf16[400,256]{1,0:T(8,128)(2,1)S(1)}, bf16[400,256]{1,0:T(8,128)(2,1)S(1)}, u32[]{:S(2)}, u32[]{:S(2)}) %collective-permute-start.1) | collective-permute-done | bytes 204832 | tf_op jit(solution)/shard_map/ppermute | solution.py:202
  105.7 25.6 %shard_map.165.refs_0_ = bf16[384,1024]{1,0:T(8,128)(2,1)} custom-call(s32[4]{0:T(128)} %iota_xor_fusion.where_ref, bf16[384,256]{1,0:T(8,128)(2,1)} %copy-done.43, bf16[384,256]{1,0:T(8,128)(2,1)} %collective-permute-done.13.refs_1_, bf16[384,256]{1,0:T(8,128)(2,1)} %collective-permute-done.14.refs_2_, bf16[384,256]{1,0:T(8,128)(2,1)} %collective-permute-done.15.refs_3_), custom_call_target="tpu_custom_call" | custom-call | bytes 1572864 | tf_op jit(solution)/shard_map/pallas_call | solution.py:188
  156.6 26.6 %shard_map.161 = bf16[400,1024]{1,0:T(8,128)(2,1)} custom-call(s32[4]{0:T(128)} %iota_xor_fusion.where_ref, bf16[400,256]{1,0:T(8,128)(2,1)} %copy-done.35, bf16[400,256]{1,0:T(8,128)(2,1)} %copy-done.60, bf16[400,256]{1,0:T(8,128)(2,1)} %copy-done.61, bf16[400,256]{1,0:T(8,128)(2,1)} %copy-done.62), custom_call_target="tpu_custom_call" | custom-call | bytes 1638400 | tf_op jit(solution)/shard_map/pallas_call | solution.py:188
  187.3 89.3 %shard_map.168 = bf16[1408,1024]{1,0:T(8,128)(2,1)} custom-call(s32[4]{0:T(128)} %iota_xor_fusion.where_ref, bf16[1408,256]{1,0:T(8,128)(2,1)} %copy-done.16, bf16[1408,256]{1,0:T(8,128)(2,1)} %collective-permute-done.23.refs_1_, bf16[1408,256]{1,0:T(8,128)(2,1)} %copy-done.44, bf16[1408,256]{1,0:T(8,128)(2,1)} %collective-permute-done.25.refs_3_), custom_call_target="tpu_custom_call" | custom-call | bytes 5767168 | tf_op jit(solution)/shard_map/pallas_call | solution.py:188
  286.3 8.8 collective-permute-done.8.refs_6_
  320.9 73.3 %shard_map.164 = bf16[1152,1024]{1,0:T(8,128)(2,1)} custom-call(s32[4]{0:T(128)} %iota_xor_fusion.where_ref, bf16[1152,256]{1,0:T(8,128)(2,1)} %copy-done.17, bf16[1152,256]{1,0:T(8,128)(2,1)} %copy-done.45, bf16[1152,256]{1,0:T(8,128)(2,1)} %copy-done.46, bf16[1152,256]{1,0:T(8,128)(2,1)} %collective-permute-done.12.refs_3_), custom_call_target="tpu_custom_call" | custom-call | bytes 4718592 | tf_op jit(solution)/shard_map/pallas_call | solution.py:188
  399.1 192.4 %shard_map.166 = bf16[3072,1024]{1,0:T(8,128)(2,1)} custom-call(s32[8]{0:T(128)} %copy-done.63, bf16[384,1024]{1,0:T(8,128)(2,1)} %shard_map.165.refs_0_, bf16[384,1024]{1,0:T(8,128)(2,1)} %copy-done.36, bf16[384,1024]{1,0:T(8,128)(2,1)} %collective-permute-done.17.refs_2_, bf16[384,1024]{1,0:T(8,128)(2,1)} %copy-done.37, ...), custom_call_target="tpu_custom_call" | custom-call | bytes 12582912 | tf_op jit(solution)/shard_map/pallas_call | solution.py:188
  600.0 192.6 %shard_map.162 = bf16[3072,1024]{1,0:T(8,128)(2,1)} custom-call(s32[8]{0:T(128)} %copy-done.63, bf16[384,1024]{1,0:T(8,128)(2,1)} %copy-done.15, bf16[384,1024]{1,0:T(8,128)(2,1)} %collective-permute-done.3.refs_1_, bf16[384,1024]{1,0:T(8,128)(2,1)} %collective-permute-done.4.refs_2_, bf16[384,1024]{1,0:T(8,128)(2,1)} %collective-permute-done.5.refs_3_, ...), custom_call_target="tpu_custom_call" | custom-call | bytes 12582912 | tf_op jit(solution)/shard_map/pallas_call | solution.py:188
  792.6 13.8 convolution_bitcast_fusion
  806.4 15.2 copy.103
  826.9 8.2 convolution_bitcast_fusion.2
  835.1 9.2 convolution_bitcast_fusion.1
  852.3 8.0 fusion.218
  868.2 8.6 fusion.5
  877.5 10.2 fusion.10
  911.7 11.6 reduce-precision_convert_fusion.6
  1035.5 20.2 %collective-permute-done.65 = f32[384,256]{1,0:T(8,128)S(1)} collective-permute-done((f32[384,256]{1,0:T(8,128)S(1)}, f32[384,256]{1,0:T(8,128)S(1)}, u32[]{:S(2)}, u32[]{:S(2)}) %collective-permute-start.65) | collective-permute-done | bytes 393248 | tf_op jit(solution)/shard_map/ppermute | solution.py:202
  1098.3 152.7 %shard_map.172 = f32[256,4608]{1,0:T(8,128)} custom-call(s32[1]{0:T(128)} %bitcast.109.base_ref, bf16[24,384,256]{2,1,0:T(8,128)(2,1)} %bitcast.515, f32[8,256,256]{2,1,0:T(8,128)} %copy-done.72), custom_call_target="tpu_custom_call" | custom-call | flops 31406948352 | bytes 6815744 | tf_op jit(solution)/shard_map/pallas_call | solution.py:156
  1315.1 126.0 %shard_map.171 = f32[256,4608]{1,0:T(8,128)} custom-call(s32[1]{0:T(128)} %bitcast.109.base_ref, f32[24,384,256]{2,1,0:T(8,128)} %bitcast_dynamic-update-slice_fusion.8.refs_0_), custom_call_target="tpu_custom_call" | custom-call | flops 43486543872 | bytes 9437184 | tf_op jit(solution)/shard_map/pallas_call | solution.py:156
  1441.1 97.1 %shard_map.169 = f32[3072,256]{1,0:T(8,128)} custom-call(s32[8]{0:T(128)} %copy-done.63, f32[384,256]{1,0:T(8,128)} %copy-done.20, f32[384,256]{1,0:T(8,128)} %copy-done.50, f32[384,256]{1,0:T(8,128)} %copy-done.51, f32[384,256]{1,0:T(8,128)} %copy-done.58, f32[384,256]{1,0:T(8,128)} %copy-done.52, f32[384,256]{1,0:T(8,128)} %copy-done.59, ...), custom_call_target="tpu_custom_call" | custom-call | bytes 6291456 | tf_op jit(solution)/shard_map/pallas_call | solution.py:188
  1545.7 97.1 %shard_map.170 = f32[3072,256]{1,0:T(8,128)} custom-call(s32[8]{0:T(128)} %copy-done.63, f32[384,256]{1,0:T(8,128)} %copy-done.19, f32[384,256]{1,0:T(8,128)} %copy-done.57, f32[384,256]{1,0:T(8,128)} %copy-done.53, f32[384,256]{1,0:T(8,128)} %collective-permute-done.50.refs_3_, f32[384,256]{1,0:T(8,128)} %copy-done.54, ...), custom_call_target="tpu_custom_call" | custom-call | bytes 6291456 | tf_op jit(solution)/shard_map/pallas_call | solution.py:188
  (546 shorter events, 369.7 us)
Async XLA Ops:
  33.8 97.5 %collective-permute-start.11 = (bf16[1152,256]{1,0:T(8,128)(2,1)S(1)}, bf16[1152,256]{1,0:T(8,128)(2,1)S(1)}, u32[]{:S(2)}, u32[]{:S(2)}) collective-permute-start(bf16[1152,256]{1,0:T(8,128)(2,1)S(1)} %slice.445.refs_0_), channel_id=1, source_target_pairs={{0,2},{1,3},{2,0},{3,1},{4,6},{5,7},{6,4},{7,5},{8,10},{9,11},{10,... | collective-permute-start | bytes 1769480 | tf_op jit(solution)/shard_map/ppermute | solution.py:202
  33.9 103.4 %collective-permute-start.12 = (bf16[1152,256]{1,0:T(8,128)(2,1)S(1)}, bf16[1152,256]{1,0:T(8,128)(2,1)}, u32[]{:S(2)}, u32[]{:S(2)}) collective-permute-start(bf16[1152,256]{1,0:T(8,128)(2,1)S(1)} %slice.445.refs_0_), channel_id=1, source_target_pairs={{0,3},{1,2},{2,1},{3,0},{4,7},{5,6},{6,5},{7,4},{8,11},{9,10},{10,... | collective-permute-start | bytes 1769480 | tf_op jit(solution)/shard_map/ppermute | solution.py:202
  137.3 139.3 %collective-permute-start.17 = (bf16[384,1024]{1,0:T(8,128)(2,1)}, bf16[384,1024]{1,0:T(8,128)(2,1)}, u32[]{:S(2)}, u32[]{:S(2)}) collective-permute-start(bf16[384,1024]{1,0:T(8,128)(2,1)} %shard_map.165.refs_0_), channel_id=1, source_target_pairs={{0,8},{4,12},{8,0},{12,4},{16,24},{20,28},{24,16},{28,20},{1,9},{5... | collective-permute-start | bytes 2359304 | tf_op jit(solution)/shard_map/ppermute | solution.py:202
  153.4 126.4 %collective-permute-start.19 = (bf16[384,1024]{1,0:T(8,128)(2,1)}, bf16[384,1024]{1,0:T(8,128)(2,1)}, u32[]{:S(2)}, u32[]{:S(2)}) collective-permute-start(bf16[384,1024]{1,0:T(8,128)(2,1)} %shard_map.165.refs_0_), channel_id=1, source_target_pairs={{0,16},{4,20},{8,24},{12,28},{16,0},{20,4},{24,8},{28,12},{1,17},{... | collective-permute-start | bytes 2359304 | tf_op jit(solution)/shard_map/ppermute | solution.py:202
  154.7 127.0 %collective-permute-start.21 = (bf16[384,1024]{1,0:T(8,128)(2,1)}, bf16[384,1024]{1,0:T(8,128)(2,1)}, u32[]{:S(2)}, u32[]{:S(2)}) collective-permute-start(bf16[384,1024]{1,0:T(8,128)(2,1)} %shard_map.165.refs_0_), channel_id=1, source_target_pairs={{0,24},{4,28},{8,16},{12,20},{16,8},{20,12},{24,0},{28,4},{1,25},{... | collective-permute-start | bytes 2359304 | tf_op jit(solution)/shard_map/ppermute | solution.py:202
  184.5 98.6 %collective-permute-start.4 = (bf16[384,1024]{1,0:T(8,128)(2,1)S(1)}, bf16[384,1024]{1,0:T(8,128)(2,1)}, u32[]{:S(2)}, u32[]{:S(2)}) collective-permute-start(bf16[384,1024]{1,0:T(8,128)(2,1)S(1)} %slice.444.refs_0_), channel_id=1, source_target_pairs={{0,8},{4,12},{8,0},{12,4},{16,24},{20,28},{24,16},{28,20},{1,9},{5... | collective-permute-start | bytes 2359304 | tf_op jit(solution)/shard_map/ppermute | solution.py:202
  184.8 99.7 %collective-permute-start.6 = (bf16[384,1024]{1,0:T(8,128)(2,1)S(1)}, bf16[384,1024]{1,0:T(8,128)(2,1)}, u32[]{:S(2)}, u32[]{:S(2)}) collective-permute-start(bf16[384,1024]{1,0:T(8,128)(2,1)S(1)} %slice.444.refs_0_), channel_id=1, source_target_pairs={{0,16},{4,20},{8,24},{12,28},{16,0},{20,4},{24,8},{28,12},{1,17},{... | collective-permute-start | bytes 2359304 | tf_op jit(solution)/shard_map/ppermute | solution.py:202
  295.2 99.0 %collective-permute-start.18 = (bf16[384,1024]{1,0:T(8,128)(2,1)}, bf16[384,1024]{1,0:T(8,128)(2,1)S(1)}, u32[]{:S(2)}, u32[]{:S(2)}) collective-permute-start(bf16[384,1024]{1,0:T(8,128)(2,1)} %collective-permute-done.17.refs_2_), channel_id=1, source_target_pairs={{0,4},{4,0},{8,12},{12,8},{16,20},{20,16},{24,28},{28,24},{1,5},{5... | collective-permute-start | bytes 2359304 | tf_op jit(solution)/shard_map/ppermute | solution.py:202
  299.8 94.5 %collective-permute-start.20 = (bf16[384,1024]{1,0:T(8,128)(2,1)}, bf16[384,1024]{1,0:T(8,128)(2,1)S(1)}, u32[]{:S(2)}, u32[]{:S(2)}) collective-permute-start(bf16[384,1024]{1,0:T(8,128)(2,1)} %collective-permute-done.19.refs_4_), channel_id=1, source_target_pairs={{0,4},{4,0},{8,12},{12,8},{16,20},{20,16},{24,28},{28,24},{1,5},{5... | collective-permute-start | bytes 2359304 | tf_op jit(solution)/shard_map/ppermute | solution.py:202
  394.2 205.8 %collective-permute-start.3 = (bf16[384,1024]{1,0:T(8,128)(2,1)S(1)}, bf16[384,1024]{1,0:T(8,128)(2,1)}, u32[]{:S(2)}, u32[]{:S(2)}) collective-permute-start(bf16[384,1024]{1,0:T(8,128)(2,1)S(1)} %slice.444.refs_0_), channel_id=1, source_target_pairs={{0,4},{4,0},{8,12},{12,8},{16,20},{20,16},{24,28},{28,24},{1,5},{5... | collective-permute-start | bytes 2359304 | tf_op jit(solution)/shard_map/ppermute | solution.py:202
  394.3 205.7 %collective-permute-start.5 = (bf16[384,1024]{1,0:T(8,128)(2,1)}, bf16[384,1024]{1,0:T(8,128)(2,1)}, u32[]{:S(2)}, u32[]{:S(2)}) collective-permute-start(bf16[384,1024]{1,0:T(8,128)(2,1)} %collective-permute-done.4.refs_2_), channel_id=1, source_target_pairs={{0,4},{4,0},{8,12},{12,8},{16,20},{20,16},{24,28},{28,24},{1,5},{5... | collective-permute-start | bytes 2359304 | tf_op jit(solution)/shard_map/ppermute | solution.py:202
  394.8 205.2 %collective-permute-start.7 = (bf16[384,1024]{1,0:T(8,128)(2,1)}, bf16[384,1024]{1,0:T(8,128)(2,1)}, u32[]{:S(2)}, u32[]{:S(2)}) collective-permute-start(bf16[384,1024]{1,0:T(8,128)(2,1)} %collective-permute-done.6.refs_4_), channel_id=1, source_target_pairs={{0,4},{4,0},{8,12},{12,8},{16,20},{20,16},{24,28},{28,24},{1,5},{5... | collective-permute-start | bytes 2359304 | tf_op jit(solution)/shard_map/ppermute | solution.py:202
  394.9 205.1 %collective-permute-start.9 = (bf16[384,1024]{1,0:T(8,128)(2,1)}, bf16[384,1024]{1,0:T(8,128)(2,1)}, u32[]{:S(2)}, u32[]{:S(2)}) collective-permute-start(bf16[384,1024]{1,0:T(8,128)(2,1)} %collective-permute-done.8.refs_6_), channel_id=1, source_target_pairs={{0,4},{4,0},{8,12},{12,8},{16,20},{20,16},{24,28},{28,24},{1,5},{5... | collective-permute-start | bytes 2359304 | tf_op jit(solution)/shard_map/ppermute | solution.py:202
  397.2 200.9 %collective-permute-start.32 = (bf16[256,1024]{1,0:T(8,128)(2,1)}, bf16[256,1024]{1,0:T(8,128)(2,1)}, u32[]{:S(2)}, u32[]{:S(2)}) collective-permute-start(bf16[256,1024]{1,0:T(8,128)(2,1)} %copy-done.47), channel_id=1, source_target_pairs={{0,4},{4,0},{8,12},{12,8},{16,20},{20,16},{24,28},{28,24},{1,5},{5... | collective-permute-start | bytes 1572872 | tf_op jit(solution)/shard_map/ppermute | solution.py:202
  1074.4 176.7 %collective-permute-start.36 = (f32[384,256]{1,0:T(8,128)}, f32[384,256]{1,0:T(8,128)S(1)}, u32[]{:S(2)}, u32[]{:S(2)}) collective-permute-start(f32[384,256]{1,0:T(8,128)} %get-tuple-element.106), channel_id=1, source_target_pairs={{0,24},{4,28},{8,16},{12,20},{16,8},{20,12},{24,0},{28,4},{1,25},{... | collective-permute-start | bytes 1179656 | tf_op jit(solution)/shard_map/ppermute | solution.py:202
  1076.8 177.0 %collective-permute-start.35 = (f32[384,256]{1,0:T(8,128)}, f32[384,256]{1,0:T(8,128)}, u32[]{:S(2)}, u32[]{:S(2)}) collective-permute-start(f32[384,256]{1,0:T(8,128)} %get-tuple-element.107), channel_id=1, source_target_pairs={{0,16},{4,20},{8,24},{12,28},{16,0},{20,4},{24,8},{28,12},{1,17},{... | collective-permute-start | bytes 1179656 | tf_op jit(solution)/shard_map/ppermute | solution.py:202
  1090.1 164.7 %collective-permute-start.34 = (f32[384,256]{1,0:T(8,128)}, f32[384,256]{1,0:T(8,128)S(1)}, u32[]{:S(2)}, u32[]{:S(2)}) collective-permute-start(f32[384,256]{1,0:T(8,128)} %get-tuple-element.105), channel_id=1, source_target_pairs={{0,8},{4,12},{8,0},{12,4},{16,24},{20,28},{24,16},{28,20},{1,9},{5... | collective-permute-start | bytes 1179656 | tf_op jit(solution)/shard_map/ppermute | solution.py:202
  1092.5 162.6 %collective-permute-start.47 = (f32[384,256]{1,0:T(8,128)S(1)}, f32[384,256]{1,0:T(8,128)S(1)}, u32[]{:S(2)}, u32[]{:S(2)}) collective-permute-start(f32[384,256]{1,0:T(8,128)S(1)} %get-tuple-element.103), channel_id=1, source_target_pairs={{0,24},{4,28},{8,16},{12,20},{16,8},{20,12},{24,0},{28,4},{1,25},{... | collective-permute-start | bytes 1179656 | tf_op jit(solution)/shard_map/ppermute | solution.py:202
  1096.8 160.7 %collective-permute-start.46 = (f32[384,256]{1,0:T(8,128)}, f32[384,256]{1,0:T(8,128)S(1)}, u32[]{:S(2)}, u32[]{:S(2)}) collective-permute-start(f32[384,256]{1,0:T(8,128)} %get-tuple-element.104), channel_id=1, source_target_pairs={{0,16},{4,20},{8,24},{12,28},{16,0},{20,4},{24,8},{28,12},{1,17},{... | collective-permute-start | bytes 1179656 | tf_op jit(solution)/shard_map/ppermute | solution.py:202
  1303.6 241.3 %collective-permute-start.48 = (f32[384,256]{1,0:T(8,128)S(1)}, f32[384,256]{1,0:T(8,128)S(1)}, u32[]{:S(2)}, u32[]{:S(2)}) collective-permute-start(f32[384,256]{1,0:T(8,128)S(1)} %fusion.169.refs_0_), channel_id=1, source_target_pairs={{0,4},{4,0},{8,12},{12,8},{16,20},{20,16},{24,28},{28,24},{1,5},{5... | collective-permute-start | bytes 1179656 | tf_op jit(solution)/shard_map/ppermute | solution.py:202
  1306.1 135.0 %collective-permute-start.43 = (f32[384,256]{1,0:T(8,128)S(1)}, f32[384,256]{1,0:T(8,128)}, u32[]{:S(2)}, u32[]{:S(2)}) collective-permute-start(f32[384,256]{1,0:T(8,128)S(1)} %collective-permute-done.42.refs_6_), channel_id=1, source_target_pairs={{0,4},{4,0},{8,12},{12,8},{16,20},{20,16},{24,28},{28,24},{1,5},{5... | collective-permute-start | bytes 1179656 | tf_op jit(solution)/shard_map/ppermute | solution.py:202
  1313.1 231.8 %collective-permute-start.50 = (f32[384,256]{1,0:T(8,128)S(1)}, f32[384,256]{1,0:T(8,128)}, u32[]{:S(2)}, u32[]{:S(2)}) collective-permute-start(f32[384,256]{1,0:T(8,128)S(1)} %collective-permute-done.49.refs_2_), channel_id=1, source_target_pairs={{0,4},{4,0},{8,12},{12,8},{16,20},{20,16},{24,28},{28,24},{1,5},{5... | collective-permute-start | bytes 1179656 | tf_op jit(solution)/shard_map/ppermute | solution.py:202
  1314.5 230.4 %collective-permute-start.52 = (f32[384,256]{1,0:T(8,128)S(1)}, f32[384,256]{1,0:T(8,128)}, u32[]{:S(2)}, u32[]{:S(2)}) collective-permute-start(f32[384,256]{1,0:T(8,128)S(1)} %collective-permute-done.51.refs_4_), channel_id=1, source_target_pairs={{0,4},{4,0},{8,12},{12,8},{16,20},{20,16},{24,28},{28,24},{1,5},{5... | collective-permute-start | bytes 1179656 | tf_op jit(solution)/shard_map/ppermute | solution.py:202
  1314.6 230.4 %collective-permute-start.54 = (f32[384,256]{1,0:T(8,128)S(1)}, f32[384,256]{1,0:T(8,128)}, u32[]{:S(2)}, u32[]{:S(2)}) collective-permute-start(f32[384,256]{1,0:T(8,128)S(1)} %collective-permute-done.53.refs_6_), channel_id=1, source_target_pairs={{0,4},{4,0},{8,12},{12,8},{16,20},{20,16},{24,28},{28,24},{1,5},{5... | collective-permute-start | bytes 1179656 | tf_op jit(solution)/shard_map/ppermute | solution.py:202
  (167 other events, 4935.9 us)

commit v2 on v1

v2 whole, which is shorter than its diff:
```python
import functools

import jax
import jax.numpy as jnp
from jax import lax
from jax.experimental import pallas as pl
from jax.experimental.pallas import tpu as pltpu
from jax.sharding import PartitionSpec as P

bpr_weight = 1.0
BF = jnp.bfloat16
F32 = jnp.float32
ITEM_BLOCK = 4096
CHUNK = 256
MIB = 1024 * 1024


def up(count, unit):
    return -(-count // unit) * unit


def lookup_kernel(has_bias, feats, cnt_ref, idr_ref, idc_ref, tab_ref, *rest):
    if has_bias:
        bias_ref, out_ref, sid, order, perm, xs, held, sems = rest
    else:
        out_ref, sid, order, perm, xs, held, sems = rest
    count = idr_ref.shape[1]
    blocks, _, width = held.shape

    def fetch(b):
        return pltpu.make_async_copy(
            tab_ref.at[:, pl.ds(b * width, width)], held.at[b], sems.at[b]
        )

    for b in range(blocks):
        fetch(b).start()
    lane = lax.broadcasted_iota(jnp.int32, (CHUNK, count), 1)
    keyr = idr_ref[...] * 4096 + lax.broadcasted_iota(jnp.int32, (1, count), 1)
    sid[...] = jnp.zeros_like(sid)
    order[...] = jnp.zeros_like(order)

    def sort_rows(i, _):
        rows = pl.ds(pl.multiple_of(i * CHUNK, CHUNK), CHUNK)
        idc = idc_ref[rows, :]
        at = i * CHUNK + lax.broadcasted_iota(jnp.int32, (CHUNK, 1), 0)
        keyc = idc * 4096 + at
        rank = jnp.sum((keyr < keyc).astype(F32), axis=1, keepdims=True).astype(jnp.int32)
        hit = rank == lane
        perm[rows, :] = hit.astype(F32).astype(BF)
        sid[...] += jnp.sum(jnp.where(hit, idc, 0).astype(F32), axis=0, keepdims=True)
        order[...] += jnp.sum(jnp.where(hit, at, 0).astype(F32), axis=0, keepdims=True)
        return 0

    lax.fori_loop(0, count // CHUNK, sort_rows, 0)
    xs[...] = jnp.zeros_like(xs)
    for b in range(blocks):
        fetch(b).wait()
        base = b * width

        def pick_chunk(c, _, b=b, base=base):
            cols = pl.ds(pl.multiple_of(c * CHUNK, CHUNK), CHUNK)
            ids = sid[:, cols].astype(jnp.int32) - base
            pick = (lax.broadcasted_iota(jnp.int32, (width, CHUNK), 0) == ids).astype(F32).astype(BF)
            xs[0:feats, cols] += jnp.dot(held[b], pick, preferred_element_type=F32)
            if has_bias:
                low = feats // 8 * 8
                value = bias_ref[:, base : base + width]
                first = value.astype(BF).astype(F32)
                second = (value - first).astype(BF).astype(F32)
                third = value - first - second
                row = lax.broadcasted_iota(jnp.int32, (8, width), 0) - (feats - low)
                parts = jnp.where(
                    row == 0, first, jnp.where(row == 1, second, jnp.where(row == 2, third, 0.0))
                ).astype(BF)
                xs[low : low + 8, cols] += jnp.dot(parts, pick, preferred_element_type=F32)
            return 0

        lax.fori_loop(
            cnt_ref[b] // CHUNK, (cnt_ref[b + 1] + CHUNK - 1) // CHUNK, pick_chunk, 0
        )
    out_ref[...] = lax.dot_general(
        perm[...], xs[...].astype(BF), (((1,), (1,)), ((), ())), preferred_element_type=F32
    ).astype(BF)


def lookup(ids, table, bias=None):
    feats, vocab = table.shape
    width = up(feats, 128)
    count = ids.shape[0]
    padded = up(count, CHUNK)
    ids = jnp.concatenate([ids, jnp.full((padded - count,), vocab, jnp.int32)])
    blocks = vocab // ITEM_BLOCK
    edges = jnp.arange(blocks + 1, dtype=jnp.int32) * ITEM_BLOCK
    cnt = jnp.sum((ids[None, :] < edges[:, None]).astype(jnp.int32), axis=1)
    vmem = pl.BlockSpec(memory_space=pltpu.VMEM)
    in_specs = [pl.BlockSpec(memory_space=pltpu.SMEM), vmem, vmem, pl.BlockSpec(memory_space=pl.ANY)]
    args = [cnt, ids.reshape(1, padded), ids.reshape(padded, 1), table]
    if bias is not None:
        in_specs.append(vmem)
        args.append(bias.reshape(1, vocab))
    return pl.pallas_call(
        functools.partial(lookup_kernel, bias is not None, feats),
        in_specs=in_specs,
        out_specs=[vmem, vmem, vmem],
        scratch_shapes=[
            pltpu.VMEM((padded, padded), BF),
            pltpu.VMEM((width, padded), F32),
            pltpu.VMEM((blocks, feats, ITEM_BLOCK), BF),
            pltpu.SemaphoreType.DMA((blocks,)),
        ],
        out_shape=[
            jax.ShapeDtypeStruct((padded, width), BF),
            jax.ShapeDtypeStruct((1, padded), F32),
            jax.ShapeDtypeStruct((1, padded), F32),
        ],
        compiler_params=pltpu.CompilerParams(vmem_limit_bytes=56 * MIB),
        cost_estimate=pl.CostEstimate(
            flops=2 * vocab * feats * 512, bytes_accessed=vocab * feats * 2, transcendentals=0
        ),
    )(*args)


def scatter_kernel(feats, plan, base_ref, edge_ref, list_ref, *refs):
    refs = list(refs)
    scale_ref = refs.pop(0) if plan["scaled"] else None
    pieces = [refs.pop(0) for _ in range(plan["pieces"])]
    negs = [refs.pop(0) for _ in range(plan["negs"])]
    if plan["scaled"]:
        out_ref, bias_ref, total, held = refs
    else:
        out_ref, total = refs
    sources = plan["pieces"]
    base = base_ref[0]
    items, width = total.shape
    total[...] = jnp.zeros_like(total)
    if plan["scaled"]:
        depth = pieces[0].shape[0]
        each = held.shape[0] // sources
        col = lax.broadcasted_iota(jnp.int32, (depth, width), 1)
        for s in range(sources):
            wide = pieces[s][...].astype(F32)
            held[s * each : s * each + depth, :] = jnp.where(col == feats, 1.0, wide)
            held[s * each + depth : (s + 1) * each, :] = negs[s][...]

    for s in range(sources):

        def add(r, _, s=s):
            item = list_ref[s, 0, r] - base
            row = list_ref[s, 1, r]
            if plan["scaled"]:
                value = held[pl.ds(s * each + row, 1), :] * scale_ref[s, row]
            else:
                value = pieces[s][pl.ds(row, 1), :]
            total[pl.ds(item, 1), :] += value
            return 0

        lax.fori_loop(edge_ref[s, 0], edge_ref[s, 1], add, 0)
    tile = 512 if items % 512 == 0 else 128
    for at in range(0, items, tile):
        turned = total[at : at + tile, :].T
        out_ref[:, at : at + tile] = turned[:feats]
        if plan["scaled"]:
            bias_ref[:, at : at + tile] = turned[feats : feats + 1]


def scatter(base, feats, items, lists, pieces, scale=None, negs=()):
    width = pieces[0].shape[-1]
    sources = len(pieces)
    each = pieces[0].shape[0] + (negs[0].shape[0] if negs else 0)
    below = lambda v: jnp.sum((lists[:, 0] < v).astype(jnp.int32), axis=1)
    edges = jnp.stack([below(base), below(base + items)], axis=1)
    scaled = scale is not None
    plan = {"scaled": scaled, "pieces": sources, "negs": len(negs)}
    smem = pl.BlockSpec(memory_space=pltpu.SMEM)
    vmem = pl.BlockSpec(memory_space=pltpu.VMEM)
    out_shape = [jax.ShapeDtypeStruct((feats, items), F32)]
    scratch = [pltpu.VMEM((items, width), F32)]
    if scaled:
        out_shape.append(jax.ShapeDtypeStruct((1, items), F32))
        scratch.append(pltpu.VMEM((sources * each, width), F32))
    return pl.pallas_call(
        functools.partial(scatter_kernel, feats, plan),
        in_specs=[smem] * (4 if scaled else 3) + [vmem] * (sources + len(negs)),
        out_specs=[vmem] * len(out_shape),
        out_shape=out_shape,
        scratch_shapes=scratch,
        compiler_params=pltpu.CompilerParams(vmem_limit_bytes=56 * MIB),
        cost_estimate=pl.CostEstimate(
            flops=0, bytes_accessed=sources * each * width * 8, transcendentals=0
        ),
    )(base.reshape(1), edges, lists, *([scale] if scaled else []), *pieces, *negs)


def place_kernel(axis, where_ref, *refs):
    *pieces, out_ref, sems = refs
    copies = []
    for k, piece in enumerate(pieces):
        size = piece.shape[axis]
        spot = pl.ds(pl.multiple_of(where_ref[k] * size, size), size)
        target = out_ref.at[spot, :] if axis == 0 else out_ref.at[:, spot]
        copies.append(pltpu.make_async_copy(piece, target, sems.at[k]))
    for copy in copies:
        copy.start()
    for copy in copies:
        copy.wait()


def place(pieces, where, axis):
    shape = list(pieces[0].shape)
    shape[axis] *= len(pieces)
    anywhere = pl.BlockSpec(memory_space=pl.ANY)
    return pl.pallas_call(
        functools.partial(place_kernel, axis),
        in_specs=[pl.BlockSpec(memory_space=pltpu.SMEM)] + [anywhere] * len(pieces),
        out_specs=pl.BlockSpec(memory_space=pltpu.VMEM),
        scratch_shapes=[pltpu.SemaphoreType.DMA((len(pieces),))],
        out_shape=jax.ShapeDtypeStruct(tuple(shape), pieces[0].dtype),
        compiler_params=pltpu.CompilerParams(vmem_limit_bytes=32 * MIB),
        cost_estimate=pl.CostEstimate(
            flops=0, bytes_accessed=2 * sum(p.size * p.dtype.itemsize for p in pieces), transcendentals=0
        ),
    )(where, *pieces)


def forward_kernel(
    x_ref, keep_ref, in_ref, hid_ref, bias_ref, z_ref, r_ref, c_ref, q_ref, prev_ref, hb_ref, hs_ref, state, low_state
):
    t, q = pl.program_id(0), pl.program_id(1)
    width = z_ref.shape[2]
    cols = pl.ds(pl.multiple_of(q * width, width), width)

    @pl.when(t == 0)
    def _():
        state[:, cols] = jnp.zeros_like(prev_ref[0])

    @pl.when(q == 0)
    def _():
        low_state[...] = (state[...] * keep_ref[0]).astype(BF)

    x = x_ref[...]
    gi = [jnp.dot(x, in_ref[g], preferred_element_type=F32) + bias_ref[g : g + 1, :] for g in range(3)]
    q_ref[0] = jnp.broadcast_to(bias_ref[3:4, :], q_ref.shape[1:])
    z_ref[0] = gi[0]
    r_ref[0] = gi[1]

    @pl.when(t > 0)
    def _():
        low_prev = low_state[...]
        z_ref[0] += jnp.dot(low_prev, hid_ref[0], preferred_element_type=F32)
        r_ref[0] += jnp.dot(low_prev, hid_ref[1], preferred_element_type=F32)
        q_ref[0] += jnp.dot(low_prev, hid_ref[2], preferred_element_type=F32)

    prev = state[:, cols] * keep_ref[0]
    z = 1.0 / (1.0 + jnp.exp(-z_ref[0]))
    r = 1.0 / (1.0 + jnp.exp(-r_ref[0]))
    c = jnp.tanh(gi[2] + r * q_ref[0])
    h = (1.0 - z) * prev + z * c
    z_ref[0] = z
    r_ref[0] = r
    c_ref[0] = c
    prev_ref[0] = prev
    hb_ref[0] = prev.astype(BF)
    hs_ref[0] = h.astype(BF)
    state[:, cols] = h


def forward(steps, slots, width, x_all, keep, in_full, hid_full, bias_all):
    full = in_full.shape[2]
    parts = full // width
    tile = pl.BlockSpec((1, slots, width), lambda t, q: (t, 0, q))
    shape = lambda dtype: jax.ShapeDtypeStruct((steps, slots, full), dtype)
    return pl.pallas_call(
        forward_kernel,
        grid=(steps, parts),
        in_specs=[
            pl.BlockSpec((slots, full), lambda t, q: (t, 0)),
            pl.BlockSpec((1, slots, 1), lambda t, q: (t, 0, 0)),
            pl.BlockSpec((3, full, width), lambda t, q: (0, 0, q)),
            pl.BlockSpec((3, full, width), lambda t, q: (0, 0, jnp.where(t == 0, 0, q))),
            pl.BlockSpec((8, width), lambda t, q: (0, q)),
        ],
        out_specs=[tile] * 7,
        out_shape=[shape(F32)] * 5 + [shape(BF)] * 2,
        scratch_shapes=[pltpu.VMEM((slots, full), F32), pltpu.VMEM((slots, full), BF)],
        compiler_params=pltpu.CompilerParams(vmem_limit_bytes=48 * MIB),
        cost_estimate=pl.CostEstimate(
            flops=2 * 6 * steps * slots * full * full,
            bytes_accessed=steps * full * (slots * 24 + full * 12),
            transcendentals=3 * steps * slots * full,
        ),
    )(x_all, keep, in_full, hid_full, bias_all)


def score_kernel(
    rows, hs_ref, one_ref, tgt_ref, neg_ref, weight_ref, ds_ref, dhs_ref, du_ref, loss_ref, s_ref
):
    shown = hs_ref[...]
    s_ref[...] = lax.dot_general(
        shown + one_ref[...], neg_ref[...], (((1,), (1,)), ((), ())), preferred_element_type=F32
    )

    @pl.when(pl.program_id(0) == 0)
    def _():
        loss_ref[...] = jnp.zeros_like(loss_ref)

    def chunk(i, _):
        at = pl.ds(pl.multiple_of(i * rows, rows), rows)
        s = s_ref[at, :]
        w = weight_ref[at, :]
        tgt = tgt_ref[at, :].astype(F32)
        u = jnp.sum((hs_ref[at, :] + one_ref[...]).astype(F32) * tgt, axis=1, keepdims=True)
        top = jnp.max(s, axis=1, keepdims=True)
        e = jnp.exp(s - top)
        above = 1.0 / (1.0 + jnp.exp(s - u))
        ea = e * above
        inv = 1.0 / jnp.sum(e, axis=1, keepdims=True)
        mixture = jnp.sum(ea, axis=1, keepdims=True) * inv
        spread = jnp.sum(e * s * s, axis=1, keepdims=True) * inv
        slope = jnp.sum(ea * (1.0 - above), axis=1, keepdims=True) * inv
        ds = (w * inv) * e * (1.0 - above * above * (1.0 / mixture) + bpr_weight * (s * s + 2.0 * s - spread))
        ds_ref[at, :] = ds.astype(BF)
        du_ref[at, :] = (-w * slope / mixture).astype(BF).astype(F32)
        loss_ref[...] += jnp.broadcast_to(
            jnp.sum(w * (-jnp.log(mixture) + bpr_weight * spread), keepdims=True), loss_ref.shape
        )
        return 0

    lax.fori_loop(0, s_ref.shape[0] // rows, chunk, 0)
    dhs_ref[...] = (
        jnp.dot(ds_ref[...], neg_ref[...], preferred_element_type=F32)
        + du_ref[...] * tgt_ref[...].astype(F32)
    )


def scores(tile, shown, one_row, t_all, neg, weight):
    events, full = shown.shape
    count = neg.shape[0]
    row_tile = lambda w: pl.BlockSpec((tile, w), lambda i: (i, 0))
    return pl.pallas_call(
        functools.partial(score_kernel, 32),
        grid=(events // tile,),
        in_specs=[
            row_tile(full),
            pl.BlockSpec((1, full), lambda i: (0, 0)),
            row_tile(full),
            pl.BlockSpec(memory_space=pltpu.VMEM),
            row_tile(1),
        ],
        out_specs=[row_tile(count), row_tile(full), row_tile(1), pl.BlockSpec((8, 128), lambda i: (0, 0))],
        out_shape=[
            jax.ShapeDtypeStruct((events, count), BF),
            jax.ShapeDtypeStruct((events, full), F32),
            jax.ShapeDtypeStruct((events, 1), F32),
            jax.ShapeDtypeStruct((8, 128), F32),
        ],
        scratch_shapes=[pltpu.VMEM((tile, count), F32)],
        compiler_params=pltpu.CompilerParams(vmem_limit_bytes=48 * MIB),
        cost_estimate=pl.CostEstimate(
            flops=4 * events * full * count,
            bytes_accessed=events * (full * 8 + count * 2) + count * full * 2,
            transcendentals=3 * events * count,
        ),
    )(shown, one_row, t_all, neg, weight)


def backward_kernel(
    me_ref, z_ref, r_ref, c_ref, q_ref, prev_ref, keep_ref, dhs_ref, hid_ref, in_ref, dx_ref, own_ref, sum_ref, later, back
):
    i, q = pl.program_id(0), pl.program_id(1)
    last_step, last_part = pl.num_programs(0) - 1, pl.num_programs(1) - 1
    width = z_ref.shape[2]
    cols = pl.ds(pl.multiple_of(q * width, width), width)

    @pl.when((i == 0) & (q == 0))
    def _():
        later[...] = jnp.zeros_like(later)
        sum_ref[...] = jnp.zeros_like(sum_ref)

    @pl.when(q == 0)
    def _():
        dx_ref[...] = jnp.zeros_like(dx_ref)
        back[...] = jnp.zeros_like(back)

    z, r, c, inner = z_ref[0], r_ref[0], c_ref[0], q_ref[0]
    dh = later[:, cols] + dhs_ref[...]
    dz = dh * (c - prev_ref[0]) * z * (1.0 - z)
    da = dh * z * (1.0 - c * c)
    dr = da * inner * r * (1.0 - r)
    dq = da * r
    grads = (dz, dr, da, dq)
    zl, rl, al, ql = [v.astype(BF) for v in grads]
    over = (((1,), (1,)), ((), ()))
    for value, g in ((zl, 0), (rl, 1), (al, 2)):
        dx_ref[...] += lax.dot_general(value, in_ref[g], over, preferred_element_type=F32)

    @pl.when(i < last_step)
    def _():
        total = lax.dot_general(zl, hid_ref[0], over, preferred_element_type=F32)
        total += lax.dot_general(rl, hid_ref[1], over, preferred_element_type=F32)
        total += lax.dot_general(ql, hid_ref[2], over, preferred_element_type=F32)
        back[...] += total
        back[:, cols] += dh * (1.0 - z)

    @pl.when(q == me_ref[0])
    def _():
        for k, value in enumerate((zl, rl, al, ql)):
            own_ref[:, k * width : (k + 1) * width] = value
            sum_ref[k : k + 1, :] += jnp.sum(grads[k], axis=0, keepdims=True)

    @pl.when(q == last_part)
    def _():
        later[...] = back[...] * keep_ref[0]


def backward(width, me, z, r, c, inner, prev, keep, dhs, hid_full, in_full):
    steps, slots, full = z.shape
    parts = full // width
    tile = pl.BlockSpec((1, slots, width), lambda i, q, me: (steps - 1 - i, 0, q))
    row = lambda w: pl.BlockSpec((slots, w), lambda i, q, me: (steps - 1 - i, 0))
    return pl.pallas_call(
        backward_kernel,
        grid_spec=pltpu.PrefetchScalarGridSpec(
            num_scalar_prefetch=1,
            grid=(steps, parts),
            in_specs=[tile] * 5
            + [
                pl.BlockSpec((1, slots, 1), lambda i, q, me: (steps - 1 - i, 0, 0)),
                pl.BlockSpec((slots, width), lambda i, q, me: (steps - 1 - i, q)),
                pl.BlockSpec((3, full, width), lambda i, q, me: (0, 0, jnp.where(i == steps - 1, parts - 1, q))),
                pl.BlockSpec((3, width, width), lambda i, q, me: (0, me[0], q)),
            ],
            out_specs=[row(width), row(4 * width), pl.BlockSpec((8, width), lambda i, q, me: (0, 0))],
            scratch_shapes=[pltpu.VMEM((slots, full), F32), pltpu.VMEM((slots, full), F32)],
        ),
        out_shape=[
            jax.ShapeDtypeStruct((steps * slots, width), F32),
            jax.ShapeDtypeStruct((steps * slots, 4 * width), BF),
            jax.ShapeDtypeStruct((8, width), F32),
        ],
        compiler_params=pltpu.CompilerParams(vmem_limit_bytes=48 * MIB),
        cost_estimate=pl.CostEstimate(
            flops=2 * steps * slots * full * (3 * full + 3 * width),
            bytes_accessed=steps * full * (slots * 24 + full * 6),
            transcendentals=0,
        ),
    )(me, z, r, c, inner, prev, keep, dhs, hid_full, in_full)


def weights_kernel(units, order_ref, x_ref, hb_ref, own_ref, sum_ref, loss_ref, kept_ref, sent_ref, total):
    width = sum_ref.shape[1]
    slots = x_ref.shape[0] - hb_ref.shape[0]
    over = (((0,), (0,)), ((), ()))
    three = 3 * width
    total[:, :three] = lax.dot_general(x_ref[...], own_ref[:, :three], over, preferred_element_type=F32)
    hb = hb_ref[...]
    total[:, three : three + 2 * width] = lax.dot_general(
        hb, own_ref[slots:, : 2 * width], over, preferred_element_type=F32
    )
    total[:, three + 2 * width :] = lax.dot_general(
        hb, own_ref[slots:, three:], over, preferred_element_type=F32
    )
    for k in range(3):
        total[units : units + 1, k * width : (k + 1) * width] = sum_ref[k : k + 1, :]
    total[units + 1 : units + 2, :width] = sum_ref[3:4, :]
    total[units + 1 : units + 2, width : width + 128] = loss_ref[0:1, :]
    rows = kept_ref.shape[1]
    for k in range(kept_ref.shape[0]):
        for ref, at in ((kept_ref, 2 * k), (sent_ref, 2 * k + 1)):
            ref[k] = total[pl.ds(pl.multiple_of(order_ref[at] * rows, rows), rows), :]


def weight_grads(units, order, x_all, hb, own, sums, loss):
    full = x_all.shape[1]
    width = sums.shape[1]
    count = order.shape[0]
    half = jax.ShapeDtypeStruct((count // 2, full // count, 6 * width), F32)
    vmem = pl.BlockSpec(memory_space=pltpu.VMEM)
    return pl.pallas_call(
        functools.partial(weights_kernel, units),
        in_specs=[pl.BlockSpec(memory_space=pltpu.SMEM)] + [vmem] * 5,
        out_specs=[vmem, vmem],
        out_shape=[half, half],
        scratch_shapes=[pltpu.VMEM((full, 6 * width), F32)],
        compiler_params=pltpu.CompilerParams(vmem_limit_bytes=56 * MIB),
        cost_estimate=pl.CostEstimate(
            flops=2 * x_all.shape[0] * full * 6 * width,
            bytes_accessed=x_all.size * 4 + full * 24 * width,
            transcendentals=0,
        ),
    )(order, x_all, hb, own, sums, loss)


def swap(value, k, axis):
    count = lax.axis_size(axis)
    return lax.ppermute(value, axis, [(i, i ^ k) for i in range(count)])


def gather_mp(value):
    count = lax.axis_size("mp")
    pieces = [value] + [swap(value, k, "mp") for k in range(1, count)]
    where = lax.axis_index("mp") ^ jnp.arange(count, dtype=jnp.int32)
    return place(pieces, where, 1)


def gather_dp(value):
    count = lax.axis_size("dp")
    chips = [value] + [swap(value, k, "dp") for k in range(2, count, 2)]
    other = [swap(piece, 1, "dp") for piece in chips]
    return [piece for pair in zip(chips, other) for piece in pair]


def reduce_dp(kept, sent):
    mine = kept + swap(sent, 1, "dp")
    total = mine[0]
    for k in range(1, mine.shape[0]):
        total = total + swap(mine[k], 2 * k, "dp")
    return total


def low(value):
    return lax.reduce_precision(value, 8, 7).astype(BF)


def on_device(
    item_ids,
    session_ends,
    negatives,
    embedding,
    in_weight,
    hid_weight,
    gate_bias,
    cand_bias,
    out_table,
    out_bias,
):
    dp, mp = lax.axis_size("dp"), lax.axis_size("mp")
    me_dp, me_mp = lax.axis_index("dp"), lax.axis_index("mp")
    order_dp = me_dp ^ jnp.arange(dp, dtype=jnp.int32)
    steps, slots = session_ends.shape
    events = steps * slots
    feats, vocab = embedding.shape
    units = hid_weight.shape[2]
    width = up(units, 128)
    full = mp * width
    neg_count = negatives.shape[0]
    neg_share = neg_count // dp

    end_float = session_ends.astype(F32)
    keep = jnp.concatenate([jnp.zeros((1, slots), F32), 1.0 - end_float[:-1]], axis=0)
    weight = ((1.0 - end_float) / (steps * slots * dp)).reshape(events, 1)
    sources = item_ids[:-1].reshape(events)
    targets = item_ids[1:].reshape(events)
    own_negs = lax.dynamic_slice_in_dim(negatives, me_dp * neg_share, neg_share)

    def padded_rows(value):
        value = value.reshape(3, mp, units, units)
        value = jnp.pad(value, ((0, 0), (0, 0), (0, width - units), (0, width - units)))
        return value.reshape(3 * full, width)

    share = 3 * full // dp
    in_share = lax.dynamic_slice_in_dim(padded_rows(in_weight), me_dp * share, share)
    hid_share = lax.dynamic_slice_in_dim(padded_rows(hid_weight), me_dp * share, share)
    biases = jnp.pad(
        jnp.concatenate([gate_bias, cand_bias[None]]), ((0, 0), (0, width - units))
    )
    first = low(biases)
    second = low(biases - first.astype(F32))
    third = low(biases - first.astype(F32) - second.astype(F32))
    bias_rows = jnp.concatenate([first, second, third, jnp.zeros((4, width), BF)])
    in_cols = gather_mp(jnp.concatenate([in_share, bias_rows]))
    bias_all = in_cols[share : share + 12].astype(F32)
    bias_all = jnp.pad(bias_all[0:4] + bias_all[4:8] + bias_all[8:12], ((0, 4), (0, 0)))
    in_full = place(gather_dp(in_cols[:share]), order_dp, 0).reshape(3, full, full)
    hid_cols = gather_mp(hid_share)
    hid_full = place(gather_dp(hid_cols), order_dp, 0).reshape(3, full, full)

    x_rows, x_sid, x_order = lookup(sources, embedding)
    x_all = gather_mp(x_rows[:events])
    t_rows, t_sid, t_order = lookup(jnp.concatenate([targets, own_negs]), out_table, out_bias)
    t_all = gather_mp(t_rows[: events + neg_share])
    neg = jnp.concatenate(gather_dp(t_all[events:]))
    gap = ((0, 0), (0, t_sid.shape[1] - x_sid.shape[1]))
    lists = jnp.concatenate([jnp.pad(x_sid, gap), jnp.pad(x_order, gap), t_sid, t_order])
    lists = jnp.stack(gather_dp(lists.astype(jnp.int32)))
    x_lists = lists[:, 0:2, : x_sid.shape[1]]
    t_lists = lists[:, 2:4]

    z, r, c, inner, prev, hb, hs = forward(
        steps, slots, width, x_all, keep[:, :, None], in_full, hid_full, bias_all
    )
    shown = hs.reshape(events, full)
    col = jnp.arange(full)[None, :]
    one_row = ((col >= units) & (col < units + 3)).astype(BF)
    own_shown = lax.dynamic_slice_in_dim(shown, me_mp * width, width, axis=1)
    rows_all = gather_dp(own_shown)

    neg_low, dhs, tgt_low, loss = scores(slots, shown, one_row, t_all, neg, weight)

    counted = jnp.where(jnp.arange(width)[None, :] == units, BF(1.0), own_shown)
    neg_table = jnp.einsum("nj,nh->jh", neg_low, counted, preferred_element_type=F32)
    neg_table = neg_table.reshape(dp // 2, 2, neg_share, width)
    neg_sum = reduce_dp(neg_table[:, 0], neg_table[:, 1])
    scale_rows = up(-(-events // width), 8)
    scale = jnp.pad(tgt_low.reshape(events), (0, scale_rows * width - events))
    neg_all = gather_dp(jnp.concatenate([neg_sum, scale.reshape(scale_rows, width)]))
    scale_all = jnp.stack([v[neg_share:].reshape(-1)[:events] for v in neg_all])
    scale_all = jnp.concatenate([scale_all, jnp.ones((dp, neg_share), F32)], axis=1)

    dx, own, sums = backward(
        width, me_mp.reshape(1), z, r, c, inner, prev, keep[:, :, None], dhs, hid_full, in_full
    )
    dx_all = gather_dp(dx)
    kept, sent = weight_grads(
        units, order_dp, x_all, hb.reshape(events, full)[slots:], own, sums, loss
    )
    grads = place(gather_dp(reduce_dp(kept, sent)), order_dp, 0)
    gate_sum = grads[units, : 3 * width].reshape(3, width)[:, :units]
    cand_sum = grads[units + 1, :units]
    loss_value = grads[units + 1, width]
    grads = grads.reshape(mp, width, 2, 3, width)[:, :units, :, :, :units]
    grads = grads.transpose(2, 3, 0, 1, 4).reshape(2, 3, mp * units, units)

    items = vocab // dp
    base = (me_dp * items).astype(jnp.int32)
    table_sum, bias_sum = scatter(
        base, units, items, t_lists, rows_all, scale_all, [v[:neg_share] for v in neg_all]
    )
    (embed_sum,) = scatter(base, units, items, x_lists, dx_all)
    return (
        loss_value,
        grads[0],
        grads[1],
        gate_sum,
        cand_sum,
        embed_sum,
        table_sum,
        bias_sum.reshape(items),
    )


def solution(mesh):
    return jax.shard_map(
        on_device,
        mesh=mesh,
        in_specs=(
            P(None, "dp"),
            P(None, "dp"),
            P(),
            P("mp", None),
            P(None, None, "mp"),
            P(None, None, "mp"),
            P(None, "mp"),
            P("mp"),
            P("mp", None),
            P(),
        ),
        out_specs=(
            P(),
            P(None, None, "mp"),
            P(None, None, "mp"),
            P(None, "mp"),
            P("mp"),
            P("mp", "dp"),
            P("mp", "dp"),
            P("dp"),
        ),
        check_vma=False,
    )
```

time: 1660 us -> 702 us (0.42)
  Pallas kernels: 1110 us -> 213 us
  waiting for transfers between devices: 130 us -> 248 us
  matrix products: 87.5 us -> 4.1 us
  other arithmetic: 73.4 us -> 11.3 us
    pallas_call x8 -> x7, Pallas kernels: 794 us -> 14.3 us  [place(): pl.pallas_call(functools.partial(place_kernel, axis), in_specs=[pl.BlockS...]
    pallas_call x2 -> x6, Pallas kernels: 279 us -> 157 us  [the longest x2 66.3 us: scatter(): pl.pallas_call(functools.partial(scatter_kernel, feats, plan), in_specs=[...]
    ppermute x94 -> x76, waiting for transfers between devices: 130 us -> 248 us  [swap(): return lax.ppermute(value, axis, [(i, i ^ k) for i in range(count)])]
    dot_general x12 -> x0, matrix products: 83.5 us -> none  [the longest x2 18.4 us: on_device(): jnp.einsum('gbh,gkh->bk', jnp.stack([zl, rl, ql]), hid_full, preferred_el...]
    convert_element_type x9 -> x1, other arithmetic: 34.6 us -> 0.02 us  [low(): return lax.reduce_precision(value, 8, 7).astype(BF)]
    another operation x28 -> x14, local copies, waits for them, and re-layouts: 23.6 us -> 2.06 us  [the longest x2 1.35 us: scatter(): edges = jnp.stack([below(base), below(base + items)], axis=1)]
    reduce_sum x10 -> x2, other arithmetic: 19 us -> 0.8 us  [scatter(): below = lambda v: jnp.sum((lists[:, 0] < v).astype(jnp.int32), axis=1)]
    unnamed x233 -> x146, local copies, waits for them, and re-layouts: 38 us -> 31.6 us
  transfers between devices with their start and end apart: 94 -> 76, of which waited for: 21 -> 19; matrix products, arithmetic and copies ran while one was open for 8% -> 8% of each run, Pallas kernels for 50% -> 31%
where the time goes in v2:
time: 702 us; the launch traced here: 688 us
  waiting for transfers between devices  248 us (35%)
  Pallas kernels  213 us (30%)
  local copies, waits for them, and re-layouts  105 us (15%)
  starting transfers between devices  105 us (15%)
  other arithmetic  11.3 us (2%)
    ppermute x76, waiting for transfers between devices, swap(): return lax.ppermute(value, axis, [(i, i ^ k) for i in range(count)])  248 us
    ppermute x76, starting transfers between devices, swap(): return lax.ppermute(value, axis, [(i, i ^ k) for i in range(count)])  105 us
    pallas_call x2, Pallas kernels, scatter(): pl.pallas_call(functools.partial(scatter_kernel, feats, plan), in_specs=[...  66.3 us
    pallas_call x2, Pallas kernels, lookup(): pl.pallas_call(functools.partial(lookup_kernel, bias is not None, feats),...  41.5 us
    unnamed x146, local copies, waits for them, and re-layouts  31.6 us
    pallas_call x1, Pallas kernels, scores(): pl.pallas_call(functools.partial(score_kernel, 32), grid=(events // tile,...  30.7 us
    pallas_call x1, Pallas kernels, forward(): pl.pallas_call(forward_kernel, grid=(steps, parts), in_specs=[pl.BlockSpe...  27.8 us
    pallas_call x1, Pallas kernels, backward(): pl.pallas_call(backward_kernel, grid_spec=pltpu.PrefetchScalarGridSpec(nu...  22.3 us
  transfers between devices with their start and end apart: 76, of which 19 were waited for; matrix products, arithmetic and copies ran while one was open for 8% of the time, Pallas kernels for 31%

profile of v2, /device:TPU:27, one launch (start us, length us, event | category | flops | bytes accessed | tf_op | source)
XLA Modules:
  0.0 688.3 jit_solution(15789323467075795149)
XLA Ops:
  9.0 16.0 %shard_map.161 = (bf16[1280,256]{1,0:T(8,128)(2,1)}, f32[1,1280]{1,0:T(1,128)}, f32[1,1280]{1,0:T(1,128)}) custom-call(s32[10]{0:T(128)} %convert_reduce_fusion.1.cnt_ref, s32[1,1280]{1,0:T(1,128)} %broadcast_in_dim.34.idr_ref, s32[1280,1]{1,0:T(8,128)} %reshape.237.idc_ref, bf16[250,36864]{1,0:T(8,128)(2,1)} %tab_ref.2), custom_call_target="tpu_custom_call" | custom-call | flops 9437184000 | bytes 18432000 | tf_op jit(solution)/shard_map/pallas_call | solution.py:101
  38.9 9.9 %collective-permute-done.3.refs_1_ = bf16[400,256]{1,0:T(8,128)(2,1)S(1)} collective-permute-done((bf16[400,256]{1,0:T(8,128)(2,1)S(1)}, bf16[400,256]{1,0:T(8,128)(2,1)S(1)}, u32[]{:S(2)}, u32[]{:S(2)}) %collective-permute-start.3) | collective-permute-done | bytes 204832 | tf_op jit(solution)/shard_map/ppermute | solution.py:495
  51.8 25.5 %shard_map.168 = (bf16[1536,256]{1,0:T(8,128)(2,1)}, f32[1,1536]{1,0:T(1,128)}, f32[1,1536]{1,0:T(1,128)}) custom-call(s32[10]{0:T(128)} %convert_reduce_fusion.cnt_ref, s32[1,1536]{1,0:T(1,128)} %broadcast_in_dim.38.idr_ref, s32[1536,1]{1,0:T(8,128)} %reshape.238.idc_ref, bf16[250,36864]{1,0:T(8,128)(2,1)} %tab_ref.3, f32[1,36864]{1,0:T(1,128)} %bitcast.149), custom_call_target="tpu_custom_call" | custom-call | flops 9437184000 | bytes 18432000 | tf_op jit(solution)/shard_map/pallas_call | solution.py:101
  78.6 22.4 %collective-permute-done.4.refs_2_ = bf16[400,256]{1,0:T(8,128)(2,1)S(1)} collective-permute-done((bf16[400,256]{1,0:T(8,128)(2,1)S(1)}, bf16[400,256]{1,0:T(8,128)(2,1)S(1)}, u32[]{:S(2)}, u32[]{:S(2)}) %collective-permute-start.4) | collective-permute-done | bytes 204832 | tf_op jit(solution)/shard_map/ppermute | solution.py:495
  118.3 9.2 %collective-permute-done.23.refs_1_ = bf16[1408,256]{1,0:T(8,128)(2,1)S(1)} collective-permute-done((bf16[1408,256]{1,0:T(8,128)(2,1)S(1)}, bf16[1408,256]{1,0:T(8,128)(2,1)S(1)}, u32[]{:S(2)}, u32[]{:S(2)}) %collective-permute-start.23) | collective-permute-done | bytes 720928 | tf_op jit(solution)/shard_map/ppermute | solution.py:495
  128.7 22.9 %collective-permute-done.24.refs_2_ = bf16[1408,256]{1,0:T(8,128)(2,1)} collective-permute-done((bf16[1408,256]{1,0:T(8,128)(2,1)S(1)}, bf16[1408,256]{1,0:T(8,128)(2,1)}, u32[]{:S(2)}, u32[]{:S(2)}) %collective-permute-start.24) | collective-permute-done | bytes 720928 | tf_op jit(solution)/shard_map/ppermute | solution.py:495
  165.4 7.7 %collective-permute-start.26 = (bf16[256,1024]{1,0:T(8,128)(2,1)}, bf16[256,1024]{1,0:T(8,128)(2,1)}, u32[]{:S(2)}, u32[]{:S(2)}) collective-permute-start(bf16[256,1024]{1,0:T(8,128)(2,1)} %get-tuple-element.65), channel_id=1, source_target_pairs={{0,4},{4,0},{8,12},{12,8},{16,20},{20,16},{24,28},{28,24},{1,5},{5... | collective-permute-start | bytes 1572872 | tf_op jit(solution)/shard_map/ppermute | solution.py:495
  182.5 9.9 %collective-permute-done.9.refs_4_ = bf16[384,1024]{1,0:T(8,128)(2,1)} collective-permute-done((bf16[384,1024]{1,0:T(8,128)(2,1)}, bf16[384,1024]{1,0:T(8,128)(2,1)}, u32[]{:S(2)}, u32[]{:S(2)}) %collective-permute-start.9) | collective-permute-done | bytes 786464 | tf_op jit(solution)/shard_map/ppermute | solution.py:495
  199.1 14.6 %collective-permute-start.18 = (bf16[384,1024]{1,0:T(8,128)(2,1)}, bf16[384,1024]{1,0:T(8,128)(2,1)S(1)}, u32[]{:S(2)}, u32[]{:S(2)}) collective-permute-start(bf16[384,1024]{1,0:T(8,128)(2,1)} %collective-permute-done.17.refs_2_), channel_id=1, source_target_pairs={{0,4},{4,0},{8,12},{12,8},{16,20},{20,16},{24,28},{28,24},{1,5},{5... | collective-permute-start | bytes 2359304 | tf_op jit(solution)/shard_map/ppermute | solution.py:495
  213.7 9.8 %collective-permute-start.22 = (bf16[384,1024]{1,0:T(8,128)(2,1)}, bf16[384,1024]{1,0:T(8,128)(2,1)S(1)}, u32[]{:S(2)}, u32[]{:S(2)}) collective-permute-start(bf16[384,1024]{1,0:T(8,128)(2,1)} %collective-permute-done.21.refs_6_), channel_id=1, source_target_pairs={{0,4},{4,0},{8,12},{12,8},{16,20},{20,16},{24,28},{28,24},{1,5},{5... | collective-permute-start | bytes 2359304 | tf_op jit(solution)/shard_map/ppermute | solution.py:495
  250.6 27.8 %shard_map.167 = (f32[3,384,1024]{2,1,0:T(8,128)}, f32[3,384,1024]{2,1,0:T(8,128)}, f32[3,384,1024]{2,1,0:T(8,128)}, f32[3,384,1024]{2,1,0:T(8,128)}, f32[3,384,...) custom-call(bf16[1152,1024]{1,0:T(8,128)(2,1)} %copy-done.7, ...), custom_call_target="tpu_custom_call" | custom-call | flops 14495514624 | bytes 66060288 | tf_op jit(solution)/shard_map/pallas_call | solution.py:272
  279.6 30.7 %shard_map.170 = (bf16[1152,2048]{1,0:T(8,128)(2,1)}, f32[1152,1024]{1,0:T(8,128)}, f32[1152,1]{1,0:T(8,128)S(1)}, f32[8,128]{1,0:T(8,128)S(1)}) custom-call(bf16[1152,1024]{1,0:T(8,128)(2,1)S(1)} %bitcast.125, bf16[1,1024]{1,0:T(2,128)(2,1)S(1)} %and_convert_fusion.one_ref, bf16[1408,1024]{1,0:T(8,128)(2,1)} %copy-done.3, bf16[2048,1024]{1,0:T(8,128)(2,1)} %copy-done.50, ...), custom_call_target="tpu_custom_call" | custom-call | flops 9663676416 | bytes 18350080 | tf_op jit(solution)/shard_map/pallas_call | solution.py:339
  310.3 22.3 %shard_map.171 = (f32[1152,256]{1,0:T(8,128)S(1)}, bf16[1152,1024]{1,0:T(8,128)(2,1)S(1)}, f32[8,256]{1,0:T(8,128)S(1)}) custom-call(s32[1]{0:T(128)} %bitcast.7.me_ref, f32[3,384,1024]{2,1,0:T(8,128)} %get-tuple-element.34.z_ref, f32[3,384,1024]{2,1,0:T(8,128)} %get-tuple-element.35.r_ref, f32[3,384,1024]{2,1,0:T(8,128)} %get-tuple-element.36.c_ref, ...), custom_call_target="tpu_custom_call" | custom-call | flops 9059696640 | bytes 47185920 | tf_op jit(solution)/shard_map/pallas_call | solution.py:420
  334.6 9.7 %shard_map.172 = (f32[4,128,1536]{2,1,0:T(8,128)}, f32[4,128,1536]{2,1,0:T(8,128)}) custom-call(s32[8]{0:T(128)} %copy-done.25, bf16[1152,1024]{1,0:T(8,128)(2,1)} %copy-done.7, bf16[768,1024]{1,0:T(8,128)(2,1)} %bitcast.131, bf16[1152,1024]{1,0:T(8,128)(2,1)} %copy-done.27, f32[8,256]{1,0:T(8,128)} %copy-done.28, f32[8,128]{1,0:T(8,128)} %copy-done.29), custom_call_target="tpu_custom_call" | custom-call | flops 3623878656 | bytes 11010048 | tf_op jit(solution)/shard_map/pallas_call | solution.py:478
  364.1 8.8 %collective-permute-done.70.refs_3_ = bf16[1152,256]{1,0:T(8,128)(2,1)S(1)} collective-permute-done((bf16[1152,256]{1,0:T(8,128)(2,1)}, bf16[1152,256]{1,0:T(8,128)(2,1)S(1)}, u32[]{:S(2)}, u32[]{:S(2)}) %collective-permute-start.70) | collective-permute-done | bytes 589856 | tf_op jit(solution)/shard_map/ppermute | solution.py:495
  374.1 12.4 %collective-permute-done.72.refs_5_ = bf16[1152,256]{1,0:T(8,128)(2,1)S(1)} collective-permute-done((bf16[1152,256]{1,0:T(8,128)(2,1)}, bf16[1152,256]{1,0:T(8,128)(2,1)S(1)}, u32[]{:S(2)}, u32[]{:S(2)}) %collective-permute-start.72) | collective-permute-done | bytes 589856 | tf_op jit(solution)/shard_map/ppermute | solution.py:495
  386.8 29.7 %collective-permute-done.61 = f32[256,256]{1,0:T(8,128)S(1)} collective-permute-done((f32[256,256]{1,0:T(8,128)S(1)}, f32[256,256]{1,0:T(8,128)S(1)}, u32[]{:S(2)}, u32[]{:S(2)}) %collective-permute-start.61) | collective-permute-done | bytes 262176 | tf_op jit(solution)/shard_map/ppermute | solution.py:495
  433.3 36.2 %collective-permute-done.54.refs_4_ = f32[1152,256]{1,0:T(8,128)} collective-permute-done((f32[1152,256]{1,0:T(8,128)S(1)}, f32[1152,256]{1,0:T(8,128)}, u32[]{:S(2)}, u32[]{:S(2)}) %collective-permute-start.54) | collective-permute-done | bytes 1179680 | tf_op jit(solution)/shard_map/ppermute | solution.py:495
  480.8 40.0 %collective-permute-done.65 = f32[264,256]{1,0:T(8,128)S(1)} collective-permute-done((f32[264,256]{1,0:T(8,128)S(1)}, f32[264,256]{1,0:T(8,128)S(1)}, u32[]{:S(2)}, u32[]{:S(2)}) %collective-permute-start.65) | collective-permute-done | bytes 270368 | tf_op jit(solution)/shard_map/ppermute | solution.py:495
  536.3 8.0 %collective-permute-done.38.refs_2_ = f32[128,1536]{1,0:T(8,128)S(1)} collective-permute-done((f32[128,1536]{1,0:T(8,128)S(1)}, f32[128,1536]{1,0:T(8,128)S(1)}, u32[]{:S(2)}, u32[]{:S(2)}) %collective-permute-start.38) | collective-permute-done | bytes 786464 | tf_op jit(solution)/shard_map/ppermute | solution.py:495
  546.3 16.0 %collective-permute-done.40.refs_4_ = f32[128,1536]{1,0:T(8,128)S(1)} collective-permute-done((f32[128,1536]{1,0:T(8,128)S(1)}, f32[128,1536]{1,0:T(8,128)S(1)}, u32[]{:S(2)}, u32[]{:S(2)}) %collective-permute-start.40) | collective-permute-done | bytes 786464 | tf_op jit(solution)/shard_map/ppermute | solution.py:495
  577.3 37.8 %shard_map.175 = (f32[250,4608]{1,0:T(8,128)}, f32[1,4608]{1,0:T(1,128)}) custom-call(s32[1]{0:T(128)} %bitcast.17.base_ref, s32[8,2]{1,0:T(8,128)} %copy.75.edge_ref, s32[8,2,1536]{2,1,0:T(2,128)} %slice.248.list_ref, f32[8,1408]{1,0:T(8,128)} %concatenate.57.refs_0_, bf16[1152,256]{1,0:T(8,128)(2,1)} %constant_dynamic-slice_fusion.refs_1_, ...), custom_call_target="tpu_custom_call" | custom-call | bytes 23068672 | tf_op jit(solution)/shard_map/pallas_call | solution.py:181
  616.5 28.5 %shard_map.174 = f32[250,4608]{1,0:T(8,128)} custom-call(s32[1]{0:T(128)} %bitcast.17.base_ref, s32[8,2]{1,0:T(8,128)} %copy.72.edge_ref, s32[8,2,1280]{2,1,0:T(2,128)} %slice.246.list_ref, f32[1152,256]{1,0:T(8,128)} %copy-done.9, f32[1152,256]{1,0:T(8,128)} %collective-permute-done.51.refs_1_, f32[1152,256]{1,0:T(8,128)} %collective-permute-done.52.refs_2_, ...), custom_call_target="tpu_custom_call" | custom-call | bytes 18874368 | tf_op jit(solution)/shard_map/pallas_call | solution.py:181
  659.4 8.1 %reshape.224 = f32[4,256,2,3,256]{1,0,4,3,2:T(4,128)} reshape(f32[1024,1536]{0,1:T(8,128)} %copy.69) | data formatting | bytes 12582912 | tf_op jit(solution)/shard_map/reshape | solution.py:620
  (385 shorter events, 222.3 us)
Async XLA Ops:
  26.1 79.5 %collective-permute-start = (bf16[1152,256]{1,0:T(8,128)(2,1)S(1)}, bf16[1152,256]{1,0:T(8,128)(2,1)S(1)}, u32[]{:S(2)}, u32[]{:S(2)}) collective-permute-start(bf16[1152,256]{1,0:T(8,128)(2,1)S(1)} %slice.173.refs_0_), channel_id=1, source_target_pairs={{0,1},{1,0},{2,3},{3,2},{4,5},{5,4},{6,7},{7,6},{8,9},{9,8},{10,11... | collective-permute-start | bytes 1769480 | tf_op jit(solution)/shard_map/ppermute | solution.py:495
  36.4 76.4 %collective-permute-start.1 = (bf16[1152,256]{1,0:T(8,128)(2,1)S(1)}, bf16[1152,256]{1,0:T(8,128)(2,1)}, u32[]{:S(2)}, u32[]{:S(2)}) collective-permute-start(bf16[1152,256]{1,0:T(8,128)(2,1)S(1)} %slice.173.refs_0_), channel_id=1, source_target_pairs={{0,2},{1,3},{2,0},{3,1},{4,6},{5,7},{6,4},{7,5},{8,10},{9,11},{10,... | collective-permute-start | bytes 1769480 | tf_op jit(solution)/shard_map/ppermute | solution.py:495
  36.4 81.5 %collective-permute-start.2 = (bf16[1152,256]{1,0:T(8,128)(2,1)S(1)}, bf16[1152,256]{1,0:T(8,128)(2,1)}, u32[]{:S(2)}, u32[]{:S(2)}) collective-permute-start(bf16[1152,256]{1,0:T(8,128)(2,1)S(1)} %slice.173.refs_0_), channel_id=1, source_target_pairs={{0,3},{1,2},{2,1},{3,0},{4,7},{5,6},{6,5},{7,4},{8,11},{9,10},{10,... | collective-permute-start | bytes 1769480 | tf_op jit(solution)/shard_map/ppermute | solution.py:495
  38.5 62.4 %collective-permute-start.4 = (bf16[400,256]{1,0:T(8,128)(2,1)S(1)}, bf16[400,256]{1,0:T(8,128)(2,1)S(1)}, u32[]{:S(2)}, u32[]{:S(2)}) collective-permute-start(bf16[400,256]{1,0:T(8,128)(2,1)S(1)} %concatenate.47.refs_0_), channel_id=1, source_target_pairs={{0,2},{1,3},{2,0},{3,1},{4,6},{5,7},{6,4},{7,5},{8,10},{9,11},{10,... | collective-permute-start | bytes 614408 | tf_op jit(solution)/shard_map/ppermute | solution.py:495
  48.8 52.1 %collective-permute-start.5 = (bf16[400,256]{1,0:T(8,128)(2,1)S(1)}, bf16[400,256]{1,0:T(8,128)(2,1)S(1)}, u32[]{:S(2)}, u32[]{:S(2)}) collective-permute-start(bf16[400,256]{1,0:T(8,128)(2,1)S(1)} %concatenate.47.refs_0_), channel_id=1, source_target_pairs={{0,3},{1,2},{2,1},{3,0},{4,7},{5,6},{6,5},{7,4},{8,11},{9,10},{10,... | collective-permute-start | bytes 614408 | tf_op jit(solution)/shard_map/ppermute | solution.py:495
  101.6 50.0 %collective-permute-start.24 = (bf16[1408,256]{1,0:T(8,128)(2,1)S(1)}, bf16[1408,256]{1,0:T(8,128)(2,1)}, u32[]{:S(2)}, u32[]{:S(2)}) collective-permute-start(bf16[1408,256]{1,0:T(8,128)(2,1)S(1)} %slice.183.refs_0_), channel_id=1, source_target_pairs={{0,2},{1,3},{2,0},{3,1},{4,6},{5,7},{6,4},{7,5},{8,10},{9,11},{10,... | collective-permute-start | bytes 2162696 | tf_op jit(solution)/shard_map/ppermute | solution.py:495
  105.6 50.7 %collective-permute-start.25 = (bf16[1408,256]{1,0:T(8,128)(2,1)S(1)}, bf16[1408,256]{1,0:T(8,128)(2,1)}, u32[]{:S(2)}, u32[]{:S(2)}) collective-permute-start(bf16[1408,256]{1,0:T(8,128)(2,1)S(1)} %slice.183.refs_0_), channel_id=1, source_target_pairs={{0,3},{1,2},{2,1},{3,0},{4,7},{5,6},{6,5},{7,4},{8,11},{9,10},{10,... | collective-permute-start | bytes 2162696 | tf_op jit(solution)/shard_map/ppermute | solution.py:495
  165.4 48.3 %collective-permute-start.26 = (bf16[256,1024]{1,0:T(8,128)(2,1)}, bf16[256,1024]{1,0:T(8,128)(2,1)}, u32[]{:S(2)}, u32[]{:S(2)}) collective-permute-start(bf16[256,1024]{1,0:T(8,128)(2,1)} %get-tuple-element.65), channel_id=1, source_target_pairs={{0,4},{4,0},{8,12},{12,8},{16,20},{20,16},{24,28},{28,24},{1,5},{5... | collective-permute-start | bytes 1572872 | tf_op jit(solution)/shard_map/ppermute | solution.py:495
  243.2 109.2 %collective-permute-start.44 = (s32[4,1536]{1,0:T(4,128)S(1)}, s32[4,1536]{1,0:T(4,128)S(1)}, u32[]{:S(2)}, u32[]{:S(2)}) collective-permute-start(s32[4,1536]{1,0:T(4,128)S(1)} %maximum_convert_fusion.1), channel_id=1, source_target_pairs={{0,4},{4,0},{8,12},{12,8},{16,20},{20,16},{24,28},{28,24},{1,5},{5... | collective-permute-start | bytes 73736 | tf_op jit(solution)/shard_map/ppermute | solution.py:495
  243.8 109.9 %collective-permute-start.45 = (s32[4,1536]{1,0:T(4,128)S(1)}, s32[4,1536]{1,0:T(4,128)S(1)}, u32[]{:S(2)}, u32[]{:S(2)}) collective-permute-start(s32[4,1536]{1,0:T(4,128)S(1)} %maximum_convert_fusion.1), channel_id=1, source_target_pairs={{0,8},{4,12},{8,0},{12,4},{16,24},{20,28},{24,16},{28,20},{1,9},{5... | collective-permute-start | bytes 73736 | tf_op jit(solution)/shard_map/ppermute | solution.py:495
  244.1 110.4 %collective-permute-start.47 = (s32[4,1536]{1,0:T(4,128)S(1)}, s32[4,1536]{1,0:T(4,128)S(1)}, u32[]{:S(2)}, u32[]{:S(2)}) collective-permute-start(s32[4,1536]{1,0:T(4,128)S(1)} %maximum_convert_fusion.1), channel_id=1, source_target_pairs={{0,16},{4,20},{8,24},{12,28},{16,0},{20,4},{24,8},{28,12},{1,17},{... | collective-permute-start | bytes 73736 | tf_op jit(solution)/shard_map/ppermute | solution.py:495
  344.4 84.9 %collective-permute-start.33 = (f32[4,128,1536]{2,1,0:T(8,128)}, f32[4,128,1536]{2,1,0:T(8,128)}, u32[]{:S(2)}, u32[]{:S(2)}) collective-permute-start(f32[4,128,1536]{2,1,0:T(8,128)} %get-tuple-element.46), channel_id=1, source_target_pairs={{0,4},{4,0},{8,12},{12,8},{16,20},{20,16},{24,28},{28,24},{1,5},{5... | collective-permute-start | bytes 9437192 | tf_op jit(solution)/shard_map/ppermute | solution.py:495
  363.8 63.5 %collective-permute-start.51 = (f32[1152,256]{1,0:T(8,128)S(1)}, f32[1152,256]{1,0:T(8,128)}, u32[]{:S(2)}, u32[]{:S(2)}) collective-permute-start(f32[1152,256]{1,0:T(8,128)S(1)} %get-tuple-element.51.refs_0_), channel_id=1, source_target_pairs={{0,4},{4,0},{8,12},{12,8},{16,20},{20,16},{24,28},{28,24},{1,5},{5... | collective-permute-start | bytes 3538952 | tf_op jit(solution)/shard_map/ppermute | solution.py:495
  372.9 56.3 %collective-permute-start.52 = (f32[1152,256]{1,0:T(8,128)S(1)}, f32[1152,256]{1,0:T(8,128)}, u32[]{:S(2)}, u32[]{:S(2)}) collective-permute-start(f32[1152,256]{1,0:T(8,128)S(1)} %get-tuple-element.51.refs_0_), channel_id=1, source_target_pairs={{0,8},{4,12},{8,0},{12,4},{16,24},{20,28},{24,16},{28,20},{1,9},{5... | collective-permute-start | bytes 3538952 | tf_op jit(solution)/shard_map/ppermute | solution.py:495
  417.7 51.8 %collective-permute-start.54 = (f32[1152,256]{1,0:T(8,128)S(1)}, f32[1152,256]{1,0:T(8,128)}, u32[]{:S(2)}, u32[]{:S(2)}) collective-permute-start(f32[1152,256]{1,0:T(8,128)S(1)} %get-tuple-element.51.refs_0_), channel_id=1, source_target_pairs={{0,16},{4,20},{8,24},{12,28},{16,0},{20,4},{24,8},{28,12},{1,17},{... | collective-permute-start | bytes 3538952 | tf_op jit(solution)/shard_map/ppermute | solution.py:495
  423.6 47.9 %collective-permute-start.56 = (f32[1152,256]{1,0:T(8,128)S(1)}, f32[1152,256]{1,0:T(8,128)}, u32[]{:S(2)}, u32[]{:S(2)}) collective-permute-start(f32[1152,256]{1,0:T(8,128)S(1)} %get-tuple-element.51.refs_0_), channel_id=1, source_target_pairs={{0,24},{4,28},{8,16},{12,20},{16,8},{20,12},{24,0},{28,4},{1,25},{... | collective-permute-start | bytes 3538952 | tf_op jit(solution)/shard_map/ppermute | solution.py:495
  471.8 51.4 %collective-permute-start.36 = (f32[128,1536]{1,0:T(8,128)S(1)}, f32[128,1536]{1,0:T(8,128)S(1)}, u32[]{:S(2)}, u32[]{:S(2)}) collective-permute-start(f32[128,1536]{1,0:T(8,128)S(1)} %get-tuple-element.63), channel_id=1, source_target_pairs={{0,24},{4,28},{8,16},{12,20},{16,8},{20,12},{24,0},{28,4},{1,25},{... | collective-permute-start | bytes 2359304 | tf_op jit(solution)/shard_map/ppermute | solution.py:495
  473.9 49.8 %collective-permute-start.35 = (f32[128,1536]{1,0:T(8,128)S(1)}, f32[128,1536]{1,0:T(8,128)S(1)}, u32[]{:S(2)}, u32[]{:S(2)}) collective-permute-start(f32[128,1536]{1,0:T(8,128)S(1)} %get-tuple-element.64), channel_id=1, source_target_pairs={{0,16},{4,20},{8,24},{12,28},{16,0},{20,4},{24,8},{28,12},{1,17},{... | collective-permute-start | bytes 2359304 | tf_op jit(solution)/shard_map/ppermute | solution.py:495
  474.2 49.6 %collective-permute-start.34 = (f32[128,1536]{1,0:T(8,128)S(1)}, f32[128,1536]{1,0:T(8,128)S(1)}, u32[]{:S(2)}, u32[]{:S(2)}) collective-permute-start(f32[128,1536]{1,0:T(8,128)S(1)} %get-tuple-element.62), channel_id=1, source_target_pairs={{0,8},{4,12},{8,0},{12,4},{16,24},{20,28},{24,16},{28,20},{1,9},{5... | collective-permute-start | bytes 2359304 | tf_op jit(solution)/shard_map/ppermute | solution.py:495
  533.6 82.8 %collective-permute-start.57 = (f32[1152,256]{1,0:T(8,128)}, f32[1152,256]{1,0:T(8,128)}, u32[]{:S(2)}, u32[]{:S(2)}) collective-permute-start(f32[1152,256]{1,0:T(8,128)} %collective-permute-done.56.refs_6_), channel_id=1, source_target_pairs={{0,4},{4,0},{8,12},{12,8},{16,20},{20,16},{24,28},{28,24},{1,5},{5... | collective-permute-start | bytes 3538952 | tf_op jit(solution)/shard_map/ppermute | solution.py:495
  536.2 108.7 %collective-permute-start.37 = (f32[128,1536]{1,0:T(8,128)S(1)}, f32[128,1536]{1,0:T(8,128)}, u32[]{:S(2)}, u32[]{:S(2)}) collective-permute-start(f32[128,1536]{1,0:T(8,128)S(1)} %fusion.3.refs_0_), channel_id=1, source_target_pairs={{0,4},{4,0},{8,12},{12,8},{16,20},{20,16},{24,28},{28,24},{1,5},{5... | collective-permute-start | bytes 2359304 | tf_op jit(solution)/shard_map/ppermute | solution.py:495
  544.3 100.7 %collective-permute-start.39 = (f32[128,1536]{1,0:T(8,128)S(1)}, f32[128,1536]{1,0:T(8,128)}, u32[]{:S(2)}, u32[]{:S(2)}) collective-permute-start(f32[128,1536]{1,0:T(8,128)S(1)} %collective-permute-done.38.refs_2_), channel_id=1, source_target_pairs={{0,4},{4,0},{8,12},{12,8},{16,20},{20,16},{24,28},{28,24},{1,5},{5... | collective-permute-start | bytes 2359304 | tf_op jit(solution)/shard_map/ppermute | solution.py:495
  562.3 82.7 %collective-permute-start.41 = (f32[128,1536]{1,0:T(8,128)S(1)}, f32[128,1536]{1,0:T(8,128)}, u32[]{:S(2)}, u32[]{:S(2)}) collective-permute-start(f32[128,1536]{1,0:T(8,128)S(1)} %collective-permute-done.40.refs_4_), channel_id=1, source_target_pairs={{0,4},{4,0},{8,12},{12,8},{16,20},{20,16},{24,28},{28,24},{1,5},{5... | collective-permute-start | bytes 2359304 | tf_op jit(solution)/shard_map/ppermute | solution.py:495
  563.5 81.5 %collective-permute-start.43 = (f32[128,1536]{1,0:T(8,128)S(1)}, f32[128,1536]{1,0:T(8,128)}, u32[]{:S(2)}, u32[]{:S(2)}) collective-permute-start(f32[128,1536]{1,0:T(8,128)S(1)} %collective-permute-done.42.refs_6_), channel_id=1, source_target_pairs={{0,4},{4,0},{8,12},{12,8},{16,20},{20,16},{24,28},{28,24},{1,5},{5... | collective-permute-start | bytes 2359304 | tf_op jit(solution)/shard_map/ppermute | solution.py:495
  (111 other events, 2559.2 us)

commit v3 on v2

v3 whole, which is shorter than its diff:
```python
import functools

import jax
import jax.numpy as jnp
from jax import lax
from jax.experimental import pallas as pl
from jax.experimental.pallas import tpu as pltpu
from jax.sharding import PartitionSpec as P

bpr_weight = 1.0
BF = jnp.bfloat16
F32 = jnp.float32
ITEM_BLOCK = 4096
CHUNK = 256
MIB = 1024 * 1024


def up(count, unit):
    return -(-count // unit) * unit


def lookup_kernel(has_bias, feats, cnt_ref, idr_ref, idc_ref, tab_ref, *rest):
    if has_bias:
        bias_ref, out_ref, sid, order, perm, xs, held, sems = rest
    else:
        out_ref, sid, order, perm, xs, held, sems = rest
    count = idr_ref.shape[1]
    blocks, _, width = held.shape

    def fetch(b):
        return pltpu.make_async_copy(
            tab_ref.at[:, pl.ds(b * width, width)], held.at[b], sems.at[b]
        )

    for b in range(blocks):
        fetch(b).start()
    lane = lax.broadcasted_iota(jnp.int32, (CHUNK, count), 1)
    keyr = idr_ref[...] * 4096 + lax.broadcasted_iota(jnp.int32, (1, count), 1)
    sid[...] = jnp.zeros_like(sid)
    order[...] = jnp.zeros_like(order)

    def sort_rows(i, _):
        rows = pl.ds(pl.multiple_of(i * CHUNK, CHUNK), CHUNK)
        idc = idc_ref[rows, :]
        at = i * CHUNK + lax.broadcasted_iota(jnp.int32, (CHUNK, 1), 0)
        keyc = idc * 4096 + at
        rank = jnp.sum((keyr < keyc).astype(F32), axis=1, keepdims=True).astype(jnp.int32)
        hit = rank == lane
        perm[rows, :] = hit.astype(F32).astype(BF)
        sid[...] += jnp.sum(jnp.where(hit, idc, 0).astype(F32), axis=0, keepdims=True)
        order[...] += jnp.sum(jnp.where(hit, at, 0).astype(F32), axis=0, keepdims=True)
        return 0

    lax.fori_loop(0, count // CHUNK, sort_rows, 0)
    xs[...] = jnp.zeros_like(xs)
    for b in range(blocks):
        fetch(b).wait()
        base = b * width

        def pick_chunk(c, _, b=b, base=base):
            cols = pl.ds(pl.multiple_of(c * CHUNK, CHUNK), CHUNK)
            ids = sid[:, cols].astype(jnp.int32) - base
            pick = (lax.broadcasted_iota(jnp.int32, (width, CHUNK), 0) == ids).astype(F32).astype(BF)
            xs[0:feats, cols] += jnp.dot(held[b], pick, preferred_element_type=F32)
            return 0

        lax.fori_loop(
            cnt_ref[b] // CHUNK, (cnt_ref[b + 1] + CHUNK - 1) // CHUNK, pick_chunk, 0
        )
    out = lax.dot_general(
        perm[...], xs[...].astype(BF), (((1,), (1,)), ((), ())), preferred_element_type=F32
    )
    if has_bias:
        value = bias_ref[...]
        first = value.astype(BF).astype(F32)
        second = (value - first).astype(BF).astype(F32)
        parts = (first, second, value - first - second)
        groups = value.shape[0]
        idc = idc_ref[...]
        group = (idc // 128 == lax.broadcasted_iota(jnp.int32, (count, groups), 1)).astype(F32).astype(BF)
        member = lax.broadcasted_iota(jnp.int32, (count, 128), 1) == idc % 128
        col = lax.broadcasted_iota(jnp.int32, out.shape, 1)
        for k, part in enumerate(parts):
            near = jnp.dot(group, part.astype(BF), preferred_element_type=F32)
            own = jnp.sum(jnp.where(member, near, 0.0), axis=1, keepdims=True)
            out = jnp.where(col == feats + k, own, out)
    out_ref[...] = out.astype(BF)


def lookup(ids, table, bias=None):
    feats, vocab = table.shape
    width = up(feats, 128)
    count = ids.shape[0]
    padded = up(count, CHUNK)
    ids = jnp.concatenate([ids, jnp.full((padded - count,), vocab, jnp.int32)])
    blocks = vocab // ITEM_BLOCK
    edges = jnp.arange(blocks + 1, dtype=jnp.int32) * ITEM_BLOCK
    cnt = jnp.sum((ids[None, :] < edges[:, None]).astype(jnp.int32), axis=1)
    vmem = pl.BlockSpec(memory_space=pltpu.VMEM)
    in_specs = [pl.BlockSpec(memory_space=pltpu.SMEM), vmem, vmem, pl.BlockSpec(memory_space=pl.ANY)]
    args = [cnt, ids.reshape(1, padded), ids.reshape(padded, 1), table]
    if bias is not None:
        in_specs.append(vmem)
        args.append(bias.reshape(vocab // 128, 128))
    return pl.pallas_call(
        functools.partial(lookup_kernel, bias is not None, feats),
        in_specs=in_specs,
        out_specs=[vmem, vmem, vmem],
        scratch_shapes=[
            pltpu.VMEM((padded, padded), BF),
            pltpu.VMEM((width, padded), F32),
            pltpu.VMEM((blocks, feats, ITEM_BLOCK), BF),
            pltpu.SemaphoreType.DMA((blocks,)),
        ],
        out_shape=[
            jax.ShapeDtypeStruct((padded, width), BF),
            jax.ShapeDtypeStruct((1, padded), F32),
            jax.ShapeDtypeStruct((1, padded), F32),
        ],
        compiler_params=pltpu.CompilerParams(vmem_limit_bytes=56 * MIB),
        cost_estimate=pl.CostEstimate(
            flops=2 * vocab * feats * 512, bytes_accessed=vocab * feats * 2, transcendentals=0
        ),
    )(*args)


def scatter_kernel(feats, plan, base_ref, edge_ref, list_ref, *refs):
    refs = list(refs)
    scale_ref = refs.pop(0) if plan["scaled"] else None
    pieces = [refs.pop(0) for _ in range(plan["pieces"])]
    negs = [refs.pop(0) for _ in range(plan["negs"])]
    if plan["scaled"]:
        out_ref, bias_ref, total, held = refs
    else:
        out_ref, total = refs
    sources = plan["pieces"]
    base = base_ref[0]
    items, width = total.shape
    total[...] = jnp.zeros_like(total)
    if plan["scaled"]:
        depth = pieces[0].shape[0]
        each = held.shape[0] // sources
        col = lax.broadcasted_iota(jnp.int32, (depth, width), 1)
        for s in range(sources):
            wide = pieces[s][...].astype(F32)
            held[s * each : s * each + depth, :] = jnp.where(col == feats, 1.0, wide)
            held[s * each + depth : (s + 1) * each, :] = negs[s][...]

    def term(s, r):
        row = list_ref[s, 1, r]
        if plan["scaled"]:
            return held[pl.ds(s * each + row, 1), :] * scale_ref[s, row]
        return pieces[s][pl.ds(row, 1), :]

    for s in range(sources):
        first, last = edge_ref[s, 0], edge_ref[s, 1]

        @pl.when(last > first)
        def _(s=s, first=first, last=last):
            item = list_ref[s, 0, first] - base
            value = total[pl.ds(item, 1), :] + term(s, first)

            def add(r, carry):
                item, value = carry
                new = list_ref[s, 0, r] - base
                ahead = total[pl.ds(new, 1), :]
                total[pl.ds(item, 1), :] = value
                return new, jnp.where(new == item, value, ahead) + term(s, r)

            item, value = lax.fori_loop(first + 1, last, add, (item, value))
            total[pl.ds(item, 1), :] = value

    tile = 512 if items % 512 == 0 else 128
    for at in range(0, items, tile):
        turned = total[at : at + tile, :].T
        out_ref[:, at : at + tile] = turned[:feats]
        if plan["scaled"]:
            bias_ref[:, at : at + tile] = turned[feats : feats + 1]


def scatter(base, feats, items, lists, pieces, scale=None, negs=()):
    width = pieces[0].shape[-1]
    sources = len(pieces)
    each = pieces[0].shape[0] + (negs[0].shape[0] if negs else 0)
    below = lambda v: jnp.sum((lists[:, 0] < v).astype(jnp.int32), axis=1)
    edges = jnp.stack([below(base), below(base + items)], axis=1)
    scaled = scale is not None
    plan = {"scaled": scaled, "pieces": sources, "negs": len(negs)}
    smem = pl.BlockSpec(memory_space=pltpu.SMEM)
    vmem = pl.BlockSpec(memory_space=pltpu.VMEM)
    out_shape = [jax.ShapeDtypeStruct((feats, items), F32)]
    scratch = [pltpu.VMEM((items, width), F32)]
    if scaled:
        out_shape.append(jax.ShapeDtypeStruct((1, items), F32))
        scratch.append(pltpu.VMEM((sources * each, width), F32))
    return pl.pallas_call(
        functools.partial(scatter_kernel, feats, plan),
        in_specs=[smem] * (4 if scaled else 3) + [vmem] * (sources + len(negs)),
        out_specs=[vmem] * len(out_shape),
        out_shape=out_shape,
        scratch_shapes=scratch,
        compiler_params=pltpu.CompilerParams(vmem_limit_bytes=56 * MIB),
        cost_estimate=pl.CostEstimate(
            flops=0, bytes_accessed=sources * each * width * 8, transcendentals=0
        ),
    )(base.reshape(1), edges, lists, *([scale] if scaled else []), *pieces, *negs)


def place_kernel(first, axis, where_ref, *refs):
    *pieces, out_ref, sems = refs
    size = out_ref.shape[axis] // len(pieces)
    copies = []
    for k, piece in enumerate(pieces):
        spot = pl.ds(pl.multiple_of(where_ref[k] * size, size), size)
        target = out_ref.at[spot, :] if axis == 0 else out_ref.at[:, spot]
        source = piece.at[pl.ds(first, target.shape[0]), :]
        copies.append(pltpu.make_async_copy(source, target, sems.at[k]))
    for copy in copies:
        copy.start()
    for copy in copies:
        copy.wait()


def place(pieces, where, axis, first=0, rows=None):
    shape = [rows or pieces[0].shape[0], pieces[0].shape[1]]
    shape[axis] *= len(pieces)
    anywhere = pl.BlockSpec(memory_space=pl.ANY)
    return pl.pallas_call(
        functools.partial(place_kernel, first, axis),
        in_specs=[pl.BlockSpec(memory_space=pltpu.SMEM)] + [anywhere] * len(pieces),
        out_specs=pl.BlockSpec(memory_space=pltpu.VMEM),
        scratch_shapes=[pltpu.SemaphoreType.DMA((len(pieces),))],
        out_shape=jax.ShapeDtypeStruct(tuple(shape), pieces[0].dtype),
        compiler_params=pltpu.CompilerParams(vmem_limit_bytes=16 * MIB),
        cost_estimate=pl.CostEstimate(
            flops=0, bytes_accessed=4 * shape[0] * shape[1], transcendentals=0
        ),
    )(where, *pieces)


def row_copies(pieces, where_ref, target, sems, first_sem):
    copies = []
    for k, piece in enumerate(pieces):
        size = piece.shape[0]
        at = pl.multiple_of(where_ref[k] * size, size) if where_ref is not None else k * size
        copies.append(
            pltpu.make_async_copy(piece, target.at[pl.ds(at, size), :], sems.at[first_sem + k])
        )
    return copies


def col_copies(pieces, where_ref, target, sems, first_sem):
    rows = target.shape[0]
    copies = []
    for k, piece in enumerate(pieces):
        size = piece.shape[1]
        spot = pl.ds(pl.multiple_of(where_ref[k] * size, size), size)
        copies.append(
            pltpu.make_async_copy(piece.at[pl.ds(0, rows), :], target.at[:, spot], sems.at[first_sem + k])
        )
    return copies


def start(copies):
    for copy in copies:
        copy.start()


def finish(copies):
    for copy in copies:
        copy.wait()


ANYWHERE = pl.BlockSpec(memory_space=pl.ANY)
IN_SMEM = pl.BlockSpec(memory_space=pltpu.SMEM)
IN_VMEM = pl.BlockSpec(memory_space=pltpu.VMEM)


def forward_kernel(mp, dp, me_ref, where_mp, where_dp, keep_ref, bias_ref, *refs):
    x_pieces, in_pieces, hid_pieces = refs[:mp], refs[mp : mp + dp], refs[mp + dp : mp + 2 * dp]
    z_ref, r_ref, c_ref, q_ref, prev_ref, hs_ref, own_ref, in_own_ref = refs[mp + 2 * dp : mp + 2 * dp + 8]
    x_all, in_all, hid_all, state, low_state, inner, sems = refs[mp + 2 * dp + 8 :]
    t, q = pl.program_id(0), pl.program_id(1)
    slots, width = z_ref.shape[1:]
    full = width * mp
    cols = pl.ds(pl.multiple_of(q * width, width), width)
    x_in = col_copies(x_pieces, where_mp, x_all, sems, 0)
    in_in = row_copies(in_pieces, where_dp, in_all, sems, mp)
    hid_in = row_copies(hid_pieces, where_dp, hid_all, sems, mp + dp)

    @pl.when((t == 0) & (q == 0))
    def _():
        start(x_in)
        start(in_in)
        start(hid_in)
        state[...] = jnp.zeros_like(state)
        finish(x_in)
        finish(in_in)
        for g in range(3):
            rows = pl.ds(pl.multiple_of(g * full + me_ref[0] * width, width), width)
            in_own_ref[g] = in_all[rows, :]

    @pl.when((t == 1) & (q == 0))
    def _():
        finish(hid_in)

    @pl.when(q == 0)
    def _():
        low_state[...] = (state[...] * keep_ref[0]).astype(BF)

    x = x_all[pl.ds(pl.multiple_of(t * slots, slots), slots), :]
    gi = [
        jnp.dot(x, in_all[g * full : (g + 1) * full, cols], preferred_element_type=F32)
        + bias_ref[g : g + 1, :]
        for g in range(3)
    ]
    z_ref[0] = gi[0]
    r_ref[0] = gi[1]
    inner[...] = jnp.broadcast_to(bias_ref[3:4, :], inner.shape)

    @pl.when(t > 0)
    def _():
        low_prev = low_state[...]
        for g, ref in ((0, z_ref.at[0]), (1, r_ref.at[0]), (2, inner)):
            ref[...] += jnp.dot(
                low_prev, hid_all[g * full : (g + 1) * full, cols], preferred_element_type=F32
            )

    prev = state[:, cols] * keep_ref[0]
    z = 1.0 / (1.0 + jnp.exp(-z_ref[0]))
    r = 1.0 / (1.0 + jnp.exp(-r_ref[0]))
    c = jnp.tanh(gi[2] + r * inner[...])
    h = (1.0 - z) * prev + z * c
    z_ref[0] = z
    r_ref[0] = r
    c_ref[0] = c
    q_ref[0] = inner[...]
    prev_ref[0] = prev
    shown = h.astype(BF)
    hs_ref[0] = shown
    state[:, cols] = h

    @pl.when(q == me_ref[0])
    def _():
        own_ref[0] = shown


def forward(steps, slots, width, me, where_mp, where_dp, keep, bias_all, x_pieces, in_pieces, hid_pieces):
    mp, dp = len(x_pieces), len(in_pieces)
    full = mp * width
    tile = pl.BlockSpec((1, slots, width), lambda t, q: (t, 0, q))
    later = pl.BlockSpec(
        (1, slots, width), lambda t, q: (jnp.maximum(t - 1, 0), 0, jnp.where(t == 0, 0, q))
    )
    shape = lambda count, dtype: jax.ShapeDtypeStruct((count, slots, full), dtype)
    return pl.pallas_call(
        functools.partial(forward_kernel, mp, dp),
        grid=(steps, mp),
        in_specs=[IN_SMEM] * 3
        + [
            pl.BlockSpec((1, slots, 1), lambda t, q: (t, 0, 0)),
            pl.BlockSpec((8, width), lambda t, q: (0, q)),
        ]
        + [ANYWHERE] * (mp + 2 * dp),
        out_specs=[
            tile,
            tile,
            tile,
            later,
            later,
            tile,
            pl.BlockSpec((1, slots, width), lambda t, q: (t, 0, 0)),
            pl.BlockSpec((3, width, full), lambda t, q: (0, 0, 0)),
        ],
        out_shape=[shape(steps, F32)] * 3
        + [shape(steps - 1, F32)] * 2
        + [
            shape(steps, BF),
            jax.ShapeDtypeStruct((steps, slots, width), BF),
            jax.ShapeDtypeStruct((3, width, full), BF),
        ],
        scratch_shapes=[
            pltpu.VMEM((steps * slots, full), BF),
            pltpu.VMEM((3 * full, full), BF),
            pltpu.VMEM((3 * full, full), BF),
            pltpu.VMEM((slots, full), F32),
            pltpu.VMEM((slots, full), BF),
            pltpu.VMEM((slots, width), F32),
            pltpu.SemaphoreType.DMA((mp + 2 * dp,)),
        ],
        compiler_params=pltpu.CompilerParams(vmem_limit_bytes=48 * MIB),
        cost_estimate=pl.CostEstimate(
            flops=2 * 6 * steps * slots * full * full,
            bytes_accessed=steps * full * (slots * 24 + full * 12),
            transcendentals=3 * steps * slots * full,
        ),
    )(me, where_mp, where_dp, keep, bias_all, *x_pieces, *in_pieces, *hid_pieces)


def score_kernel(rows, mp, dp, where_mp, hs_ref, one_ref, weight_ref, *refs):
    tgt_pieces, neg_pieces = refs[:mp], refs[mp : mp + dp]
    ds_ref, dhs_ref, du_ref, loss_ref, s_ref, tgt_all, neg_all, sems = refs[mp + dp :]
    i = pl.program_id(0)
    tile = hs_ref.shape[0]
    tgt_in = col_copies(tgt_pieces, where_mp, tgt_all, sems, 0)
    neg_in = row_copies(neg_pieces, None, neg_all, sems, mp)

    @pl.when(i == 0)
    def _():
        start(neg_in)
        start(tgt_in)
        loss_ref[...] = jnp.zeros_like(loss_ref)
        finish(neg_in)

    s_ref[...] = lax.dot_general(
        hs_ref[...] + one_ref[...], neg_all[...], (((1,), (1,)), ((), ())), preferred_element_type=F32
    )

    @pl.when(i == 0)
    def _():
        finish(tgt_in)

    def chunk(j, _):
        at = pl.ds(pl.multiple_of(j * rows, rows), rows)
        s = s_ref[at, :]
        w = weight_ref[at, :]
        tgt = tgt_all[pl.ds(pl.multiple_of(i * tile + j * rows, rows), rows), :].astype(F32)
        u = jnp.sum((hs_ref[at, :] + one_ref[...]).astype(F32) * tgt, axis=1, keepdims=True)
        top = jnp.max(s, axis=1, keepdims=True)
        e = jnp.exp(s - top)
        above = 1.0 / (1.0 + jnp.exp(s - u))
        ea = e * above
        inv = 1.0 / jnp.sum(e, axis=1, keepdims=True)
        mixture = jnp.sum(ea, axis=1, keepdims=True) * inv
        spread = jnp.sum(e * s * s, axis=1, keepdims=True) * inv
        slope = jnp.sum(ea * (1.0 - above), axis=1, keepdims=True) * inv
        shift = s + 1.0
        ds = (w * inv * e) * (bpr_weight * (shift * shift - spread) - above * above * (1.0 / mixture))
        ds_ref[at, :] = ds.astype(BF)
        du_ref[at, :] = (-w * slope / mixture).astype(BF).astype(F32)
        loss_ref[...] += jnp.broadcast_to(
            jnp.sum(w * (-jnp.log(mixture) + bpr_weight * spread), keepdims=True), loss_ref.shape
        )
        return 0

    lax.fori_loop(0, tile // rows, chunk, 0)
    own = pl.ds(pl.multiple_of(i * tile, tile), tile)
    dhs_ref[...] = jnp.dot(ds_ref[...], neg_all[...], preferred_element_type=F32) + du_ref[
        ...
    ] * tgt_all[own, :].astype(F32)


def scores(tile, where_mp, shown, one_row, weight, tgt_pieces, neg_pieces):
    events, full = shown.shape
    mp, dp = len(tgt_pieces), len(neg_pieces)
    count = dp * neg_pieces[0].shape[0]
    row_tile = lambda w: pl.BlockSpec((tile, w), lambda i: (i, 0))
    return pl.pallas_call(
        functools.partial(score_kernel, 32, mp, dp),
        grid=(events // tile,),
        in_specs=[IN_SMEM, row_tile(full), pl.BlockSpec((1, full), lambda i: (0, 0)), row_tile(1)]
        + [ANYWHERE] * (mp + dp),
        out_specs=[row_tile(count), row_tile(full), row_tile(1), pl.BlockSpec((8, 128), lambda i: (0, 0))],
        out_shape=[
            jax.ShapeDtypeStruct((events, count), BF),
            jax.ShapeDtypeStruct((events, full), F32),
            jax.ShapeDtypeStruct((events, 1), F32),
            jax.ShapeDtypeStruct((8, 128), F32),
        ],
        scratch_shapes=[
            pltpu.VMEM((tile, count), F32),
            pltpu.VMEM((events, full), BF),
            pltpu.VMEM((count, full), BF),
            pltpu.SemaphoreType.DMA((mp + dp,)),
        ],
        compiler_params=pltpu.CompilerParams(vmem_limit_bytes=48 * MIB),
        cost_estimate=pl.CostEstimate(
            flops=4 * events * full * count,
            bytes_accessed=events * (full * 8 + count * 2) + count * full * 2,
            transcendentals=3 * events * count,
        ),
    )(where_mp, shown, one_row, weight, *tgt_pieces, *neg_pieces)


def backward_kernel(
    dp, me_ref, where_dp, z_ref, r_ref, c_ref, q_ref, prev_ref, keep_ref, dhs_ref, bias_ref, in_ref, *refs
):
    hid_pieces = refs[:dp]
    dx_ref, own_ref, sum_ref, later, back, hid_all, sems = refs[dp:]
    i, q = pl.program_id(0), pl.program_id(1)
    last_step, last_part = pl.num_programs(0) - 1, pl.num_programs(1) - 1
    width = z_ref.shape[2]
    full = hid_all.shape[1]
    cols = pl.ds(pl.multiple_of(q * width, width), width)
    hid_in = row_copies(hid_pieces, where_dp, hid_all, sems, 0)

    @pl.when((i == 0) & (q == 0))
    def _():
        start(hid_in)
        later[...] = jnp.zeros_like(later)
        sum_ref[...] = jnp.zeros_like(sum_ref)
        finish(hid_in)

    @pl.when(q == 0)
    def _():
        dx_ref[...] = jnp.zeros_like(dx_ref)
        back[...] = jnp.zeros_like(back)

    z, r, c = z_ref[0], r_ref[0], c_ref[0]
    begun = i < last_step
    inner = jnp.where(begun, q_ref[0], jnp.broadcast_to(bias_ref[3:4, :], z.shape))
    prev = jnp.where(begun, prev_ref[0], 0.0)
    dh = later[:, cols] + dhs_ref[...]
    rest = 1.0 - z
    dz = dh * (c - prev) * z * rest
    da = dh * z * (1.0 - c * c)
    dr = da * inner * r * (1.0 - r)
    dq = da * r
    grads = (dz, dr, da, dq)
    zl, rl, al, ql = [v.astype(BF) for v in grads]
    over = (((1,), (1,)), ((), ()))
    dx = lax.dot_general(zl, in_ref[0], over, preferred_element_type=F32)
    dx += lax.dot_general(rl, in_ref[1], over, preferred_element_type=F32)
    dx += lax.dot_general(al, in_ref[2], over, preferred_element_type=F32)
    dx_ref[...] += dx

    @pl.when(begun)
    def _():
        hid = lambda g: hid_all[g * full : (g + 1) * full, cols]
        total = lax.dot_general(zl, hid(0), over, preferred_element_type=F32)
        total += lax.dot_general(rl, hid(1), over, preferred_element_type=F32)
        total += lax.dot_general(ql, hid(2), over, preferred_element_type=F32)
        back[...] += total
        back[:, cols] += dh * rest

    @pl.when(q == me_ref[0])
    def _():
        for k, value in enumerate((zl, rl, al, ql)):
            own_ref[:, k * width : (k + 1) * width] = value
            sum_ref[k : k + 1, :] += jnp.sum(grads[k], axis=0, keepdims=True)

    @pl.when(q == last_part)
    def _():
        later[...] = back[...] * keep_ref[0]


def backward(width, me, where_dp, z, r, c, inner, prev, keep, dhs, bias_all, in_own, hid_pieces):
    steps, slots, full = z.shape
    dp = len(hid_pieces)
    parts = full // width
    tile = pl.BlockSpec((1, slots, width), lambda i, q: (steps - 1 - i, 0, q))
    later = pl.BlockSpec(
        (1, slots, width),
        lambda i, q: (jnp.maximum(steps - 2 - i, 0), 0, jnp.where(i == steps - 1, parts - 1, q)),
    )
    row = lambda w: pl.BlockSpec((slots, w), lambda i, q: (steps - 1 - i, 0))
    return pl.pallas_call(
        functools.partial(backward_kernel, dp),
        grid=(steps, parts),
        in_specs=[IN_SMEM] * 2
        + [tile] * 3
        + [later] * 2
        + [
            pl.BlockSpec((1, slots, 1), lambda i, q: (steps - 1 - i, 0, 0)),
            pl.BlockSpec((slots, width), lambda i, q: (steps - 1 - i, q)),
            pl.BlockSpec((8, width), lambda i, q: (0, q)),
            pl.BlockSpec((3, width, width), lambda i, q: (0, 0, q)),
        ]
        + [ANYWHERE] * dp,
        out_specs=[row(width), row(4 * width), pl.BlockSpec((8, width), lambda i, q: (0, 0))],
        out_shape=[
            jax.ShapeDtypeStruct((steps * slots, width), F32),
            jax.ShapeDtypeStruct((steps * slots, 4 * width), BF),
            jax.ShapeDtypeStruct((8, width), F32),
        ],
        scratch_shapes=[
            pltpu.VMEM((slots, full), F32),
            pltpu.VMEM((slots, full), F32),
            pltpu.VMEM((3 * full, full), BF),
            pltpu.SemaphoreType.DMA((dp,)),
        ],
        compiler_params=pltpu.CompilerParams(vmem_limit_bytes=48 * MIB),
        cost_estimate=pl.CostEstimate(
            flops=2 * steps * slots * full * (3 * full + 3 * width),
            bytes_accessed=steps * full * (slots * 24 + full * 6),
            transcendentals=0,
        ),
    )(me, where_dp, z, r, c, inner, prev, keep, dhs, bias_all, in_own, *hid_pieces)


def weights_kernel(units, mp, order_ref, where_mp, hs_ref, keep_ref, own_ref, sum_ref, loss_ref, *refs):
    x_pieces = refs[:mp]
    kept_ref, sent_ref, total, x_all, sems = refs[mp:]
    x_in = col_copies(x_pieces, where_mp, x_all, sems, 0)
    start(x_in)
    width = sum_ref.shape[1]
    events = x_all.shape[0]
    slots = hs_ref.shape[1]
    over = (((0,), (0,)), ((), ()))
    three = 3 * width
    part = jnp.zeros((total.shape[0], three), F32)
    for t in range(events // slots - 1):
        hb = (hs_ref[t].astype(F32) * keep_ref[t + 1]).astype(BF)
        rows = slice((t + 1) * slots, (t + 2) * slots)
        state = jnp.concatenate([own_ref[rows, : 2 * width], own_ref[rows, three:]], axis=1)
        part += lax.dot_general(hb, state, over, preferred_element_type=F32)
    total[:, three:] = part
    finish(x_in)
    total[:, :three] = lax.dot_general(x_all[...], own_ref[:, :three], over, preferred_element_type=F32)
    for k in range(3):
        total[units : units + 1, k * width : (k + 1) * width] = sum_ref[k : k + 1, :]
    total[units + 1 : units + 2, :width] = sum_ref[3:4, :]
    total[units + 1 : units + 2, width : width + 128] = loss_ref[0:1, :]
    rows = kept_ref.shape[1]
    for k in range(kept_ref.shape[0]):
        for ref, at in ((kept_ref, 2 * k), (sent_ref, 2 * k + 1)):
            ref[k] = total[pl.ds(pl.multiple_of(order_ref[at] * rows, rows), rows), :]


def weight_grads(units, order, where_mp, hs, keep, own, sums, loss, x_pieces):
    mp = len(x_pieces)
    events, width = own.shape[0], sums.shape[1]
    full = hs.shape[2]
    count = order.shape[0]
    half = jax.ShapeDtypeStruct((count // 2, full // count, 6 * width), F32)
    return pl.pallas_call(
        functools.partial(weights_kernel, units, mp),
        in_specs=[IN_SMEM] * 2 + [IN_VMEM] * 5 + [ANYWHERE] * mp,
        out_specs=[IN_VMEM, IN_VMEM],
        out_shape=[half, half],
        scratch_shapes=[
            pltpu.VMEM((full, 6 * width), F32),
            pltpu.VMEM((events, full), BF),
            pltpu.SemaphoreType.DMA((mp,)),
        ],
        compiler_params=pltpu.CompilerParams(vmem_limit_bytes=56 * MIB),
        cost_estimate=pl.CostEstimate(
            flops=2 * events * full * 6 * width,
            bytes_accessed=events * full * 4 + full * 24 * width,
            transcendentals=0,
        ),
    )(order, where_mp, hs, keep, own, sums, loss, *x_pieces)


def output_kernel(units, where_dp, *refs):
    dp = len(refs) - 7
    pieces = refs[:dp]
    in_ref, hid_ref, gate_ref, cand_ref, loss_ref, total, sems = refs[dp:]
    copies = row_copies(pieces, where_dp, total, sems, 0)
    start(copies)
    finish(copies)
    width = total.shape[1] // 6
    for k, ref in enumerate((in_ref, hid_ref)):
        for g in range(3):
            at = (3 * k + g) * width
            for q in range(total.shape[0] // width):
                ref[g, q * units : (q + 1) * units, :] = total[q * width : q * width + units, at : at + units]
    for g in range(3):
        gate_ref[g : g + 1, :] = total[units : units + 1, g * width : g * width + units]
    cand_ref[...] = total[units + 1 : units + 2, :units]
    loss_ref[...] = total[units + 1 : units + 2, width : width + 128]


def outputs(units, mp, where_dp, pieces):
    rows, cols = pieces[0].shape
    dp = len(pieces)
    grad = jax.ShapeDtypeStruct((3, mp * units, units), F32)
    return pl.pallas_call(
        functools.partial(output_kernel, units),
        in_specs=[IN_SMEM] + [ANYWHERE] * dp,
        out_specs=[IN_VMEM] * 5,
        out_shape=[
            grad,
            grad,
            jax.ShapeDtypeStruct((3, units), F32),
            jax.ShapeDtypeStruct((1, units), F32),
            jax.ShapeDtypeStruct((1, 128), F32),
        ],
        scratch_shapes=[pltpu.VMEM((rows * dp, cols), F32), pltpu.SemaphoreType.DMA((dp,))],
        compiler_params=pltpu.CompilerParams(vmem_limit_bytes=48 * MIB),
        cost_estimate=pl.CostEstimate(
            flops=0, bytes_accessed=8 * rows * dp * cols, transcendentals=0
        ),
    )(where_dp, *pieces)


def swap(value, k, axis):
    count = lax.axis_size(axis)
    return lax.ppermute(value, axis, [(i, i ^ k) for i in range(count)])


def gather_mp(value):
    count = lax.axis_size("mp")
    if count != 4:
        return [value] + [swap(value, k, "mp") for k in range(1, count)]
    near = swap(value, 1, "mp")
    middle = lax.ppermute(value, "mp", [(1, 2), (2, 1)])
    over = swap(value, 2, "mp")
    far = lax.ppermute(over, "mp", [(1, 0), (2, 3)])
    place_now = lax.axis_index("mp")
    inside = (place_now == 1) | (place_now == 2)
    return [value, near, over, jnp.where(inside, middle, far)]


def gather_dp(value):
    count = lax.axis_size("dp")
    chips = [value] + [swap(value, k, "dp") for k in range(2, count, 2)]
    other = [swap(piece, 1, "dp") for piece in chips]
    return [piece for pair in zip(chips, other) for piece in pair]


def reduce_dp(kept, sent):
    mine = kept + swap(sent, 1, "dp")
    total = mine[0]
    for k in range(1, mine.shape[0]):
        total = total + swap(mine[k], 2 * k, "dp")
    return total


def low(value):
    return lax.reduce_precision(value, 8, 7).astype(BF)


def on_device(
    item_ids,
    session_ends,
    negatives,
    embedding,
    in_weight,
    hid_weight,
    gate_bias,
    cand_bias,
    out_table,
    out_bias,
):
    dp, mp = lax.axis_size("dp"), lax.axis_size("mp")
    me_dp, me_mp = lax.axis_index("dp"), lax.axis_index("mp")
    order_dp = me_dp ^ jnp.arange(dp, dtype=jnp.int32)
    order_mp = me_mp ^ jnp.arange(mp, dtype=jnp.int32)
    me = me_mp.astype(jnp.int32).reshape(1)
    steps, slots = session_ends.shape
    events = steps * slots
    feats, vocab = embedding.shape
    units = hid_weight.shape[2]
    width = up(units, 128)
    full = mp * width
    neg_count = negatives.shape[0]
    neg_share = neg_count // dp

    end_float = session_ends.astype(F32)
    keep = jnp.concatenate([jnp.zeros((1, slots), F32), 1.0 - end_float[:-1]], axis=0)
    weight = ((1.0 - end_float) / (steps * slots * dp)).reshape(events, 1)
    sources = item_ids[:-1].reshape(events)
    targets = item_ids[1:].reshape(events)
    own_negs = lax.dynamic_slice_in_dim(negatives, me_dp * neg_share, neg_share)

    def padded_rows(value):
        value = value.reshape(3, mp, units, units)
        value = jnp.pad(value, ((0, 0), (0, 0), (0, width - units), (0, width - units)))
        return value.reshape(3 * full, width)

    share = 3 * full // dp
    in_share = lax.dynamic_slice_in_dim(padded_rows(in_weight), me_dp * share, share)
    hid_share = lax.dynamic_slice_in_dim(padded_rows(hid_weight), me_dp * share, share)
    biases = jnp.pad(
        jnp.concatenate([gate_bias, cand_bias[None]]), ((0, 0), (0, width - units))
    )
    first = low(biases)
    second = low(biases - first.astype(F32))
    third = low(biases - first.astype(F32) - second.astype(F32))
    bias_rows = jnp.concatenate([first, second, third, jnp.zeros((4, width), BF)])
    cols = gather_mp(jnp.concatenate([in_share, hid_share, bias_rows]))
    bias_all = place(cols, order_mp, 1, 2 * share, 16)[:12].astype(F32)
    bias_all = jnp.pad(bias_all[0:4] + bias_all[4:8] + bias_all[8:12], ((0, 4), (0, 0)))
    in_pieces = gather_dp(place(cols, order_mp, 1, 0, share))
    hid_pieces = gather_dp(place(cols, order_mp, 1, share, share))

    x_rows, x_sid, x_order = lookup(sources, embedding)
    x_pieces = gather_mp(x_rows[:events])
    t_rows, t_sid, t_order = lookup(jnp.concatenate([targets, own_negs]), out_table, out_bias)
    t_pieces = gather_mp(t_rows[: events + neg_share])
    neg_pieces = gather_dp(place(t_pieces, order_mp, 1, events, neg_share))
    gap = ((0, 0), (0, t_sid.shape[1] - x_sid.shape[1]))
    lists = jnp.concatenate([jnp.pad(x_sid, gap), jnp.pad(x_order, gap), t_sid, t_order])
    lists = jnp.stack(gather_dp(lists.astype(jnp.int32)))
    x_lists = lists[:, 0:2, : x_sid.shape[1]]
    t_lists = lists[:, 2:4]

    keep = keep[:, :, None]
    z, r, c, inner, prev, hs, own_shown, in_own = forward(
        steps, slots, width, me, order_mp, order_dp, keep, bias_all, x_pieces, in_pieces, hid_pieces
    )
    shown = hs.reshape(events, full)
    own_shown = own_shown.reshape(events, width)
    rows_all = gather_dp(own_shown)
    col = jnp.arange(full)[None, :]
    one_row = ((col >= units) & (col < units + 3)).astype(BF)
    neg_low, dhs, tgt_low, loss = scores(slots, order_mp, shown, one_row, weight, t_pieces, neg_pieces)

    counted = jnp.where(jnp.arange(width)[None, :] == units, BF(1.0), own_shown)
    neg_table = jnp.einsum("nj,nh->jh", neg_low, counted, preferred_element_type=F32)
    neg_table = neg_table.reshape(dp // 2, 2, neg_share, width)
    neg_sum = reduce_dp(neg_table[:, 0], neg_table[:, 1])
    scale_rows = up(-(-events // width), 8)
    scale = jnp.pad(tgt_low.reshape(events), (0, scale_rows * width - events))
    neg_all = gather_dp(jnp.concatenate([neg_sum, scale.reshape(scale_rows, width)]))
    scale_all = jnp.stack([v[neg_share:].reshape(-1)[:events] for v in neg_all])
    scale_all = jnp.concatenate([scale_all, jnp.ones((dp, neg_share), F32)], axis=1)

    dx, own, sums = backward(
        width, me, order_dp, z, r, c, inner, prev, keep, dhs, bias_all, in_own, hid_pieces
    )
    dx_all = gather_dp(dx)
    kept, sent = weight_grads(units, order_dp, order_mp, hs, keep, own, sums, loss, x_pieces)
    in_sum, hid_sum, gate_sum, cand_sum, loss_sum = outputs(
        units, mp, order_dp, gather_dp(reduce_dp(kept, sent))
    )

    items = vocab // dp
    base = (me_dp * items).astype(jnp.int32)
    table_sum, bias_sum = scatter(
        base, units, items, t_lists, rows_all, scale_all, [v[:neg_share] for v in neg_all]
    )
    (embed_sum,) = scatter(base, units, items, x_lists, dx_all)
    return (
        loss_sum[0, 0],
        in_sum,
        hid_sum,
        gate_sum,
        cand_sum.reshape(units),
        embed_sum,
        table_sum,
        bias_sum.reshape(items),
    )


def solution(mesh):
    return jax.shard_map(
        on_device,
        mesh=mesh,
        in_specs=(
            P(None, "dp"),
            P(None, "dp"),
            P(),
            P("mp", None),
            P(None, None, "mp"),
            P(None, None, "mp"),
            P(None, "mp"),
            P("mp"),
            P("mp", None),
            P(),
        ),
        out_specs=(
            P(),
            P(None, None, "mp"),
            P(None, None, "mp"),
            P(None, "mp"),
            P("mp"),
            P("mp", "dp"),
            P("mp", "dp"),
            P("dp"),
        ),
        check_vma=False,
    )
```

time: 702 us -> 623 us (0.89)
  the two profiles are of different devices: /device:TPU:27 before, /device:TPU:7 now
where the time goes in v3:
time: 623 us; the launch traced here: 616 us
  Pallas kernels  222 us (36%)
  waiting for transfers between devices  181 us (29%)
  starting transfers between devices  146 us (23%)
  local copies, waits for them, and re-layouts  47.9 us (8%)
  other arithmetic  12.8 us (2%)
    ppermute x70, waiting for transfers between devices, swap(): return lax.ppermute(value, axis, [(i, i ^ k) for i in range(count)])  156 us
    ppermute x70, starting transfers between devices, swap(): return lax.ppermute(value, axis, [(i, i ^ k) for i in range(count)])  139 us
    pallas_call x2, Pallas kernels, scatter(): pl.pallas_call(functools.partial(scatter_kernel, feats, plan), in_specs=[...  84.5 us
    pallas_call x2, Pallas kernels, lookup(): pl.pallas_call(functools.partial(lookup_kernel, bias is not None, feats),...  36.1 us
    pallas_call x1, Pallas kernels, scores(): pl.pallas_call(functools.partial(score_kernel, 32, mp, dp), grid=(events...  29.8 us
    pallas_call x1, Pallas kernels, forward(): pl.pallas_call(functools.partial(forward_kernel, mp, dp), grid=(steps, mp...  27.2 us
    ppermute x3, waiting for transfers between devices, gather_mp(): far = lax.ppermute(over, 'mp', [(1, 0), (2, 3)])  25.3 us
    pallas_call x1, Pallas kernels, backward(): pl.pallas_call(functools.partial(backward_kernel, dp), grid=(steps, parts...  23 us
  transfers between devices with their start and end apart: 76, of which 24 were waited for; matrix products, arithmetic and copies ran while one was open for 9% of the time, Pallas kernels for 35%

profile of v3, /device:TPU:7, one launch (start us, length us, event | category | flops | bytes accessed | tf_op | source)
XLA Modules:
  0.0 615.6 jit_solution(10351276575302404430)
XLA Ops:
  15.7 16.0 %shard_map.162 = (bf16[1280,256]{1,0:T(8,128)(2,1)}, f32[1,1280]{1,0:T(1,128)}, f32[1,1280]{1,0:T(1,128)}) custom-call(s32[10]{0:T(128)} %convert_reduce_fusion.1.cnt_ref, s32[1,1280]{1,0:T(1,128)} %broadcast_in_dim.36.idr_ref, s32[1280,1]{1,0:T(8,128)} %reshape.231.idc_ref, bf16[250,36864]{1,0:T(8,128)(2,1)} %tab_ref.2), custom_call_target="tpu_custom_call" | custom-call | flops 9437184000 | bytes 18432000 | tf_op jit(solution)/shard_map/pallas_call | solution.py:105
  38.7 20.1 %shard_map.166 = (bf16[1536,256]{1,0:T(8,128)(2,1)}, f32[1,1536]{1,0:T(1,128)}, f32[1,1536]{1,0:T(1,128)}) custom-call(s32[10]{0:T(128)} %convert_reduce_fusion.cnt_ref, s32[1,1536]{1,0:T(1,128)} %broadcast_in_dim.37.idr_ref, s32[1536,1]{1,0:T(8,128)} %reshape.233.idc_ref, bf16[250,36864]{1,0:T(8,128)(2,1)} %tab_ref.3, f32[288,128]{1,0:T(8,128)} %bitcast.136), custom_call_target="tpu_custom_call" | custom-call | flops 9437184000 | bytes 18432000 | tf_op jit(solution)/shard_map/pallas_call | solution.py:105
  69.4 21.7 %collective-permute-start.22 = (bf16[1408,256]{1,0:T(8,128)(2,1)S(1)}, bf16[1408,256]{1,0:T(8,128)(2,1)}, u32[]{:S(2)}, u32[]{:S(2)}) collective-permute-start(bf16[1408,256]{1,0:T(8,128)(2,1)S(1)} %slice.148.refs_0_), channel_id=1, source_target_pairs={{0,1},{1,0},{2,3},{3,2},{4,5},{5,4},{6,7},{7,6},{8,9},{9,8},{10,11... | collective-permute-start | bytes 2162696 | tf_op jit(solution)/shard_map/ppermute | solution.py:689
  93.5 12.8 %collective-permute-done.23.refs_2_ = bf16[1408,256]{1,0:T(8,128)(2,1)} collective-permute-done((bf16[1408,256]{1,0:T(8,128)(2,1)S(1)}, bf16[1408,256]{1,0:T(8,128)(2,1)}, u32[]{:S(2)}, u32[]{:S(2)}) %collective-permute-start.23) | collective-permute-done | bytes 720928 | tf_op jit(solution)/shard_map/ppermute | solution.py:689
  107.8 13.9 %collective-permute-done.22.refs_1_ = bf16[1408,256]{1,0:T(8,128)(2,1)} collective-permute-done((bf16[1408,256]{1,0:T(8,128)(2,1)S(1)}, bf16[1408,256]{1,0:T(8,128)(2,1)}, u32[]{:S(2)}, u32[]{:S(2)}) %collective-permute-start.22) | collective-permute-done | bytes 720928 | tf_op jit(solution)/shard_map/ppermute | solution.py:689
  121.9 12.4 %collective-permute-done.7 = bf16[1152,256]{1,0:T(8,128)(2,1)} collective-permute-done((bf16[1152,256]{1,0:T(8,128)(2,1)}, bf16[1152,256]{1,0:T(8,128)(2,1)}, u32[]{:S(2)}, u32[]{:S(2)}) %collective-permute-start.7) | collective-permute-done | bytes 589856 | tf_op jit(solution)/shard_map/ppermute | solution.py:699
  136.9 12.8 %collective-permute-done.25 = bf16[1408,256]{1,0:T(8,128)(2,1)S(1)} collective-permute-done((bf16[1408,256]{1,0:T(8,128)(2,1)}, bf16[1408,256]{1,0:T(8,128)(2,1)S(1)}, u32[]{:S(2)}, u32[]{:S(2)}) %collective-permute-start.25) | collective-permute-done | bytes 720928 | tf_op jit(solution)/shard_map/ppermute | solution.py:699
  159.3 9.4 %collective-permute-done.9.refs_6_ = bf16[384,1024]{1,0:T(8,128)(2,1)} collective-permute-done((bf16[384,1024]{1,0:T(8,128)(2,1)}, bf16[384,1024]{1,0:T(8,128)(2,1)}, u32[]{:S(2)}, u32[]{:S(2)}) %collective-permute-start.9) | collective-permute-done | bytes 786464 | tf_op jit(solution)/shard_map/ppermute | solution.py:689
  169.2 16.4 %collective-permute-done.13.refs_10_ = bf16[384,1024]{1,0:T(8,128)(2,1)} collective-permute-done((bf16[384,1024]{1,0:T(8,128)(2,1)}, bf16[384,1024]{1,0:T(8,128)(2,1)}, u32[]{:S(2)}, u32[]{:S(2)}) %collective-permute-start.13) | collective-permute-done | bytes 786464 | tf_op jit(solution)/shard_map/ppermute | solution.py:689
  198.9 10.5 %collective-permute-start.10 = (bf16[384,1024]{1,0:T(8,128)(2,1)}, bf16[384,1024]{1,0:T(8,128)(2,1)S(1)}, u32[]{:S(2)}, u32[]{:S(2)}) collective-permute-start(bf16[384,1024]{1,0:T(8,128)(2,1)} %collective-permute-done.9.refs_6_), channel_id=1, source_target_pairs={{0,4},{4,0},{8,12},{12,8},{16,20},{20,16},{24,28},{28,24},{1,5},{5... | collective-permute-start | bytes 2359304 | tf_op jit(solution)/shard_map/ppermute | solution.py:689
  214.4 27.2 %shard_map.165 = (f32[3,384,1024]{2,1,0:T(8,128)}, f32[3,384,1024]{2,1,0:T(8,128)}, f32[3,384,1024]{2,1,0:T(8,128)}, f32[2,384,1024]{2,1,0:T(8,128)}, f32[2,384,...) custom-call(s32[1]{0:T(128)} %bitcast.me_ref, ...), custom_call_target="tpu_custom_call" | custom-call | flops 14495514624 | bytes 66060288 | tf_op jit(solution)/shard_map/pallas_call | solution.py:356
  244.1 29.8 %shard_map.168 = (bf16[1152,2048]{1,0:T(8,128)(2,1)}, f32[1152,1024]{1,0:T(8,128)}, f32[1152,1]{1,0:T(8,128)S(1)}, f32[8,128]{1,0:T(8,128)S(1)}) custom-call(s32[4]{0:T(128)S(1)} %iota_xor_fusion.where_ref.where_mp, bf16[1152,1024]{1,0:T(8,128)(2,1)} %bitcast.139, bf16[1,1024]{1,0:T(2,128)(2,1)S(1)} %and_convert_fusion.one_ref, f32[1152,1]{1,0:T(8,128)S(1)} %bitcast.115, ...), custom_call_target="tpu_custom_call" | custom-call | flops 9663676416 | bytes 18350080 | tf_op jit(solution)/shard_map/pallas_call | solution.py:458
  273.9 6.8 %copy.75 = bf16[2048,1152]{1,0:T(8,128)(2,1)} copy(bf16[2048,1152]{0,1:T(8,128)(2,1)} %bitcast.116) | data formatting | bytes 9437184 | tf_op jit(solution)/shard_map/nj,nh->jh/dot_general | solution.py:801
  286.6 23.0 %shard_map.169 = (f32[1152,256]{1,0:T(8,128)}, bf16[1152,1024]{1,0:T(8,128)(2,1)}, f32[8,256]{1,0:T(8,128)S(1)}) custom-call(s32[1]{0:T(128)} %bitcast.me_ref, s32[8]{0:T(128)S(1)} %iota_xor_fusion.1.where_dp.order_ref, f32[3,384,1024]{2,1,0:T(8,128)} %get-tuple-element.40.z_ref, f32[3,384,1024]{2,1,0:T(8,128)} %get-tuple-element.41.r_ref, ...), custom_call_target="tpu_custom_call" | custom-call | flops 9059696640 | bytes 47185920 | tf_op jit(solution)/shard_map/pallas_call | solution.py:557
  310.3 11.1 %shard_map.170 = (f32[4,128,1536]{2,1,0:T(8,128)}, f32[4,128,1536]{2,1,0:T(8,128)}) custom-call(s32[8]{0:T(128)} %copy-done.18, s32[4]{0:T(128)} %copy-done.17, bf16[3,384,1024]{2,1,0:T(8,128)(2,1)} %get-tuple-element.39.hs_ref, f32[3,384,1]{2,1,0:T(8,128)} %copy.63.keep_ref, bf16[1152,1024]{1,0:T(8,128)(2,1)} %get-tuple-element.48.own_ref, ...), custom_call_target="tpu_custom_call" | custom-call | flops 3623878656 | bytes 11010048 | tf_op jit(solution)/shard_map/pallas_call | solution.py:626
  329.8 9.0 %collective-permute-done.70.refs_3_ = bf16[1152,256]{1,0:T(8,128)(2,1)S(1)} collective-permute-done((bf16[1152,256]{1,0:T(8,128)(2,1)S(1)}, bf16[1152,256]{1,0:T(8,128)(2,1)S(1)}, u32[]{:S(2)}, u32[]{:S(2)}) %collective-permute-start.70) | collective-permute-done | bytes 589856 | tf_op jit(solution)/shard_map/ppermute | solution.py:689
  342.7 12.5 %collective-permute-done.72.refs_5_ = bf16[1152,256]{1,0:T(8,128)(2,1)S(1)} collective-permute-done((bf16[1152,256]{1,0:T(8,128)(2,1)S(1)}, bf16[1152,256]{1,0:T(8,128)(2,1)S(1)}, u32[]{:S(2)}, u32[]{:S(2)}) %collective-permute-start.72) | collective-permute-done | bytes 589856 | tf_op jit(solution)/shard_map/ppermute | solution.py:689
  379.4 16.1 %collective-permute-done.52.refs_2_ = f32[1152,256]{1,0:T(8,128)} collective-permute-done((f32[1152,256]{1,0:T(8,128)}, f32[1152,256]{1,0:T(8,128)}, u32[]{:S(2)}, u32[]{:S(2)}) %collective-permute-start.52) | collective-permute-done | bytes 1179680 | tf_op jit(solution)/shard_map/ppermute | solution.py:689
  396.8 25.1 %collective-permute-start.34 = (f32[128,1536]{1,0:T(8,128)S(1)}, f32[128,1536]{1,0:T(8,128)S(1)}, u32[]{:S(2)}, u32[]{:S(2)}) collective-permute-start(f32[128,1536]{1,0:T(8,128)S(1)} %get-tuple-element.72), channel_id=1, source_target_pairs={{0,8},{4,12},{8,0},{12,4},{16,24},{20,28},{24,16},{28,20},{1,9},{5... | collective-permute-start | bytes 2359304 | tf_op jit(solution)/shard_map/ppermute | solution.py:689
  429.0 37.9 %collective-permute-done.67 = f32[264,256]{1,0:T(8,128)S(1)} collective-permute-done((f32[264,256]{1,0:T(8,128)S(1)}, f32[264,256]{1,0:T(8,128)S(1)}, u32[]{:S(2)}, u32[]{:S(2)}) %collective-permute-start.67) | collective-permute-done | bytes 270368 | tf_op jit(solution)/shard_map/ppermute | solution.py:689
  479.8 10.0 %collective-permute-done.38.refs_2_ = f32[128,1536]{1,0:T(8,128)S(1)} collective-permute-done((f32[128,1536]{1,0:T(8,128)S(1)}, f32[128,1536]{1,0:T(8,128)S(1)}, u32[]{:S(2)}, u32[]{:S(2)}) %collective-permute-start.38) | collective-permute-done | bytes 786464 | tf_op jit(solution)/shard_map/ppermute | solution.py:689
  491.8 16.8 %collective-permute-start.41 = (f32[128,1536]{1,0:T(8,128)S(1)}, f32[128,1536]{1,0:T(8,128)}, u32[]{:S(2)}, u32[]{:S(2)}) collective-permute-start(f32[128,1536]{1,0:T(8,128)S(1)} %collective-permute-done.40.refs_4_), channel_id=1, source_target_pairs={{0,4},{4,0},{8,12},{12,8},{16,20},{20,16},{24,28},{28,24},{1,5},{5... | collective-permute-start | bytes 2359304 | tf_op jit(solution)/shard_map/ppermute | solution.py:689
  523.9 50.0 %shard_map.173 = (f32[250,4608]{1,0:T(8,128)}, f32[1,4608]{1,0:T(1,128)}) custom-call(s32[1]{0:T(128)} %bitcast.13.base_ref, s32[8,2]{1,0:T(8,128)} %copy.72.edge_ref, s32[8,2,1536]{2,1,0:T(2,128)} %slice.197.list_ref, f32[8,1408]{1,0:T(8,128)} %concatenate.53.refs_0_, bf16[1152,256]{1,0:T(8,128)(2,1)} %bitcast.114, bf16[1152,256]{1,0:T(8,128)(2,1)} %copy-done.30, ...), custom_call_target="tpu_custom_call" | custom-call | bytes 23068672 | tf_op jit(solution)/shard_map/pallas_call | solution.py:196
  575.3 34.5 %shard_map.172 = f32[250,4608]{1,0:T(8,128)} custom-call(s32[1]{0:T(128)} %bitcast.13.base_ref, s32[8,2]{1,0:T(8,128)} %copy.68.edge_ref, s32[8,2,1280]{2,1,0:T(2,128)} %slice.195.list_ref, f32[1152,256]{1,0:T(8,128)} %get-tuple-element.62.refs_0_, f32[1152,256]{1,0:T(8,128)} %collective-permute-done.51.refs_1_, ...), custom_call_target="tpu_custom_call" | custom-call | bytes 18874368 | tf_op jit(solution)/shard_map/pallas_call | solution.py:196
  (346 shorter events, 157.8 us)
Async XLA Ops:
  7.6 52.4 %collective-permute-start.1 = (bf16[784,256]{1,0:T(8,128)(2,1)S(1)}, bf16[784,256]{1,0:T(8,128)(2,1)S(1)}, u32[]{:S(2)}, u32[]{:S(2)}) collective-permute-start(bf16[784,256]{1,0:T(8,128)(2,1)S(1)} %concatenate.43.refs_0_), channel_id=1, source_target_pairs={{0,2},{1,3},{2,0},{3,1},{4,6},{5,7},{6,4},{7,5},{8,10},{9,11},{10,... | collective-permute-start | bytes 1204232 | tf_op jit(solution)/shard_map/ppermute | solution.py:689
  10.0 54.0 %collective-permute-start.2 = (bf16[784,256]{1,0:T(8,128)(2,1)S(1)}, bf16[784,256]{1,0:T(8,128)(2,1)S(1)}, u32[]{:S(2)}, u32[]{:S(2)}) collective-permute-start(bf16[784,256]{1,0:T(8,128)(2,1)S(1)} %concatenate.43.refs_0_), channel_id=1, source_target_pairs={{1,2},{2,1},{5,6},{6,5},{9,10},{10,9},{13,14},{14,13},{17,18},{18,... | collective-permute-start | bytes 1204232 | tf_op jit(solution)/shard_map/ppermute | solution.py:697
  10.7 54.6 %collective-permute-start = (bf16[784,256]{1,0:T(8,128)(2,1)S(1)}, bf16[784,256]{1,0:T(8,128)(2,1)S(1)}, u32[]{:S(2)}, u32[]{:S(2)}) collective-permute-start(bf16[784,256]{1,0:T(8,128)(2,1)S(1)} %concatenate.43.refs_0_), channel_id=1, source_target_pairs={{0,1},{1,0},{2,3},{3,2},{4,5},{5,4},{6,7},{7,6},{8,9},{9,8},{10,11... | collective-permute-start | bytes 1204232 | tf_op jit(solution)/shard_map/ppermute | solution.py:689
  60.1 46.2 %collective-permute-start.23 = (bf16[1408,256]{1,0:T(8,128)(2,1)S(1)}, bf16[1408,256]{1,0:T(8,128)(2,1)}, u32[]{:S(2)}, u32[]{:S(2)}) collective-permute-start(bf16[1408,256]{1,0:T(8,128)(2,1)S(1)} %slice.148.refs_0_), channel_id=1, source_target_pairs={{0,2},{1,3},{2,0},{3,1},{4,6},{5,7},{6,4},{7,5},{8,10},{9,11},{10,... | collective-permute-start | bytes 2162696 | tf_op jit(solution)/shard_map/ppermute | solution.py:689
  69.4 52.3 %collective-permute-start.22 = (bf16[1408,256]{1,0:T(8,128)(2,1)S(1)}, bf16[1408,256]{1,0:T(8,128)(2,1)}, u32[]{:S(2)}, u32[]{:S(2)}) collective-permute-start(bf16[1408,256]{1,0:T(8,128)(2,1)S(1)} %slice.148.refs_0_), channel_id=1, source_target_pairs={{0,1},{1,0},{2,3},{3,2},{4,5},{5,4},{6,7},{7,6},{8,9},{9,8},{10,11... | collective-permute-start | bytes 2162696 | tf_op jit(solution)/shard_map/ppermute | solution.py:689
  93.2 56.8 %collective-permute-start.16 = (bf16[384,1024]{1,0:T(8,128)(2,1)S(1)}, bf16[384,1024]{1,0:T(8,128)(2,1)S(1)}, u32[]{:S(2)}, u32[]{:S(2)}) collective-permute-start(bf16[384,1024]{1,0:T(8,128)(2,1)S(1)} %shard_map.164.refs_12_.refs_0_), channel_id=1, source_target_pairs={{0,8},{4,12},{8,0},{12,4},{16,24},{20,28},{24,16},{28,20},{1,9},{5... | collective-permute-start | bytes 2359304 | tf_op jit(solution)/shard_map/ppermute | solution.py:689
  106.3 43.9 %collective-permute-start.18 = (bf16[384,1024]{1,0:T(8,128)(2,1)S(1)}, bf16[384,1024]{1,0:T(8,128)(2,1)S(1)}, u32[]{:S(2)}, u32[]{:S(2)}) collective-permute-start(bf16[384,1024]{1,0:T(8,128)(2,1)S(1)} %shard_map.164.refs_12_.refs_0_), channel_id=1, source_target_pairs={{0,16},{4,20},{8,24},{12,28},{16,0},{20,4},{24,8},{28,12},{1,17},{... | collective-permute-start | bytes 2359304 | tf_op jit(solution)/shard_map/ppermute | solution.py:689
  156.1 53.4 %collective-permute-start.17 = (bf16[384,1024]{1,0:T(8,128)(2,1)}, bf16[384,1024]{1,0:T(8,128)(2,1)S(1)}, u32[]{:S(2)}, u32[]{:S(2)}) collective-permute-start(bf16[384,1024]{1,0:T(8,128)(2,1)} %copy-done.6), channel_id=1, source_target_pairs={{0,4},{4,0},{8,12},{12,8},{16,20},{20,16},{24,28},{28,24},{1,5},{5... | collective-permute-start | bytes 2359304 | tf_op jit(solution)/shard_map/ppermute | solution.py:689
  211.2 110.9 %collective-permute-start.44 = (s32[4,1536]{1,0:T(4,128)S(1)}, s32[4,1536]{1,0:T(4,128)S(1)}, u32[]{:S(2)}, u32[]{:S(2)}) collective-permute-start(s32[4,1536]{1,0:T(4,128)S(1)} %maximum_convert_fusion.1), channel_id=1, source_target_pairs={{0,4},{4,0},{8,12},{12,8},{16,20},{20,16},{24,28},{28,24},{1,5},{5... | collective-permute-start | bytes 73736 | tf_op jit(solution)/shard_map/ppermute | solution.py:689
  242.6 80.8 %collective-permute-start.45 = (s32[4,1536]{1,0:T(4,128)S(1)}, s32[4,1536]{1,0:T(4,128)S(1)}, u32[]{:S(2)}, u32[]{:S(2)}) collective-permute-start(s32[4,1536]{1,0:T(4,128)S(1)} %maximum_convert_fusion.1), channel_id=1, source_target_pairs={{0,8},{4,12},{8,0},{12,4},{16,24},{20,28},{24,16},{28,20},{1,9},{5... | collective-permute-start | bytes 73736 | tf_op jit(solution)/shard_map/ppermute | solution.py:689
  243.8 79.8 %collective-permute-start.47 = (s32[4,1536]{1,0:T(4,128)S(1)}, s32[4,1536]{1,0:T(4,128)S(1)}, u32[]{:S(2)}, u32[]{:S(2)}) collective-permute-start(s32[4,1536]{1,0:T(4,128)S(1)} %maximum_convert_fusion.1), channel_id=1, source_target_pairs={{0,16},{4,20},{8,24},{12,28},{16,0},{20,4},{24,8},{28,12},{1,17},{... | collective-permute-start | bytes 73736 | tf_op jit(solution)/shard_map/ppermute | solution.py:689
  285.9 54.1 %collective-permute-start.58 = (f32[4,256,256]{2,1,0:T(8,128)}, f32[4,256,256]{2,1,0:T(8,128)S(1)}, u32[]{:S(2)}, u32[]{:S(2)}) collective-permute-start(f32[4,256,256]{2,1,0:T(8,128)} %slice_bitcast_fusion), channel_id=1, source_target_pairs={{0,4},{4,0},{8,12},{12,8},{16,20},{20,16},{24,28},{28,24},{1,5},{5... | collective-permute-start | bytes 3145736 | tf_op jit(solution)/shard_map/ppermute | solution.py:689
  321.3 54.2 %collective-permute-start.33 = (f32[4,128,1536]{2,1,0:T(8,128)}, f32[4,128,1536]{2,1,0:T(8,128)}, u32[]{:S(2)}, u32[]{:S(2)}) collective-permute-start(f32[4,128,1536]{2,1,0:T(8,128)} %get-tuple-element.52), channel_id=1, source_target_pairs={{0,4},{4,0},{8,12},{12,8},{16,20},{20,16},{24,28},{28,24},{1,5},{5... | collective-permute-start | bytes 9437192 | tf_op jit(solution)/shard_map/ppermute | solution.py:689
  365.6 56.4 %collective-permute-start.56 = (f32[1152,256]{1,0:T(8,128)}, f32[1152,256]{1,0:T(8,128)}, u32[]{:S(2)}, u32[]{:S(2)}) collective-permute-start(f32[1152,256]{1,0:T(8,128)} %get-tuple-element.62.refs_0_), channel_id=1, source_target_pairs={{0,24},{4,28},{8,16},{12,20},{16,8},{20,12},{24,0},{28,4},{1,25},{... | collective-permute-start | bytes 3538952 | tf_op jit(solution)/shard_map/ppermute | solution.py:689
  372.2 50.8 %collective-permute-start.51 = (f32[1152,256]{1,0:T(8,128)}, f32[1152,256]{1,0:T(8,128)}, u32[]{:S(2)}, u32[]{:S(2)}) collective-permute-start(f32[1152,256]{1,0:T(8,128)} %get-tuple-element.62.refs_0_), channel_id=1, source_target_pairs={{0,4},{4,0},{8,12},{12,8},{16,20},{20,16},{24,28},{28,24},{1,5},{5... | collective-permute-start | bytes 3538952 | tf_op jit(solution)/shard_map/ppermute | solution.py:689
  379.3 47.2 %collective-permute-start.63 = (f32[264,256]{1,0:T(8,128)S(1)}, f32[264,256]{1,0:T(8,128)S(1)}, u32[]{:S(2)}, u32[]{:S(2)}) collective-permute-start(f32[264,256]{1,0:T(8,128)S(1)} %pad_maximum_fusion), channel_id=1, source_target_pairs={{0,8},{4,12},{8,0},{12,4},{16,24},{20,28},{24,16},{28,20},{1,9},{5... | collective-permute-start | bytes 811016 | tf_op jit(solution)/shard_map/ppermute | solution.py:689
  396.8 71.7 %collective-permute-start.34 = (f32[128,1536]{1,0:T(8,128)S(1)}, f32[128,1536]{1,0:T(8,128)S(1)}, u32[]{:S(2)}, u32[]{:S(2)}) collective-permute-start(f32[128,1536]{1,0:T(8,128)S(1)} %get-tuple-element.72), channel_id=1, source_target_pairs={{0,8},{4,12},{8,0},{12,4},{16,24},{20,28},{24,16},{28,20},{1,9},{5... | collective-permute-start | bytes 2359304 | tf_op jit(solution)/shard_map/ppermute | solution.py:689
  422.0 47.1 %collective-permute-start.35 = (f32[128,1536]{1,0:T(8,128)S(1)}, f32[128,1536]{1,0:T(8,128)S(1)}, u32[]{:S(2)}, u32[]{:S(2)}) collective-permute-start(f32[128,1536]{1,0:T(8,128)S(1)} %get-tuple-element.74), channel_id=1, source_target_pairs={{0,16},{4,20},{8,24},{12,28},{16,0},{20,4},{24,8},{28,12},{1,17},{... | collective-permute-start | bytes 2359304 | tf_op jit(solution)/shard_map/ppermute | solution.py:689
  423.1 46.0 %collective-permute-start.36 = (f32[128,1536]{1,0:T(8,128)S(1)}, f32[128,1536]{1,0:T(8,128)S(1)}, u32[]{:S(2)}, u32[]{:S(2)}) collective-permute-start(f32[128,1536]{1,0:T(8,128)S(1)} %get-tuple-element.73), channel_id=1, source_target_pairs={{0,24},{4,28},{8,16},{12,20},{16,8},{20,12},{24,0},{28,4},{1,25},{... | collective-permute-start | bytes 2359304 | tf_op jit(solution)/shard_map/ppermute | solution.py:689
  477.2 98.2 %collective-permute-start.57 = (f32[1152,256]{1,0:T(8,128)}, f32[1152,256]{1,0:T(8,128)}, u32[]{:S(2)}, u32[]{:S(2)}) collective-permute-start(f32[1152,256]{1,0:T(8,128)} %collective-permute-done.56.refs_6_), channel_id=1, source_target_pairs={{0,4},{4,0},{8,12},{12,8},{16,20},{20,16},{24,28},{28,24},{1,5},{5... | collective-permute-start | bytes 3538952 | tf_op jit(solution)/shard_map/ppermute | solution.py:689
  479.8 130.0 %collective-permute-start.37 = (f32[128,1536]{1,0:T(8,128)S(1)}, f32[128,1536]{1,0:T(8,128)}, u32[]{:S(2)}, u32[]{:S(2)}) collective-permute-start(f32[128,1536]{1,0:T(8,128)S(1)} %fusion.5.refs_0_), channel_id=1, source_target_pairs={{0,4},{4,0},{8,12},{12,8},{16,20},{20,16},{24,28},{28,24},{1,5},{5... | collective-permute-start | bytes 2359304 | tf_op jit(solution)/shard_map/ppermute | solution.py:689
  489.8 120.0 %collective-permute-start.39 = (f32[128,1536]{1,0:T(8,128)S(1)}, f32[128,1536]{1,0:T(8,128)}, u32[]{:S(2)}, u32[]{:S(2)}) collective-permute-start(f32[128,1536]{1,0:T(8,128)S(1)} %collective-permute-done.38.refs_2_), channel_id=1, source_target_pairs={{0,4},{4,0},{8,12},{12,8},{16,20},{20,16},{24,28},{28,24},{1,5},{5... | collective-permute-start | bytes 2359304 | tf_op jit(solution)/shard_map/ppermute | solution.py:689
  491.8 118.0 %collective-permute-start.41 = (f32[128,1536]{1,0:T(8,128)S(1)}, f32[128,1536]{1,0:T(8,128)}, u32[]{:S(2)}, u32[]{:S(2)}) collective-permute-start(f32[128,1536]{1,0:T(8,128)S(1)} %collective-permute-done.40.refs_4_), channel_id=1, source_target_pairs={{0,4},{4,0},{8,12},{12,8},{16,20},{20,16},{24,28},{28,24},{1,5},{5... | collective-permute-start | bytes 2359304 | tf_op jit(solution)/shard_map/ppermute | solution.py:689
  508.6 101.2 %collective-permute-start.43 = (f32[128,1536]{1,0:T(8,128)S(1)}, f32[128,1536]{1,0:T(8,128)}, u32[]{:S(2)}, u32[]{:S(2)}) collective-permute-start(f32[128,1536]{1,0:T(8,128)S(1)} %collective-permute-done.42.refs_6_), channel_id=1, source_target_pairs={{0,4},{4,0},{8,12},{12,8},{16,20},{20,16},{24,28},{28,24},{1,5},{5... | collective-permute-start | bytes 2359304 | tf_op jit(solution)/shard_map/ppermute | solution.py:689
  (102 other events, 2376.5 us)
